TPU v7x, 256 devices: a whole 4x4x8 slice. The times are simulated.
256 devices in a mesh: pipe: 4 (over y), row: 16 (over z, core), col: 4 (over x).
Axes of the slice: x: 4, y: 4, z: 8, core: 2. Of those that a mesh axis runs over, the one named last changes fastest.
Arguments:
- activations: bfloat16 [4, 128, 64, 512], P('pipe', 'row', 'col'), may hold values from -6 to 6
- qkv_weight: bfloat16 [4, 512, 1536], P('pipe'), may hold values from -9 to 9
- out_weight: bfloat16 [4, 512, 512], P('pipe'), may hold values from -0.25 to 0.25
- cotangent: float32 [128, 64, 512], P('row', 'col'), may hold values from -6 to 6
Outputs:
- input_grads: float32 [4, 128, 64, 512], P('pipe', 'row', 'col')
- qkv_grads: float32 [4, 512, 1536], P('pipe', ('row', 'col'))
- out_grads: float32 [4, 512, 512], P('pipe', ('row', 'col'))
All inputs are finite; a program needn't handle non-finite values.
Results may differ from a plain program's by a relative error of at most 0.015.
Values may be sent and summed in bfloat16 or wider, within the bound.
No kernel may reach another device: no remote copies, remote signals or barrier semaphores. Data moves between devices by JAX's collectives and lax.ppermute only.
A program may use at most 128 MiB of HBM per device.

v0:
```python
import functools

import jax
import jax.numpy as jnp
import numpy as np
from jax import lax
from jax.experimental import pallas as pl
from jax.experimental.pallas import tpu as pltpu
from jax.sharding import Mesh
from jax.sharding import PartitionSpec as P

F32 = jnp.float32
BF16 = jnp.bfloat16
AXES = ("pipe", "z", "core", "col")
D = 512
PAIRS = 4
TOK = 128
OWN = 256
REGION = 768
BLOCK = 32
VMEM_LIMIT = 40 * 1024 * 1024


def nn(a, b):
    return lax.dot_general(a, b, (((1,), (0,)), ((), ())), preferred_element_type=F32)


def nt(a, b):
    return lax.dot_general(a, b, (((1,), (1,)), ((), ())), preferred_element_type=F32)


def tn(a, b):
    return lax.dot_general(a, b, (((0,), (0,)), ((), ())), preferred_element_type=F32)


def two_heads(block):
    lane = lax.broadcasted_iota(jnp.int32, block.shape, 1)
    zero = jnp.zeros_like(block)
    return jnp.concatenate(
        [jnp.where(lane < 64, block, zero), jnp.where(lane < 64, zero, block)], axis=0
    )


def one_block(stacked):
    half = stacked.shape[0] // 2
    lane = lax.broadcasted_iota(jnp.int32, (half, 128), 1)
    return jnp.where(lane < 64, stacked[:half], stacked[half:])


def place(index, core):
    piece = index >> 8
    inner = index & 255
    side = inner - 128
    is_centre = inner < 128
    row = jnp.where(is_centre, inner >> 4, (side & 63) >> 3)
    col = jnp.where(is_centre, inner & 15, jnp.where(side < 64, (side & 7) - 8, (side & 7) + 16))
    mate = jnp.where(core == 0, 8, -8)
    row = row + jnp.where(piece == 1, mate, jnp.where(piece == 2, -mate, 0))
    return row, col


def window(where_ref, keys_own):
    row0, col0, core, rows, cols = (where_ref[i] for i in range(5))
    own = lax.broadcasted_iota(jnp.int32, (TOK, 1), 0)
    reach_row, reach_col = place(lax.broadcasted_iota(jnp.int32, (1, REGION), 1), core)
    grid_row, grid_col = row0 + reach_row, col0 + reach_col
    inside = (grid_row >= 0) & (grid_row < rows) & (grid_col >= 0) & (grid_col < cols)
    reach_row = jnp.where(inside, reach_row, 1 << 20)
    if keys_own:
        step_row, step_col = (own >> 4) - reach_row, (own & 15) - reach_col
    else:
        step_row, step_col = reach_row - (own >> 4), reach_col - (own & 15)
    return (step_row >= -8) & (step_row <= 7) & (step_col >= -8) & (step_col <= 7)


def put_sides(block, left_ref, right_ref):
    sides = block.reshape(8, 2, 8, block.shape[-1])
    left_ref[...] = sides[:, 0].reshape(64, -1).astype(BF16)
    right_ref[...] = sides[:, 1].reshape(64, -1).astype(BF16)


def first_kernel(where_ref, x_ref, base_ref, left_ref, right_ref):
    base_ref[:TOK] = x_ref[...]
    base_ref[TOK:] = jnp.zeros((TOK, D), BF16)
    put_sides(x_ref[...].astype(F32), left_ref, right_ref)


def normed_low(x_ref):
    x = x_ref[...].astype(F32)
    inverse = lax.rsqrt(jnp.mean(x * x, axis=-1, keepdims=True) + 1e-06)
    return (x * inverse).astype(BF16)


def centre_kernel(where_ref, x_ref, w_ref, cot_ref, proj_ref, nlow_ref, cot_low_ref):
    low = normed_low(x_ref)
    nlow_ref[...] = low
    proj_ref[...] = nn(low, w_ref[...]).astype(BF16)
    cot_low_ref[...] = cot_ref[...].astype(BF16)


def side_kernel(where_ref, left_ref, right_ref, w_ref, wo_ref, cot_ref, proj_ref, dm_ref):
    low = jnp.concatenate([normed_low(left_ref), normed_low(right_ref)], axis=0)
    proj_ref[...] = nn(low, w_ref[...]).astype(BF16)
    dm_ref[...] = nt(cot_ref[...], wo_ref[...]).astype(BF16)


def forward_kernel(
    where_ref, x1, x2, proj_ref, side_ref, w_ref, cot_ref, dm_ref,
    kv_ref, prob_ref, nlow_ref, far_ref, mixed_ref, pack_ref, left_ref, right_ref,
):
    kv_ref[:TOK] = proj_ref[:, D:]
    kv_ref[TOK:OWN] = side_ref[:, D:]
    for piece, x_ref in enumerate((x1, x2)):
        low = normed_low(x_ref)
        far_ref[piece * OWN : (piece + 1) * OWN] = low
        if piece == 0:
            nlow_ref[...] = low[:TOK]
        kv_ref[(piece + 1) * OWN : (piece + 2) * OWN] = nn(low, w_ref[:, D:]).astype(BF16)
    ok = window(where_ref, False)
    ok2 = jnp.concatenate([ok, ok], axis=0)
    lane = lax.broadcasted_iota(jnp.int32, (TOK, 128), 1)
    stats = jnp.zeros((TOK, 128), F32)
    for pair in range(PAIRS):
        at = slice(128 * pair, 128 * pair + 128)
        query = two_heads(proj_ref[:, at] * 0.125)
        scores = nt(query, kv_ref[:, at])
        scores = jnp.where(ok2, scores, -1e30)
        highest = jnp.max(scores, axis=-1, keepdims=True)
        grown = jnp.exp(scores - highest)
        total = jnp.sum(grown, axis=-1, keepdims=True)
        probs = (grown * (1.0 / total)).astype(BF16)
        prob_ref[pair] = probs
        value = kv_ref[:, D + 128 * pair : D + 128 * pair + 128]
        mixed = one_block(nn(probs, value)).astype(BF16)
        mixed_ref[:, at] = mixed
        log_total = highest + jnp.log(total)
        delta = two_sums(dm_ref[:, at], mixed)
        for first, rest in ((0, log_total), (24, delta)):
            for part in range(3):
                piece = rest.astype(BF16).astype(F32)
                rest = rest - piece
                for head in range(2):
                    chosen = lane == first + 8 * part + 2 * pair + head
                    stats = jnp.where(chosen, piece[TOK * head : TOK * head + TOK], stats)
    starts = where_ref[5] == 0
    pack_ref[:, D:] = stats.astype(BF16)

    @pl.when(starts)
    def _():
        pack_ref[:, :D] = cot_ref[...]

    @pl.when(jnp.logical_not(starts))
    def _():
        pack_ref[:, :D] = mixed_ref[...]

    put_sides(pack_ref[...].astype(F32), left_ref, right_ref)


def turned_kernel(where_ref, proj_ref, side_ref, far_ref, w_ref, n0, n1, query_ref, nt_ref, full_ref):
    query_ref[:, :TOK] = proj_ref[:, :D].astype(F32).T.astype(BF16)
    query_ref[:, TOK:OWN] = side_ref[:, :D].astype(F32).T.astype(BF16)
    far = nn(far_ref[...], w_ref[:, :D]).astype(BF16)
    query_ref[:, OWN:] = far.astype(F32).T.astype(BF16)
    full_ref[:, :TOK] = n0[...].astype(F32).T
    full_ref[:, TOK:] = n1[...].astype(F32).T
    nt_ref[...] = own_half(where_ref, full_ref).astype(BF16)


def own_half(where_ref, full_ref):
    rows = [
        full_ref[pl.ds(pl.multiple_of((2 * at + where_ref[2]) * BLOCK, BLOCK), BLOCK)]
        for at in range(full_ref.shape[0] // (2 * BLOCK))
    ]
    return jnp.concatenate(rows, axis=0)


def key_probs_kernel(
    where_ref, p0, p1, p2, proj_ref, query_ref, prob_ref, mixed_ref, delta_ref
):
    head = lax.broadcasted_iota(jnp.int32, (8, 128), 0)
    lane = lax.broadcasted_iota(jnp.int32, (8, 128), 1)
    stats = jnp.concatenate([p[:, D:] for p in (p0, p1, p2)], axis=0)
    sums = []
    for first in (0, 24):
        chosen = ((lane & 7) == head) & (lane >= first) & (lane < first + 24)
        sums.append(nt(jnp.where(chosen, 1.0, 0.0).astype(BF16), stats))
    log_total, delta_ref[...] = sums

    @pl.when(where_ref[5] != 0)
    def _():
        for piece, p in enumerate((p0, p1, p2)):
            mixed_ref[:, piece * OWN : (piece + 1) * OWN] = p[:, :D].astype(F32).T.astype(BF16)

    ok = window(where_ref, True)
    for pair in range(PAIRS):
        key = two_heads(proj_ref[:, D + 128 * pair : D + 128 * pair + 128] * 0.125)
        scores = nn(key, query_ref[128 * pair : 128 * pair + 128])
        for side in range(2):
            at = 2 * pair + side
            part = scores[TOK * side : TOK * side + TOK] - log_total[at : at + 1]
            probs = jnp.exp(jnp.where(ok, part, -1e30))
            prob_ref[pair, TOK * side : TOK * side + TOK] = probs.astype(BF16)


def two_sums(grad, mixed):
    prod = grad.astype(F32) * mixed.astype(F32)
    lane = lax.broadcasted_iota(jnp.int32, prod.shape, 1)
    return jnp.concatenate(
        [
            jnp.sum(jnp.where(lane < 64, prod, 0.0), axis=-1, keepdims=True),
            jnp.sum(jnp.where(lane < 64, 0.0, prod), axis=-1, keepdims=True),
        ],
        axis=0,
    )


def query_kernel(where_ref, g_ref, w_ref, mixed_ref, kv_ref, prob_ref, dq_ref, dm_ref, *, turn):
    @pl.when(where_ref[5] == turn)
    def _():
        dm_ref[...] = nt(g_ref[...], w_ref[...]).astype(BF16)

        def one_pair(pair, carry):
            low = pl.multiple_of(128 * pair, 128)
            at = pl.ds(low, 128)
            grad = dm_ref[:, at]
            delta = two_sums(grad, mixed_ref[:, at])
            pressure = nt(two_heads(grad), kv_ref[:, pl.ds(low + D, 128)])
            slopes = (prob_ref[pair].astype(F32) * (pressure - delta)).astype(BF16)
            dq_ref[:, at] = (one_block(nn(slopes, kv_ref[:, at])) * 0.125).astype(BF16)
            return carry

        lax.fori_loop(0, PAIRS, one_pair, 0)


def turned_block(stacked):
    row = lax.broadcasted_iota(jnp.int32, (128, 128), 0)
    return jnp.where(row < 64, stacked[:, :128], stacked[:, 128:]).T


def key_kernel(
    where_ref, g0, g1, g2, wo_ref, delta_ref, proj_ref, query_ref, prob_ref, dq_ref, mixed_ref,
    *rest, turn, last,
):
    ins, rest = ((), rest) if last else (rest[:3], rest[3:])
    prev = (3 - last) if turn else 0
    prev, rest = rest[:prev], rest[prev:]
    outs, sends, dm_ref = rest[: 3 - last], rest[3 - last : -1], rest[-1]
    dp_ref, gl_ref = outs[:2]
    active = where_ref[5] == turn

    if prev:

        @pl.when(jnp.logical_not(active))
        def _():
            for new, old in zip(outs, prev):
                new[...] = old[...]

    @pl.when(active)
    def _():
        for piece, g in enumerate((g0, g1, g2)):
            d_mixed = nt(wo_ref[...], g[:, :D]).astype(BF16)
            dm_ref[:, piece * OWN : (piece + 1) * OWN] = d_mixed
        dp_ref[:, :D] = dq_ref[...]
        dp_ref[:, 3 * D :] = mixed_ref[...]
        gl_ref[:TOK] = g0[:TOK, :D]
        gl_ref[TOK:] = g1[:TOK, :D]
        for pair in range(PAIRS):
            at = slice(128 * pair, 128 * pair + 128)
            value = two_heads(proj_ref[:, 2 * D + 128 * pair : 2 * D + 128 * pair + 128])
            grad = dm_ref[at]
            if turn:
                prod = grad.astype(F32) * delta_ref[at].astype(F32)
                deltas = [jnp.sum(prod[r : r + 64], axis=0, keepdims=True) for r in (0, 64)]
            else:
                deltas = [delta_ref[2 * pair + side : 2 * pair + side + 1] for side in range(2)]
            pressure = nn(value, grad)
            probs = prob_ref[pair]
            d_value = nt(grad, probs)
            slopes = []
            for side in range(2):
                rows = slice(TOK * side, TOK * side + TOK)
                slopes.append(
                    (probs[rows].astype(F32) * (pressure[rows] - deltas[side])).astype(BF16)
                )
            d_key = nt(query_ref[at], jnp.concatenate(slopes, axis=0))
            low, high = D + 128 * pair, D + 128 * pair + 128
            dp_ref[:, low:high] = (turned_block(d_key) * 0.125).astype(BF16)
            dp_ref[:, D + low : D + high] = turned_block(d_value).astype(BF16)
        if not last:
            out = input_grad(dp_ref, *ins)
            outs[2][...] = out
            low_ref, left_ref, right_ref = sends
            low_ref[...] = out.astype(BF16)
            put_sides(out, left_ref, right_ref)


def input_grad(dp_ref, g_ref, wq_ref, x_ref):
    d_normed = nt(dp_ref[:, : 3 * D], wq_ref[...])
    x = x_ref[...].astype(F32)
    inverse = lax.rsqrt(jnp.mean(x * x, axis=-1, keepdims=True) + 1e-06)
    normed = x * inverse
    inner = jnp.mean(d_normed * normed, axis=-1, keepdims=True)
    return g_ref[...].astype(F32) + inverse * (d_normed - normed * inner)


def input_kernel(where_ref, dp_ref, g_ref, wq_ref, x_ref, prev_ref, in_ref, *, turn):
    @pl.when(where_ref[5] == turn)
    def _():
        in_ref[...] = input_grad(dp_ref, g_ref, wq_ref, x_ref)

    @pl.when(where_ref[5] != turn)
    def _():
        in_ref[...] = prev_ref[...]


def weight_kernel(where_ref, nt_ref, d0, d1, g_ref, *refs):
    outs, (left_ref, full_ref) = refs[:-2], refs[-2:]
    d_proj = jnp.concatenate([d0[:, : 3 * D], d1[:, : 3 * D]], axis=0)
    mixed = jnp.concatenate([d0[:, 3 * D :], d1[:, 3 * D :]], axis=0)
    full_ref[...] = tn(mixed, g_ref[...])
    left_ref[...] = nn(nt_ref[...], d_proj)
    core, cols = where_ref[2], len(outs)
    for distance, out_ref in enumerate(outs):
        col = lax.rem(where_ref[6] + distance, cols)
        for at, ref, step, first in (
            (slice(0, 3 * D), left_ref, BLOCK, 0), (slice(3 * D, 4 * D), full_ref, 2 * BLOCK, core)
        ):
            rows = [
                ref[pl.ds(pl.multiple_of(step * chip + first * BLOCK + 8 * col, 8), 8)]
                for chip in range(out_ref.shape[0] // 8)
            ]
            out_ref[:, at] = jnp.concatenate(rows, axis=0).astype(BF16)


def col_total_kernel(where_ref, *refs):
    total = refs[0][...].astype(F32)
    for ref in refs[1:-1]:
        total = total + ref[...].astype(F32)
    refs[-1][...] = total.astype(BF16)


def total_kernel(where_ref, part_ref, qkv_ref, out_ref, *, scale):
    total = part_ref[0].astype(F32)
    for source in range(1, part_ref.shape[0]):
        total = total + part_ref[source].astype(F32)
    qkv_ref[...] = total[:, : 3 * D] * scale
    out_ref[...] = total[:, 3 * D :] * scale


def call(kernel, outs, *args, scratch=(), flops=0):
    vmem = pl.BlockSpec(memory_space=pltpu.VMEM)
    return pl.pallas_call(
        kernel,
        out_shape=[jax.ShapeDtypeStruct(s, t) for s, t in outs],
        in_specs=[pl.BlockSpec(memory_space=pltpu.SMEM)] + [vmem] * (len(args) - 1),
        out_specs=[vmem] * len(outs),
        scratch_shapes=list(scratch),
        compiler_params=pltpu.CompilerParams(vmem_limit_bytes=VMEM_LIMIT),
        cost_estimate=pl.CostEstimate(flops=flops, bytes_accessed=4 << 20, transcendentals=0),
    )(*args)


def body(sizes, activations, qkv_weight, out_weight, cotangent):
    pipes, chips, cols = sizes

    def routed(block, step):
        pairs = []
        for p in range(pipes):
            for r in range(2 * chips):
                for c in range(cols):
                    p2, r2, c2 = step(p, r, c)
                    target = ((p2 % pipes) * 2 * chips + r2 % (2 * chips)) * cols + c2 % cols
                    pairs.append(((p * 2 * chips + r) * cols + c, target))
        return lax.ppermute(block, AXES, pairs)

    def col_rims(left_half, right_half, down=0):
        left = routed(right_half, lambda p, r, c: (p - down, r, c + 1))
        right = routed(left_half, lambda p, r, c: (p - down, r, c - 1))
        return left, right

    def mate(p, r, c):
        return p, r ^ 1, c

    def row_rims(pieces):
        own = jnp.concatenate(pieces, axis=0)
        beyond = routed(own, lambda p, r, c: (p, r - 1 + 2 * (r & 1), c))
        return own, routed(own, mate), beyond

    pipe, z, core, col = (lax.axis_index(axis) for axis in AXES)
    x = activations.reshape(TOK, D)
    w_qkv, w_out = qkv_weight[0], out_weight[0]
    cot = cotangent.reshape(TOK, D)
    row_total, col_total = 16 * chips, 16 * cols
    where = jnp.stack(
        [8 * (2 * z + core), 16 * col, core, row_total, col_total, pipes - 1 - pipe, col]
    ).astype(jnp.int32)

    base, low_side, high_side = call(
        first_kernel, [((OWN, D), BF16), ((64, D), BF16), ((64, D), BF16)], where, x
    )
    proj, nlow, cot_low = call(
        centre_kernel, [((TOK, 3 * D), BF16), ((TOK, D), BF16), ((TOK, D), BF16)],
        where, x, w_qkv, cot, flops=1 << 28,
    )
    left, right = col_rims(low_side, high_side)
    base, proj = lax.optimization_barrier((base, proj))
    own = lax.dynamic_update_slice(base, left, (TOK, 0))
    own, near, far = row_rims([lax.dynamic_update_slice(own, right, (TOK + 64, 0))])
    side_proj, d_mixed = call(
        side_kernel, [((TOK, 3 * D), BF16), ((TOK, D), BF16)],
        where, left, right, w_qkv, w_out, cot_low, flops=1 << 28,
    )
    wide = D + 128
    kv, q_probs, nlow_mate, low_far, mixed, pack, low_side, high_side = call(
        forward_kernel,
        [((REGION, 2 * D), BF16), ((PAIRS, OWN, REGION), BF16), ((TOK, D), BF16),
         ((2 * OWN, D), BF16), ((TOK, D), BF16), ((TOK, wide), BF16), ((64, wide), BF16),
         ((64, wide), BF16)],
        where, near, far, proj, side_proj, w_qkv, cot_low, d_mixed, flops=2 << 30,
    )
    sides = col_rims(low_side, high_side)
    queries, n_turned = call(
        turned_kernel, [((D, REGION), BF16), ((OWN, OWN), BF16)],
        where, proj, side_proj, low_far, w_qkv, nlow, nlow_mate,
        scratch=[pltpu.VMEM((D, OWN), F32)], flops=1 << 28,
    )

    def query_side(turn, gradient):
        return call(
            functools.partial(query_kernel, turn=turn), [((TOK, D), BF16)],
            where, gradient, w_out, mixed, kv, q_probs,
            scratch=[pltpu.VMEM((TOK, D), BF16)], flops=1 << 29,
        )[0]

    d_query = query_side(0, cot_low)
    left, right = sides
    right, queries, d_query = lax.optimization_barrier((right, queries, d_query))
    packs = row_rims([pack, left, right])
    k_probs, mixed_turned, delta = call(
        key_probs_kernel,
        [((PAIRS, OWN, REGION), BF16), ((D, REGION), BF16), ((8, REGION), F32)],
        where, *packs, proj, queries, flops=1 << 28,
    )
    gradient, gs = cot_low, packs
    state = ()
    for turn in range(pipes):
        last = turn == pipes - 1
        if turn > 0:
            low, low_side, high_side = sends
            gradient = routed(low, lambda p, r, c: (p - 1, r, c))
            left, right = col_rims(low_side, high_side, 1)
            left, d_query = lax.optimization_barrier((left, query_side(turn, gradient)))
            gs = row_rims([gradient, left, right])
        outs = [((TOK, 4 * D), BF16), ((OWN, D), BF16)]
        if not last:
            outs += [((TOK, D), F32), ((TOK, D), BF16), ((64, D), BF16), ((64, D), BF16)]
        ins = () if last else (gradient if turn else cot, w_qkv, x)
        outs = call(
            functools.partial(key_kernel, turn=turn, last=last), outs,
            where, *gs, w_out, mixed_turned if turn else delta, proj, queries, k_probs, d_query,
            mixed, *ins, *state[: 2 if last else 3],
            scratch=[pltpu.VMEM((D, REGION), BF16)], flops=1 << 30,
        )
        if last:
            d_proj, g_low = outs
            (d_in,) = call(
                functools.partial(input_kernel, turn=turn), [((TOK, D), F32)],
                where, d_proj, gradient, w_qkv, x, state[2], flops=1 << 28,
            )
        state, sends = outs[:3], outs[3:]
    parts = call(
        weight_kernel, [((8 * chips, 4 * D), BF16)] * cols,
        where, n_turned, d_proj, routed(d_proj, mate), g_low,
        scratch=[pltpu.VMEM((OWN, 3 * D), F32), pltpu.VMEM((D, D), F32)], flops=1 << 29,
    )
    parts = list(parts)
    for distance in sorted(range(1, cols), key=lambda d: -min(d, cols - d)):
        parts[distance] = routed(parts[distance], lambda p, r, c: (p, r, c + distance))
    parts[-1], d_in = lax.optimization_barrier((parts[-1], d_in))
    (part,) = call(col_total_kernel, [((8 * chips, 4 * D), BF16)], where, *parts)
    part = part.reshape(chips, 8, 4 * D)
    part = lax.all_to_all(part, "z", 0, 0, tiled=True)
    qkv_part, out_part = call(
        functools.partial(total_kernel, scale=(row_total * col_total) ** (-0.5)),
        [((8, 3 * D), F32), ((8, D), F32)], where, part,
    )
    return d_in.reshape(1, 8, 16, D), qkv_part[None], out_part[None]


def solution(mesh):
    pipes, rows, cols = (mesh.shape[axis] for axis in ("pipe", "row", "col"))
    fine = Mesh(np.asarray(mesh.devices).reshape(pipes, rows // 2, 2, cols), AXES)
    row = ("z", "core")
    return jax.shard_map(
        functools.partial(body, (pipes, rows // 2, cols)),
        mesh=fine,
        in_specs=(
            P("pipe", row, "col", None),
            P("pipe", None, None),
            P("pipe", None, None),
            P(row, "col", None),
        ),
        out_specs=(
            P("pipe", row, "col", None),
            P("pipe", ("z", "core", "col"), None),
            P("pipe", ("z", "core", "col"), None),
        ),
        check_vma=False,
    )
```

profile of v0, /device:TPU:6, one launch (start us, length us, event | category | flops | bytes accessed | tf_op | source)
XLA Modules:
  0.0 137.6 jit_solution(11527794801542978313)
XLA Ops:
  2.2 2.3 %collective-permute-start = (bf16[64,512]{1,0:T(8,128)(2,1)S(1)}, bf16[64,512]{1,0:T(8,128)(2,1)S(1)}, u32[]{:S(2)}, u32[]{:S(2)}) collective-permute-start(bf16[64,512]{1,0:T(8,128)(2,1)S(1)} %get-tuple-element.66), channel_id=1, source_target_pairs={{0,1},{1,2},{2,3},{3,0},{4,5},{5,6},{6,7},{7,4},{8,9},{9,10},{10,1... | collective-permute-start | bytes 196616 | tf_op jit(solution)/shard_map/ppermute | solution.py:374
  7.9 2.1 %collective-permute-done.1.right_ref = bf16[64,512]{1,0:T(8,128)(2,1)S(1)} collective-permute-done((bf16[64,512]{1,0:T(8,128)(2,1)S(1)}, bf16[64,512]{1,0:T(8,128)(2,1)S(1)}, u32[]{:S(2)}, u32[]{:S(2)}) %collective-permute-start.1) | collective-permute-done | bytes 65568 | tf_op jit(solution)/shard_map/ppermute | solution.py:374
  10.0 2.6 %collective-permute-start.3 = (bf16[256,512]{1,0:T(8,128)(2,1)S(1)}, bf16[256,512]{1,0:T(8,128)(2,1)S(1)}, u32[]{:S(2)}, u32[]{:S(2)}) collective-permute-start(bf16[256,512]{1,0:T(8,128)(2,1)S(1)} %constant_dynamic-update-slice_fusion.12), channel_id=1, source_target_pairs={{0,60},{1,61},{2,62},{3,63},{4,8},{5,9},{6,10},{7,11},{8,4},{9,5},... | collective-permute-start | bytes 786440 | tf_op jit(solution)/shard_map/ppermute | solution.py:374
  13.7 3.3 %collective-permute-done.3.x2 = bf16[256,512]{1,0:T(8,128)(2,1)S(1)} collective-permute-done((bf16[256,512]{1,0:T(8,128)(2,1)S(1)}, bf16[256,512]{1,0:T(8,128)(2,1)S(1)}, u32[]{:S(2)}, u32[]{:S(2)}) %collective-permute-start.3) | collective-permute-done | bytes 262176 | tf_op jit(solution)/shard_map/ppermute | solution.py:374
  17.0 4.0 %shard_map.70 = (bf16[768,1024]{1,0:T(8,128)(2,1)S(1)}, bf16[4,256,768]{2,1,0:T(8,128)(2,1)S(1)}, bf16[128,512]{1,0:T(8,128)(2,1)S(1)}, bf16[512,512]{1,0:T(8,12...) custom-call(s32[7]{0:T(128)S(1)} %stack.23.where_ref, ...), custom_call_target="tpu_custom_call" | custom-call | flops 2147483648 | bytes 4194304 | tf_op jit(solution)/shard_map/pallas_call | solution.py:352
  24.8 3.2 %collective-permute-done.5 = bf16[64,640]{1,0:T(8,128)(2,1)S(1)} collective-permute-done((bf16[64,640]{1,0:T(8,128)(2,1)S(1)}, bf16[64,640]{1,0:T(8,128)(2,1)S(1)}, u32[]{:S(2)}, u32[]{:S(2)}) %collective-permute-start.5) | collective-permute-done | bytes 81952 | tf_op jit(solution)/shard_map/ppermute | solution.py:374
  28.1 2.1 %collective-permute-start.7 = (bf16[256,640]{1,0:T(8,128)(2,1)S(1)}, bf16[256,640]{1,0:T(8,128)(2,1)S(1)}, u32[]{:S(2)}, u32[]{:S(2)}) collective-permute-start(bf16[256,640]{1,0:T(8,128)(2,1)S(1)} %constant_dynamic-update-slice_fusion.p0.g0), channel_id=1, source_target_pairs={{0,60},{1,61},{2,62},{3,63},{4,8},{5,9},{6,10},{7,11},{8,4},{9,5},... | collective-permute-start | bytes 983048 | tf_op jit(solution)/shard_map/ppermute | solution.py:374
  30.1 5.7 %collective-permute-done.7.p2.g2 = bf16[256,640]{1,0:T(8,128)(2,1)S(1)} collective-permute-done((bf16[256,640]{1,0:T(8,128)(2,1)S(1)}, bf16[256,640]{1,0:T(8,128)(2,1)S(1)}, u32[]{:S(2)}, u32[]{:S(2)}) %collective-permute-start.7) | collective-permute-done | bytes 327712 | tf_op jit(solution)/shard_map/ppermute | solution.py:374
  38.6 5.5 %collective-permute-start.8 = (bf16[128,512]{1,0:T(8,128)(2,1)S(1)}, bf16[128,512]{1,0:T(8,128)(2,1)S(1)}, u32[]{:S(2)}, u32[]{:S(2)}) collective-permute-start(bf16[128,512]{1,0:T(8,128)(2,1)S(1)} %get-tuple-element.88), channel_id=1, source_target_pairs={{0,192},{1,193},{2,194},{3,195},{4,196},{5,197},{6,198},{7,199},{8... | collective-permute-start | bytes 393224 | tf_op jit(solution)/shard_map/ppermute | solution.py:374
  45.3 2.1 %collective-permute-done.8.g_ref.rest_0_ = bf16[128,512]{1,0:T(8,128)(2,1)S(1)} collective-permute-done((bf16[128,512]{1,0:T(8,128)(2,1)S(1)}, bf16[128,512]{1,0:T(8,128)(2,1)S(1)}, u32[]{:S(2)}, u32[]{:S(2)}) %collective-permute-start.8) | collective-permute-done | bytes 131104 | tf_op jit(solution)/shard_map/ppermute | solution.py:374
  49.3 2.3 %collective-permute-done.10 = bf16[64,512]{1,0:T(8,128)(2,1)S(1)} collective-permute-done((bf16[64,512]{1,0:T(8,128)(2,1)S(1)}, bf16[64,512]{1,0:T(8,128)(2,1)S(1)}, u32[]{:S(2)}, u32[]{:S(2)}) %collective-permute-start.10) | collective-permute-done | bytes 65568 | tf_op jit(solution)/shard_map/ppermute | solution.py:374
  53.5 5.2 %collective-permute-done.12.g2 = bf16[256,512]{1,0:T(8,128)(2,1)S(1)} collective-permute-done((bf16[256,512]{1,0:T(8,128)(2,1)S(1)}, bf16[256,512]{1,0:T(8,128)(2,1)S(1)}, u32[]{:S(2)}, u32[]{:S(2)}) %collective-permute-start.12) | collective-permute-done | bytes 262176 | tf_op jit(solution)/shard_map/ppermute | solution.py:374
  60.7 4.6 %collective-permute-start.14 = (bf16[64,512]{1,0:T(8,128)(2,1)S(1)}, bf16[64,512]{1,0:T(8,128)(2,1)S(1)}, u32[]{:S(2)}, u32[]{:S(2)}) collective-permute-start(bf16[64,512]{1,0:T(8,128)(2,1)S(1)} %get-tuple-element.98), channel_id=1, source_target_pairs={{0,193},{1,194},{2,195},{3,192},{4,197},{5,198},{6,199},{7,196},{8... | collective-permute-start | bytes 196616 | tf_op jit(solution)/shard_map/ppermute | solution.py:374
  67.3 4.4 %collective-permute-done.15 = bf16[64,512]{1,0:T(8,128)(2,1)S(1)} collective-permute-done((bf16[64,512]{1,0:T(8,128)(2,1)S(1)}, bf16[64,512]{1,0:T(8,128)(2,1)S(1)}, u32[]{:S(2)}, u32[]{:S(2)}) %collective-permute-start.15) | collective-permute-done | bytes 65568 | tf_op jit(solution)/shard_map/ppermute | solution.py:374
  73.4 5.3 %collective-permute-done.17.g2 = bf16[256,512]{1,0:T(8,128)(2,1)S(1)} collective-permute-done((bf16[256,512]{1,0:T(8,128)(2,1)S(1)}, bf16[256,512]{1,0:T(8,128)(2,1)S(1)}, u32[]{:S(2)}, u32[]{:S(2)}) %collective-permute-start.17) | collective-permute-done | bytes 262176 | tf_op jit(solution)/shard_map/ppermute | solution.py:374
  81.3 4.2 %collective-permute-start.20 = (bf16[64,512]{1,0:T(8,128)(2,1)S(1)}, bf16[64,512]{1,0:T(8,128)(2,1)S(1)}, u32[]{:S(2)}, u32[]{:S(2)}) collective-permute-start(bf16[64,512]{1,0:T(8,128)(2,1)S(1)} %get-tuple-element.108), channel_id=1, source_target_pairs={{0,195},{1,192},{2,193},{3,194},{4,199},{5,196},{6,197},{7,198},{8... | collective-permute-start | bytes 196616 | tf_op jit(solution)/shard_map/ppermute | solution.py:374
  85.5 2.9 %shard_map.79.dq_ref = bf16[128,512]{1,0:T(8,128)(2,1)S(1)} custom-call(s32[7]{0:T(128)S(1)} %stack.23.where_ref, bf16[128,512]{1,0:T(8,128)(2,1)S(1)} %collective-permute-done.18.g_ref, bf16[512,512]{1,0:T(8,128)(2,1)S(1)} %bitcast.28, bf16[128,512]{1,0:T(8,128)(2,1)S(1)} %get-tuple-element.80.mixed_ref, bf16[768,1024]{1,0:T(8,128)(2,1)S(1)} %get-tuple-element.81.kv_ref, ...), custom_call_target="tpu_custom_call" | custom-call | flops 536870912 | bytes 4194304 | tf_op jit(solution)/shard_map/pallas_call | solution.py:352
  88.5 4.6 %collective-permute-start.22 = (bf16[256,512]{1,0:T(8,128)(2,1)S(1)}, bf16[256,512]{1,0:T(8,128)(2,1)S(1)}, u32[]{:S(2)}, u32[]{:S(2)}) collective-permute-start(bf16[256,512]{1,0:T(8,128)(2,1)S(1)} %constant_dynamic-update-slice_fusion.9.g0), channel_id=1, source_target_pairs={{0,60},{1,61},{2,62},{3,63},{4,8},{5,9},{6,10},{7,11},{8,4},{9,5},... | collective-permute-start | bytes 786440 | tf_op jit(solution)/shard_map/ppermute | solution.py:374
  93.0 4.1 %collective-permute-done.22.g2 = bf16[256,512]{1,0:T(8,128)(2,1)S(1)} collective-permute-done((bf16[256,512]{1,0:T(8,128)(2,1)S(1)}, bf16[256,512]{1,0:T(8,128)(2,1)S(1)}, u32[]{:S(2)}, u32[]{:S(2)}) %collective-permute-start.22) | collective-permute-done | bytes 262176 | tf_op jit(solution)/shard_map/ppermute | solution.py:374
  97.1 2.7 %shard_map.80 = (bf16[128,2048]{1,0:T(8,128)(2,1)S(1)}, bf16[256,512]{1,0:T(8,128)(2,1)S(1)}) custom-call(s32[7]{0:T(128)S(1)} %stack.23.where_ref, bf16[256,512]{1,0:T(8,128)(2,1)S(1)} %constant_dynamic-update-slice_fusion.9.g0, bf16[256,512]{1,0:T(8,128)(2,1)S(1)} %collective-permute-done.21.g1, bf16[256,512]{1,0:T(8,128)(2,1)S(1)} %collective-permute-done.22.g2, ...), custom_call_target="tpu_custom_call" | custom-call | flops 1073741824 | bytes 4194304 | tf_op jit(solution)/shard_map/pallas_call | solution.py:352
  107.3 2.0 %shard_map.82 = f32[128,512]{1,0:T(8,128)} custom-call(s32[7]{0:T(128)S(1)} %stack.23.where_ref, bf16[128,2048]{1,0:T(8,128)(2,1)S(1)} %get-tuple-element.112.d0.dp_ref, bf16[128,512]{1,0:T(8,128)(2,1)S(1)} %collective-permute-done.18.g_ref, bf16[512,1536]{1,0:T(8,128)(2,1)S(1)} %bitcast.20, bf16[128,512]{1,0:T(8,128)(2,1)S(1)} %bitcast.35, ...), custom_call_target="tpu_custom_call" | custom-call | flops 268435456 | bytes 4194304 | tf_op jit(solution)/shard_map/pallas_call | solution.py:352
  109.3 3.5 %collective-permute-done.24.refs_3_ = bf16[64,2048]{1,0:T(8,128)(2,1)S(1)} collective-permute-done((bf16[64,2048]{1,0:T(8,128)(2,1)S(1)}, bf16[64,2048]{1,0:T(8,128)(2,1)S(1)}, u32[]{:S(2)}, u32[]{:S(2)}) %collective-permute-start.24) | collective-permute-done | bytes 262176 | tf_op jit(solution)/shard_map/ppermute | solution.py:374
  112.8 4.8 %collective-permute-done.25.refs_1_ = bf16[64,2048]{1,0:T(8,128)(2,1)S(1)} collective-permute-done((bf16[64,2048]{1,0:T(8,128)(2,1)S(1)}, bf16[64,2048]{1,0:T(8,128)(2,1)S(1)}, u32[]{:S(2)}, u32[]{:S(2)}) %collective-permute-start.25) | collective-permute-done | bytes 262176 | tf_op jit(solution)/shard_map/ppermute | solution.py:374
  119.7 16.7 %all_to_all.5.part_ref = bf16[8,8,2048]{2,1,0:T(8,128)(2,1)S(1)} all-to-all(bf16[8,8,2048]{2,1,0:T(8,128)(2,1)S(1)} %bitcast.38), channel_id=1, replica_groups=mesh['pipe'=4,'z'=8,'core'=2,'col'=4] {'z'}, dimensions={0} | all-to-all | bytes 524288 | tf_op jit(solution)/shard_map/all_to_all | solution.py:482
  (78 shorter events, 36.6 us)
Async XLA Ops:
  2.2 5.7 %collective-permute-start = (bf16[64,512]{1,0:T(8,128)(2,1)S(1)}, bf16[64,512]{1,0:T(8,128)(2,1)S(1)}, u32[]{:S(2)}, u32[]{:S(2)}) collective-permute-start(bf16[64,512]{1,0:T(8,128)(2,1)S(1)} %get-tuple-element.66), channel_id=1, source_target_pairs={{0,1},{1,2},{2,3},{3,0},{4,5},{5,6},{6,7},{7,4},{8,9},{9,10},{10,1... | collective-permute-start | bytes 196616 | tf_op jit(solution)/shard_map/ppermute | solution.py:374
  4.5 5.5 %collective-permute-start.1 = (bf16[64,512]{1,0:T(8,128)(2,1)S(1)}, bf16[64,512]{1,0:T(8,128)(2,1)S(1)}, u32[]{:S(2)}, u32[]{:S(2)}) collective-permute-start(bf16[64,512]{1,0:T(8,128)(2,1)S(1)} %get-tuple-element.67), channel_id=1, source_target_pairs={{0,3},{1,0},{2,1},{3,2},{4,7},{5,4},{6,5},{7,6},{8,11},{9,8},{10,9... | collective-permute-start | bytes 196616 | tf_op jit(solution)/shard_map/ppermute | solution.py:374
  10.0 7.0 %collective-permute-start.3 = (bf16[256,512]{1,0:T(8,128)(2,1)S(1)}, bf16[256,512]{1,0:T(8,128)(2,1)S(1)}, u32[]{:S(2)}, u32[]{:S(2)}) collective-permute-start(bf16[256,512]{1,0:T(8,128)(2,1)S(1)} %constant_dynamic-update-slice_fusion.12), channel_id=1, source_target_pairs={{0,60},{1,61},{2,62},{3,63},{4,8},{5,9},{6,10},{7,11},{8,4},{9,5},... | collective-permute-start | bytes 786440 | tf_op jit(solution)/shard_map/ppermute | solution.py:374
  21.0 7.0 %collective-permute-start.4 = (bf16[64,640]{1,0:T(8,128)(2,1)S(1)}, bf16[64,640]{1,0:T(8,128)(2,1)S(1)}, u32[]{:S(2)}, u32[]{:S(2)}) collective-permute-start(bf16[64,640]{1,0:T(8,128)(2,1)S(1)} %get-tuple-element.77), channel_id=1, source_target_pairs={{0,1},{1,2},{2,3},{3,0},{4,5},{5,6},{6,7},{7,4},{8,9},{9,10},{10,1... | collective-permute-start | bytes 245768 | tf_op jit(solution)/shard_map/ppermute | solution.py:374
  22.4 5.7 %collective-permute-start.5 = (bf16[64,640]{1,0:T(8,128)(2,1)S(1)}, bf16[64,640]{1,0:T(8,128)(2,1)S(1)}, u32[]{:S(2)}, u32[]{:S(2)}) collective-permute-start(bf16[64,640]{1,0:T(8,128)(2,1)S(1)} %get-tuple-element.78), channel_id=1, source_target_pairs={{0,3},{1,0},{2,1},{3,2},{4,7},{5,4},{6,5},{7,6},{8,11},{9,8},{10,9... | collective-permute-start | bytes 245768 | tf_op jit(solution)/shard_map/ppermute | solution.py:374
  28.1 7.8 %collective-permute-start.7 = (bf16[256,640]{1,0:T(8,128)(2,1)S(1)}, bf16[256,640]{1,0:T(8,128)(2,1)S(1)}, u32[]{:S(2)}, u32[]{:S(2)}) collective-permute-start(bf16[256,640]{1,0:T(8,128)(2,1)S(1)} %constant_dynamic-update-slice_fusion.p0.g0), channel_id=1, source_target_pairs={{0,60},{1,61},{2,62},{3,63},{4,8},{5,9},{6,10},{7,11},{8,4},{9,5},... | collective-permute-start | bytes 983048 | tf_op jit(solution)/shard_map/ppermute | solution.py:374
  30.1 5.7 %collective-permute-start.6 = (bf16[256,640]{1,0:T(8,128)(2,1)S(1)}, bf16[256,640]{1,0:T(8,128)(2,1)S(1)}, u32[]{:S(2)}, u32[]{:S(2)}) collective-permute-start(bf16[256,640]{1,0:T(8,128)(2,1)S(1)} %constant_dynamic-update-slice_fusion.p0.g0), channel_id=1, source_target_pairs={{0,4},{1,5},{2,6},{3,7},{4,0},{5,1},{6,2},{7,3},{8,12},{9,13},{10,... | collective-permute-start | bytes 983048 | tf_op jit(solution)/shard_map/ppermute | solution.py:374
  38.6 8.7 %collective-permute-start.8 = (bf16[128,512]{1,0:T(8,128)(2,1)S(1)}, bf16[128,512]{1,0:T(8,128)(2,1)S(1)}, u32[]{:S(2)}, u32[]{:S(2)}) collective-permute-start(bf16[128,512]{1,0:T(8,128)(2,1)S(1)} %get-tuple-element.88), channel_id=1, source_target_pairs={{0,192},{1,193},{2,194},{3,195},{4,196},{5,197},{6,198},{7,199},{8... | collective-permute-start | bytes 393224 | tf_op jit(solution)/shard_map/ppermute | solution.py:374
  44.1 5.2 %collective-permute-start.9 = (bf16[64,512]{1,0:T(8,128)(2,1)S(1)}, bf16[64,512]{1,0:T(8,128)(2,1)S(1)}, u32[]{:S(2)}, u32[]{:S(2)}) collective-permute-start(bf16[64,512]{1,0:T(8,128)(2,1)S(1)} %get-tuple-element.89), channel_id=1, source_target_pairs={{0,193},{1,194},{2,195},{3,192},{4,197},{5,198},{6,199},{7,196},{8... | collective-permute-start | bytes 196616 | tf_op jit(solution)/shard_map/ppermute | solution.py:374
  45.3 6.4 %collective-permute-start.10 = (bf16[64,512]{1,0:T(8,128)(2,1)S(1)}, bf16[64,512]{1,0:T(8,128)(2,1)S(1)}, u32[]{:S(2)}, u32[]{:S(2)}) collective-permute-start(bf16[64,512]{1,0:T(8,128)(2,1)S(1)} %get-tuple-element.91), channel_id=1, source_target_pairs={{0,195},{1,192},{2,193},{3,194},{4,199},{5,196},{6,197},{7,198},{8... | collective-permute-start | bytes 196616 | tf_op jit(solution)/shard_map/ppermute | solution.py:374
  51.6 7.0 %collective-permute-start.12 = (bf16[256,512]{1,0:T(8,128)(2,1)S(1)}, bf16[256,512]{1,0:T(8,128)(2,1)S(1)}, u32[]{:S(2)}, u32[]{:S(2)}) collective-permute-start(bf16[256,512]{1,0:T(8,128)(2,1)S(1)} %constant_dynamic-update-slice_fusion.3.g0), channel_id=1, source_target_pairs={{0,60},{1,61},{2,62},{3,63},{4,8},{5,9},{6,10},{7,11},{8,4},{9,5},... | collective-permute-start | bytes 786440 | tf_op jit(solution)/shard_map/ppermute | solution.py:374
  53.5 5.2 %collective-permute-start.11 = (bf16[256,512]{1,0:T(8,128)(2,1)S(1)}, bf16[256,512]{1,0:T(8,128)(2,1)S(1)}, u32[]{:S(2)}, u32[]{:S(2)}) collective-permute-start(bf16[256,512]{1,0:T(8,128)(2,1)S(1)} %constant_dynamic-update-slice_fusion.3.g0), channel_id=1, source_target_pairs={{0,4},{1,5},{2,6},{3,7},{4,0},{5,1},{6,2},{7,3},{8,12},{9,13},{10,... | collective-permute-start | bytes 786440 | tf_op jit(solution)/shard_map/ppermute | solution.py:374
  59.3 6.4 %collective-permute-start.13 = (bf16[128,512]{1,0:T(8,128)(2,1)S(1)}, bf16[128,512]{1,0:T(8,128)(2,1)S(1)}, u32[]{:S(2)}, u32[]{:S(2)}) collective-permute-start(bf16[128,512]{1,0:T(8,128)(2,1)S(1)} %get-tuple-element.97), channel_id=1, source_target_pairs={{0,192},{1,193},{2,194},{3,195},{4,196},{5,197},{6,198},{7,199},{8... | collective-permute-start | bytes 393224 | tf_op jit(solution)/shard_map/ppermute | solution.py:374
  60.7 6.5 %collective-permute-start.14 = (bf16[64,512]{1,0:T(8,128)(2,1)S(1)}, bf16[64,512]{1,0:T(8,128)(2,1)S(1)}, u32[]{:S(2)}, u32[]{:S(2)}) collective-permute-start(bf16[64,512]{1,0:T(8,128)(2,1)S(1)} %get-tuple-element.98), channel_id=1, source_target_pairs={{0,193},{1,194},{2,195},{3,192},{4,197},{5,198},{6,199},{7,196},{8... | collective-permute-start | bytes 196616 | tf_op jit(solution)/shard_map/ppermute | solution.py:374
  65.3 6.4 %collective-permute-start.15 = (bf16[64,512]{1,0:T(8,128)(2,1)S(1)}, bf16[64,512]{1,0:T(8,128)(2,1)S(1)}, u32[]{:S(2)}, u32[]{:S(2)}) collective-permute-start(bf16[64,512]{1,0:T(8,128)(2,1)S(1)} %get-tuple-element.100), channel_id=1, source_target_pairs={{0,195},{1,192},{2,193},{3,194},{4,199},{5,196},{6,197},{7,198},{8... | collective-permute-start | bytes 196616 | tf_op jit(solution)/shard_map/ppermute | solution.py:374
  71.7 7.0 %collective-permute-start.17 = (bf16[256,512]{1,0:T(8,128)(2,1)S(1)}, bf16[256,512]{1,0:T(8,128)(2,1)S(1)}, u32[]{:S(2)}, u32[]{:S(2)}) collective-permute-start(bf16[256,512]{1,0:T(8,128)(2,1)S(1)} %constant_dynamic-update-slice_fusion.6.g0), channel_id=1, source_target_pairs={{0,60},{1,61},{2,62},{3,63},{4,8},{5,9},{6,10},{7,11},{8,4},{9,5},... | collective-permute-start | bytes 786440 | tf_op jit(solution)/shard_map/ppermute | solution.py:374
  73.4 5.3 %collective-permute-start.16 = (bf16[256,512]{1,0:T(8,128)(2,1)S(1)}, bf16[256,512]{1,0:T(8,128)(2,1)S(1)}, u32[]{:S(2)}, u32[]{:S(2)}) collective-permute-start(bf16[256,512]{1,0:T(8,128)(2,1)S(1)} %constant_dynamic-update-slice_fusion.6.g0), channel_id=1, source_target_pairs={{0,4},{1,5},{2,6},{3,7},{4,0},{5,1},{6,2},{7,3},{8,12},{9,13},{10,... | collective-permute-start | bytes 786440 | tf_op jit(solution)/shard_map/ppermute | solution.py:374
  79.6 6.0 %collective-permute-start.18 = (bf16[128,512]{1,0:T(8,128)(2,1)S(1)}, bf16[128,512]{1,0:T(8,128)(2,1)S(1)}, u32[]{:S(2)}, u32[]{:S(2)}) collective-permute-start(bf16[128,512]{1,0:T(8,128)(2,1)S(1)} %get-tuple-element.105), channel_id=1, source_target_pairs={{0,192},{1,193},{2,194},{3,195},{4,196},{5,197},{6,198},{7,199},{8... | collective-permute-start | bytes 393224 | tf_op jit(solution)/shard_map/ppermute | solution.py:374
  80.9 7.5 %collective-permute-start.19 = (bf16[64,512]{1,0:T(8,128)(2,1)S(1)}, bf16[64,512]{1,0:T(8,128)(2,1)S(1)}, u32[]{:S(2)}, u32[]{:S(2)}) collective-permute-start(bf16[64,512]{1,0:T(8,128)(2,1)S(1)} %get-tuple-element.106), channel_id=1, source_target_pairs={{0,193},{1,194},{2,195},{3,192},{4,197},{5,198},{6,199},{7,196},{8... | collective-permute-start | bytes 196616 | tf_op jit(solution)/shard_map/ppermute | solution.py:374
  81.3 7.1 %collective-permute-start.20 = (bf16[64,512]{1,0:T(8,128)(2,1)S(1)}, bf16[64,512]{1,0:T(8,128)(2,1)S(1)}, u32[]{:S(2)}, u32[]{:S(2)}) collective-permute-start(bf16[64,512]{1,0:T(8,128)(2,1)S(1)} %get-tuple-element.108), channel_id=1, source_target_pairs={{0,195},{1,192},{2,193},{3,194},{4,199},{5,196},{6,197},{7,198},{8... | collective-permute-start | bytes 196616 | tf_op jit(solution)/shard_map/ppermute | solution.py:374
  88.5 8.6 %collective-permute-start.22 = (bf16[256,512]{1,0:T(8,128)(2,1)S(1)}, bf16[256,512]{1,0:T(8,128)(2,1)S(1)}, u32[]{:S(2)}, u32[]{:S(2)}) collective-permute-start(bf16[256,512]{1,0:T(8,128)(2,1)S(1)} %constant_dynamic-update-slice_fusion.9.g0), channel_id=1, source_target_pairs={{0,60},{1,61},{2,62},{3,63},{4,8},{5,9},{6,10},{7,11},{8,4},{9,5},... | collective-permute-start | bytes 786440 | tf_op jit(solution)/shard_map/ppermute | solution.py:374
  103.1 9.7 %collective-permute-start.24 = (bf16[64,2048]{1,0:T(8,128)(2,1)S(1)}, bf16[64,2048]{1,0:T(8,128)(2,1)S(1)}, u32[]{:S(2)}, u32[]{:S(2)}) collective-permute-start(bf16[64,2048]{1,0:T(8,128)(2,1)S(1)} %get-tuple-element.114), channel_id=1, source_target_pairs={{0,3},{1,0},{2,1},{3,2},{4,7},{5,4},{6,5},{7,6},{8,11},{9,8},{10,9... | collective-permute-start | bytes 786440 | tf_op jit(solution)/shard_map/ppermute | solution.py:374
  104.6 13.0 %collective-permute-start.25 = (bf16[64,2048]{1,0:T(8,128)(2,1)S(1)}, bf16[64,2048]{1,0:T(8,128)(2,1)S(1)}, u32[]{:S(2)}, u32[]{:S(2)}) collective-permute-start(bf16[64,2048]{1,0:T(8,128)(2,1)S(1)} %get-tuple-element.118), channel_id=1, source_target_pairs={{0,1},{1,2},{2,3},{3,0},{4,5},{5,6},{6,7},{7,4},{8,9},{9,10},{10,1... | collective-permute-start | bytes 786440 | tf_op jit(solution)/shard_map/ppermute | solution.py:374
  106.4 12.6 %collective-permute-start.26 = (bf16[64,2048]{1,0:T(8,128)(2,1)S(1)}, bf16[64,2048]{1,0:T(8,128)(2,1)S(1)}, u32[]{:S(2)}, u32[]{:S(2)}) collective-permute-start(bf16[64,2048]{1,0:T(8,128)(2,1)S(1)} %get-tuple-element.119), channel_id=1, source_target_pairs={{0,2},{1,3},{2,0},{3,1},{4,6},{5,7},{6,4},{7,5},{8,10},{9,11},{10,... | collective-permute-start | bytes 786440 | tf_op jit(solution)/shard_map/ppermute | solution.py:374
  (10 other events, 51.1 us)
where the time goes:
time: 139 us; the launch traced here: 138 us
  waiting for transfers between devices  51.7 us (37%)
  starting transfers between devices  40.5 us (29%)
  Pallas kernels  24.3 us (17%)
  blocking collectives  16.7 us (12%)
  local copies, waits for them, and re-layouts  3.49 us (3%)
    ppermute x27, waiting for transfers between devices, routed(): return lax.ppermute(block, AXES, pairs)  51.7 us
    ppermute x27, starting transfers between devices, routed(): return lax.ppermute(block, AXES, pairs)  40.5 us
    pallas_call x18, Pallas kernels, call(): pl.pallas_call(kernel, out_shape=[jax.ShapeDtypeStruct(s, t) for s, t in...  24.3 us
    all_to_all x1, blocking collectives, body(): part = lax.all_to_all(part, 'z', 0, 0, tiled=True)  16.7 us
    unnamed x22, local copies, waits for them, and re-layouts  3.36 us
  transfers between devices with their start and end apart: 27, of which 16 were waited for; matrix products, arithmetic and copies ran while one was open for 0% of the time, Pallas kernels for 7%

commit v1 on v0

--- a/solution.py
+++ b/solution.py
@@ -79,29 +79,28 @@
     right_ref[...] = sides[:, 1].reshape(64, -1).astype(BF16)
 
 
-def first_kernel(where_ref, x_ref, base_ref, left_ref, right_ref):
-    base_ref[:TOK] = x_ref[...]
-    base_ref[TOK:] = jnp.zeros((TOK, D), BF16)
-    put_sides(x_ref[...].astype(F32), left_ref, right_ref)
-
-
 def normed_low(x_ref):
     x = x_ref[...].astype(F32)
     inverse = lax.rsqrt(jnp.mean(x * x, axis=-1, keepdims=True) + 1e-06)
     return (x * inverse).astype(BF16)
 
 
-def centre_kernel(where_ref, x_ref, w_ref, cot_ref, proj_ref, nlow_ref, cot_low_ref):
+def centre_kernel(where_ref, x_ref, w_ref, base_ref, proj_ref, nlow_ref):
+    base_ref[:TOK] = x_ref[...]
+    base_ref[TOK:] = jnp.zeros((TOK, D), BF16)
     low = normed_low(x_ref)
     nlow_ref[...] = low
     proj_ref[...] = nn(low, w_ref[...]).astype(BF16)
-    cot_low_ref[...] = cot_ref[...].astype(BF16)
-
-
-def side_kernel(where_ref, left_ref, right_ref, w_ref, wo_ref, cot_ref, proj_ref, dm_ref):
+
+
+def side_kernel(
+    where_ref, left_ref, right_ref, w_ref, wo_ref, cot_ref, proj_ref, cot_low_ref, dm_ref
+):
     low = jnp.concatenate([normed_low(left_ref), normed_low(right_ref)], axis=0)
     proj_ref[...] = nn(low, w_ref[...]).astype(BF16)
-    dm_ref[...] = nt(cot_ref[...], wo_ref[...]).astype(BF16)
+    grad = cot_ref[...].astype(BF16)
+    cot_low_ref[...] = grad
+    dm_ref[...] = nt(grad, wo_ref[...]).astype(BF16)
 
 
 def forward_kernel(
@@ -175,7 +174,7 @@
 
 
 def key_probs_kernel(
-    where_ref, p0, p1, p2, proj_ref, query_ref, prob_ref, mixed_ref, delta_ref
+    where_ref, p0, p1, p2, proj_ref, query_ref, prob_ref, mixed_ref, delta_ref, total_ref
 ):
     head = lax.broadcasted_iota(jnp.int32, (8, 128), 0)
     lane = lax.broadcasted_iota(jnp.int32, (8, 128), 1)
@@ -191,15 +190,20 @@
         for piece, p in enumerate((p0, p1, p2)):
             mixed_ref[:, piece * OWN : (piece + 1) * OWN] = p[:, :D].astype(F32).T.astype(BF16)
 
+    total_ref[...] = log_total
     ok = window(where_ref, True)
-    for pair in range(PAIRS):
-        key = two_heads(proj_ref[:, D + 128 * pair : D + 128 * pair + 128] * 0.125)
-        scores = nn(key, query_ref[128 * pair : 128 * pair + 128])
+
+    def one_pair(pair, carry):
+        low = pl.multiple_of(128 * pair, 128)
+        key = two_heads(proj_ref[:, pl.ds(low + D, 128)] * 0.125)
+        scores = nn(key, query_ref[pl.ds(low, 128)])
         for side in range(2):
-            at = 2 * pair + side
-            part = scores[TOK * side : TOK * side + TOK] - log_total[at : at + 1]
+            part = scores[TOK * side : TOK * side + TOK] - total_ref[pl.ds(2 * pair + side, 1)]
             probs = jnp.exp(jnp.where(ok, part, -1e30))
             prob_ref[pair, TOK * side : TOK * side + TOK] = probs.astype(BF16)
+        return carry
+
+    lax.fori_loop(0, PAIRS, one_pair, 0)
 
 
 def two_sums(grad, mixed):
@@ -214,7 +218,16 @@
     )
 
 
-def query_kernel(where_ref, g_ref, w_ref, mixed_ref, kv_ref, prob_ref, dq_ref, dm_ref, *, turn):
+def query_kernel(
+    where_ref, g_ref, w_ref, mixed_ref, kv_ref, prob_ref, *rest, turn
+):
+    (dq_ref, dm_ref), prev = rest[-2:], rest[:-2]
+    for ref in prev:
+
+        @pl.when(where_ref[5] != turn)
+        def _():
+            dq_ref[...] = ref[:, :D]
+
     @pl.when(where_ref[5] == turn)
     def _():
         dm_ref[...] = nt(g_ref[...], w_ref[...]).astype(BF16)
@@ -238,14 +251,13 @@
 
 
 def key_kernel(
-    where_ref, g0, g1, g2, wo_ref, delta_ref, proj_ref, query_ref, prob_ref, dq_ref, mixed_ref,
-    *rest, turn, last,
+    where_ref, g0, g1, g2, wo_ref, delta_ref, proj_ref, query_ref, prob_ref, *rest, turn, last
 ):
-    ins, rest = ((), rest) if last else (rest[:3], rest[3:])
-    prev = (3 - last) if turn else 0
-    prev, rest = rest[:prev], rest[prev:]
-    outs, sends, dm_ref = rest[: 3 - last], rest[3 - last : -1], rest[-1]
-    dp_ref, gl_ref = outs[:2]
+    ins, rest = ((), rest) if last else (rest[:4], rest[4:])
+    count = 1 if last else 3
+    prev, rest = (rest[:count], rest[count:]) if turn else ((), rest)
+    outs, sends, dm_ref = rest[:count], rest[count:-1], rest[-1]
+    kv_ref = outs[0] if last else outs[0].at[:, D:]
     active = where_ref[5] == turn
 
     if prev:
@@ -253,17 +265,13 @@
         @pl.when(jnp.logical_not(active))
         def _():
             for new, old in zip(outs, prev):
-                new[...] = old[...]
+                new[...] = old[:, D:] if last else old[...]
 
     @pl.when(active)
     def _():
         for piece, g in enumerate((g0, g1, g2)):
-            d_mixed = nt(wo_ref[...], g[:, :D]).astype(BF16)
+            d_mixed = nt(wo_ref[...], g[:OWN, :D]).astype(BF16)
             dm_ref[:, piece * OWN : (piece + 1) * OWN] = d_mixed
-        dp_ref[:, :D] = dq_ref[...]
-        dp_ref[:, 3 * D :] = mixed_ref[...]
-        gl_ref[:TOK] = g0[:TOK, :D]
-        gl_ref[TOK:] = g1[:TOK, :D]
         for pair in range(PAIRS):
             at = slice(128 * pair, 128 * pair + 128)
             value = two_heads(proj_ref[:, 2 * D + 128 * pair : 2 * D + 128 * pair + 128])
@@ -283,19 +291,21 @@
                     (probs[rows].astype(F32) * (pressure[rows] - deltas[side])).astype(BF16)
                 )
             d_key = nt(query_ref[at], jnp.concatenate(slopes, axis=0))
-            low, high = D + 128 * pair, D + 128 * pair + 128
-            dp_ref[:, low:high] = (turned_block(d_key) * 0.125).astype(BF16)
-            dp_ref[:, D + low : D + high] = turned_block(d_value).astype(BF16)
+            kv_ref[:, at] = (turned_block(d_key) * 0.125).astype(BF16)
+            kv_ref[:, D + 128 * pair : D + 128 * pair + 128] = turned_block(d_value).astype(BF16)
         if not last:
-            out = input_grad(dp_ref, *ins)
+            dq_ref, *ins_rest = ins
+            outs[0][:, :D] = dq_ref[...]
+            outs[1][:TOK] = g0[:TOK, :D]
+            outs[1][TOK:] = g1[:TOK, :D]
+            out = input_grad(nt(outs[0][...], ins_rest[1][...]), ins_rest[0], ins_rest[2])
             outs[2][...] = out
             low_ref, left_ref, right_ref = sends
             low_ref[...] = out.astype(BF16)
             put_sides(out, left_ref, right_ref)
 
 
-def input_grad(dp_ref, g_ref, wq_ref, x_ref):
-    d_normed = nt(dp_ref[:, : 3 * D], wq_ref[...])
+def input_grad(d_normed, g_ref, x_ref):
     x = x_ref[...].astype(F32)
     inverse = lax.rsqrt(jnp.mean(x * x, axis=-1, keepdims=True) + 1e-06)
     normed = x * inverse
@@ -303,51 +313,77 @@
     return g_ref[...].astype(F32) + inverse * (d_normed - normed * inner)
 
 
-def input_kernel(where_ref, dp_ref, g_ref, wq_ref, x_ref, prev_ref, in_ref, *, turn):
+def input_kernel(where_ref, dq_ref, kv_ref, g_ref, wq_ref, x_ref, prev_ref, in_ref, *, turn):
     @pl.when(where_ref[5] == turn)
     def _():
-        in_ref[...] = input_grad(dp_ref, g_ref, wq_ref, x_ref)
+        d_normed = nt(dq_ref[...], wq_ref[:, :D]) + nt(kv_ref[...], wq_ref[:, D:])
+        in_ref[...] = input_grad(d_normed, g_ref, x_ref)
 
     @pl.when(where_ref[5] != turn)
     def _():
         in_ref[...] = prev_ref[...]
 
 
-def weight_kernel(where_ref, nt_ref, d0, d1, g_ref, *refs):
-    outs, (left_ref, full_ref) = refs[:-2], refs[-2:]
-    d_proj = jnp.concatenate([d0[:, : 3 * D], d1[:, : 3 * D]], axis=0)
-    mixed = jnp.concatenate([d0[:, 3 * D :], d1[:, 3 * D :]], axis=0)
-    full_ref[...] = tn(mixed, g_ref[...])
-    left_ref[...] = nn(nt_ref[...], d_proj)
-    core, cols = where_ref[2], len(outs)
+def split_rows(where_ref, parts, outs):
+    cols = len(outs)
     for distance, out_ref in enumerate(outs):
         col = lax.rem(where_ref[6] + distance, cols)
-        for at, ref, step, first in (
-            (slice(0, 3 * D), left_ref, BLOCK, 0), (slice(3 * D, 4 * D), full_ref, 2 * BLOCK, core)
-        ):
+        for at, ref, step, first in parts:
             rows = [
-                ref[pl.ds(pl.multiple_of(step * chip + first * BLOCK + 8 * col, 8), 8)]
+                ref[pl.ds(pl.multiple_of(step * chip + first + 8 * col, 8), 8)]
                 for chip in range(out_ref.shape[0] // 8)
             ]
             out_ref[:, at] = jnp.concatenate(rows, axis=0).astype(BF16)
 
 
+def early_kernel(where_ref, nt_ref, dq_ref, mixed_ref, g0, m, prev_ref, *refs, turn):
+    outs, (left_ref, full_ref, g_ref) = refs[:-3], refs[-3:]
+
+    @pl.when(where_ref[5] == turn)
+    def _():
+        g_ref[:TOK] = g0[:TOK]
+        g_ref[TOK:] = m[:TOK]
+
+    @pl.when(where_ref[5] != turn)
+    def _():
+        g_ref[...] = prev_ref[...]
+
+    d_query = jnp.concatenate([dq_ref[...], m[OWN : OWN + TOK]], axis=0)
+    left_ref[...] = nn(nt_ref[...], d_query)
+    mixed = jnp.concatenate([mixed_ref[...], m[OWN + TOK :]], axis=0)
+    full_ref[...] = tn(mixed, g_ref[...])
+    split_rows(
+        where_ref,
+        [(slice(0, D), left_ref, BLOCK, 0), (slice(D, 2 * D), full_ref, 2 * BLOCK, where_ref[2] * BLOCK)],
+        outs,
+    )
+
+
+def late_kernel(where_ref, nt_ref, d0, d1, *refs):
+    outs, left_ref = refs[:-1], refs[-1]
+    left_ref[...] = nn(nt_ref[...], jnp.concatenate([d0[...], d1[...]], axis=0))
+    split_rows(where_ref, [(slice(0, 2 * D), left_ref, BLOCK, 0)], outs)
+
+
 def col_total_kernel(where_ref, *refs):
-    total = refs[0][...].astype(F32)
-    for ref in refs[1:-1]:
-        total = total + ref[...].astype(F32)
-    refs[-1][...] = total.astype(BF16)
+    count = (len(refs) - 1) // 2
+    for at, parts in ((slice(0, 2 * D), refs[:count]), (slice(2 * D, 4 * D), refs[count:-1])):
+        total = parts[0][...].astype(F32)
+        for ref in parts[1:]:
+            total = total + ref[...].astype(F32)
+        refs[-1][:, at] = total.astype(BF16)
 
 
 def total_kernel(where_ref, part_ref, qkv_ref, out_ref, *, scale):
     total = part_ref[0].astype(F32)
     for source in range(1, part_ref.shape[0]):
         total = total + part_ref[source].astype(F32)
-    qkv_ref[...] = total[:, : 3 * D] * scale
-    out_ref[...] = total[:, 3 * D :] * scale
-
-
-def call(kernel, outs, *args, scratch=(), flops=0):
+    qkv_ref[:, :D] = total[:, :D] * scale
+    qkv_ref[:, D:] = total[:, 2 * D :] * scale
+    out_ref[...] = total[:, D : 2 * D] * scale
+
+
+def call(kernel, outs, *args, scratch=(), flops=0, moved=4 << 20):
     vmem = pl.BlockSpec(memory_space=pltpu.VMEM)
     return pl.pallas_call(
         kernel,
@@ -356,16 +392,16 @@
         out_specs=[vmem] * len(outs),
         scratch_shapes=list(scratch),
         compiler_params=pltpu.CompilerParams(vmem_limit_bytes=VMEM_LIMIT),
-        cost_estimate=pl.CostEstimate(flops=flops, bytes_accessed=4 << 20, transcendentals=0),
+        cost_estimate=pl.CostEstimate(flops=flops, bytes_accessed=moved, transcendentals=0),
     )(*args)
 
 
 def body(sizes, activations, qkv_weight, out_weight, cotangent):
     pipes, chips, cols = sizes
 
-    def routed(block, step):
+    def routed(block, step, plane=None):
         pairs = []
-        for p in range(pipes):
+        for p in range(pipes) if plane is None else (plane,):
             for r in range(2 * chips):
                 for c in range(cols):
                     p2, r2, c2 = step(p, r, c)
@@ -381,10 +417,12 @@
     def mate(p, r, c):
         return p, r ^ 1, c
 
-    def row_rims(pieces):
+    def row_rims(pieces, plane=None, extra=()):
         own = jnp.concatenate(pieces, axis=0)
-        beyond = routed(own, lambda p, r, c: (p, r - 1 + 2 * (r & 1), c))
-        return own, routed(own, mate), beyond
+        beyond = routed(own, lambda p, r, c: (p, r - 1 + 2 * (r & 1), c), plane)
+        if extra:
+            return own, routed(jnp.concatenate([*pieces, *extra], axis=0), mate), beyond
+        return own, routed(own, mate, plane), beyond
 
     pipe, z, core, col = (lax.axis_index(axis) for axis in AXES)
     x = activations.reshape(TOK, D)
@@ -395,20 +433,18 @@
         [8 * (2 * z + core), 16 * col, core, row_total, col_total, pipes - 1 - pipe, col]
     ).astype(jnp.int32)
 
-    base, low_side, high_side = call(
-        first_kernel, [((OWN, D), BF16), ((64, D), BF16), ((64, D), BF16)], where, x
-    )
-    proj, nlow, cot_low = call(
-        centre_kernel, [((TOK, 3 * D), BF16), ((TOK, D), BF16), ((TOK, D), BF16)],
-        where, x, w_qkv, cot, flops=1 << 28,
+    x_sides = x.reshape(8, 2, 8, D)
+    low_side, high_side = x_sides[:, 0].reshape(64, D), x_sides[:, 1].reshape(64, D)
+    base, proj, nlow = call(
+        centre_kernel, [((OWN, D), BF16), ((TOK, 3 * D), BF16), ((TOK, D), BF16)],
+        where, x, w_qkv, flops=1 << 28,
     )
     left, right = col_rims(low_side, high_side)
-    base, proj = lax.optimization_barrier((base, proj))
     own = lax.dynamic_update_slice(base, left, (TOK, 0))
     own, near, far = row_rims([lax.dynamic_update_slice(own, right, (TOK + 64, 0))])
-    side_proj, d_mixed = call(
-        side_kernel, [((TOK, 3 * D), BF16), ((TOK, D), BF16)],
-        where, left, right, w_qkv, w_out, cot_low, flops=1 << 28,
+    side_proj, cot_low, d_mixed = call(
+        side_kernel, [((TOK, 3 * D), BF16), ((TOK, D), BF16), ((TOK, D), BF16)],
+        where, left, right, w_qkv, w_out, cot, flops=1 << 28,
     )
     wide = D + 128
     kv, q_probs, nlow_mate, low_far, mixed, pack, low_side, high_side = call(
@@ -425,10 +461,10 @@
         scratch=[pltpu.VMEM((D, OWN), F32)], flops=1 << 28,
     )
 
-    def query_side(turn, gradient):
+    def query_side(turn, gradient, *prev):
         return call(
             functools.partial(query_kernel, turn=turn), [((TOK, D), BF16)],
-            where, gradient, w_out, mixed, kv, q_probs,
+            where, gradient, w_out, mixed, kv, q_probs, *prev,
             scratch=[pltpu.VMEM((TOK, D), BF16)], flops=1 << 29,
         )[0]
 
@@ -439,45 +475,63 @@
     k_probs, mixed_turned, delta = call(
         key_probs_kernel,
         [((PAIRS, OWN, REGION), BF16), ((D, REGION), BF16), ((8, REGION), F32)],
-        where, *packs, proj, queries, flops=1 << 28,
+        where, *packs, proj, queries, scratch=[pltpu.VMEM((8, REGION), F32)], flops=1 << 28,
     )
     gradient, gs = cot_low, packs
+    def over_cols(parts):
+        moved = list(parts)
+        for distance in sorted(range(1, cols), key=lambda d: -min(d, cols - d)):
+            moved[distance] = routed(parts[distance], lambda p, r, c: (p, r, c + distance))
+        return moved
+
     state = ()
     for turn in range(pipes):
-        last = turn == pipes - 1
+        plane, last = pipes - 1 - turn, turn == pipes - 1
         if turn > 0:
             low, low_side, high_side = sends
             gradient = routed(low, lambda p, r, c: (p - 1, r, c))
             left, right = col_rims(low_side, high_side, 1)
-            left, d_query = lax.optimization_barrier((left, query_side(turn, gradient)))
-            gs = row_rims([gradient, left, right])
-        outs = [((TOK, 4 * D), BF16), ((OWN, D), BF16)]
+            left, d_query = lax.optimization_barrier(
+                (left, query_side(turn, gradient, *((state[0],) if last else ())))
+            )
+            gs = row_rims([gradient, left, right], plane, (d_query, mixed) if last else ())
+        fixed = (w_out, mixed_turned if turn else delta, proj, queries, k_probs)
+        scratch = [pltpu.VMEM((D, REGION), BF16)]
         if not last:
-            outs += [((TOK, D), F32), ((TOK, D), BF16), ((64, D), BF16), ((64, D), BF16)]
-        ins = () if last else (gradient if turn else cot, w_qkv, x)
-        outs = call(
-            functools.partial(key_kernel, turn=turn, last=last), outs,
-            where, *gs, w_out, mixed_turned if turn else delta, proj, queries, k_probs, d_query,
-            mixed, *ins, *state[: 2 if last else 3],
-            scratch=[pltpu.VMEM((D, REGION), BF16)], flops=1 << 30,
-        )
-        if last:
-            d_proj, g_low = outs
-            (d_in,) = call(
-                functools.partial(input_kernel, turn=turn), [((TOK, D), F32)],
-                where, d_proj, gradient, w_qkv, x, state[2], flops=1 << 28,
+            outs = call(
+                functools.partial(key_kernel, turn=turn, last=False),
+                [((TOK, 3 * D), BF16), ((OWN, D), BF16), ((TOK, D), F32), ((TOK, D), BF16),
+                 ((64, D), BF16), ((64, D), BF16)],
+                where, *gs, *fixed, d_query, gradient if turn else cot, w_qkv, x, *state,
+                scratch=scratch, flops=1 << 30,
             )
-        state, sends = outs[:3], outs[3:]
-    parts = call(
-        weight_kernel, [((8 * chips, 4 * D), BF16)] * cols,
-        where, n_turned, d_proj, routed(d_proj, mate), g_low,
-        scratch=[pltpu.VMEM((OWN, 3 * D), F32), pltpu.VMEM((D, D), F32)], flops=1 << 29,
-    )
-    parts = list(parts)
-    for distance in sorted(range(1, cols), key=lambda d: -min(d, cols - d)):
-        parts[distance] = routed(parts[distance], lambda p, r, c: (p, r, c + distance))
-    parts[-1], d_in = lax.optimization_barrier((parts[-1], d_in))
-    (part,) = call(col_total_kernel, [((8 * chips, 4 * D), BF16)], where, *parts)
+            state, sends = outs[:3], outs[3:]
+    d_proj, g_low, d_in = state
+    early = call(
+        functools.partial(early_kernel, turn=turn), [((8 * chips, 2 * D), BF16)] * cols,
+        where, n_turned, d_query, mixed, gs[0], gs[1], g_low,
+        scratch=[pltpu.VMEM((OWN, D), F32), pltpu.VMEM((D, D), F32), pltpu.VMEM((OWN, D), BF16)],
+        flops=1 << 28,
+    )
+    _, beyond = lax.optimization_barrier((early[0], gs[2]))
+    early, gs = over_cols(early), (*gs[:2], beyond)
+    (d_kv,) = call(
+        functools.partial(key_kernel, turn=turn, last=True), [((TOK, 2 * D), BF16)],
+        where, *gs, *fixed, d_proj, scratch=scratch, flops=1 << 30,
+    )
+    late = call(
+        late_kernel, [((8 * chips, 2 * D), BF16)] * cols, where, n_turned, d_kv, routed(d_kv, mate),
+        scratch=[pltpu.VMEM((OWN, 2 * D), F32)], flops=1 << 29,
+    )
+    late = list(late)
+    late[1], early[2] = lax.optimization_barrier((late[1], early[2]))
+    late = over_cols(late)
+    (d_in,) = call(
+        functools.partial(input_kernel, turn=turn), [((TOK, D), F32)],
+        where, d_query, d_kv, gradient, w_qkv, x, d_in, flops=1 << 28,
+    )
+    late[-1], d_in = lax.optimization_barrier((late[-1], d_in))
+    (part,) = call(col_total_kernel, [((8 * chips, 4 * D), BF16)], where, *early, *late)
     part = part.reshape(chips, 8, 4 * D)
     part = lax.all_to_all(part, "z", 0, 0, tiled=True)
     qkv_part, out_part = call(

time: 139 us -> 141 us (1.014)
  starting transfers between devices: 40.5 us -> 58.4 us
  waiting for transfers between devices: 51.7 us -> 35.8 us
  blocking collectives: 16.7 us -> 15.2 us
    ppermute x27 -> x30, starting transfers between devices: 40.5 us -> 58.4 us  [routed(): return lax.ppermute(block, AXES, pairs)]
    ppermute x27 -> x30, waiting for transfers between devices: 51.7 us -> 35.8 us  [routed(): return lax.ppermute(block, AXES, pairs)]
    all_to_all x1, blocking collectives: 16.7 us -> 15.2 us  [body(): part = lax.all_to_all(part, 'z', 0, 0, tiled=True)]
    unnamed x22 -> x24, local copies, waits for them, and re-layouts: 3.36 us -> 3.49 us
  transfers between devices with their start and end apart: 27 -> 30, of which waited for: 16 -> 15; matrix products, arithmetic and copies ran while one was open for 0% -> 0% of each run, Pallas kernels for 7% -> 8%
where the time goes in v1:
time: 141 us; the launch traced here: 140 us
  starting transfers between devices  58.4 us (41%)
  waiting for transfers between devices  35.8 us (25%)
  Pallas kernels  24.9 us (18%)
  blocking collectives  15.2 us (11%)
  local copies, waits for them, and re-layouts  4.54 us (3%)
    ppermute x30, starting transfers between devices, routed(): return lax.ppermute(block, AXES, pairs)  58.4 us
    ppermute x30, waiting for transfers between devices, routed(): return lax.ppermute(block, AXES, pairs)  35.8 us
    pallas_call x18, Pallas kernels, call(): pl.pallas_call(kernel, out_shape=[jax.ShapeDtypeStruct(s, t) for s, t in...  24.9 us
    all_to_all x1, blocking collectives, body(): part = lax.all_to_all(part, 'z', 0, 0, tiled=True)  15.2 us
    unnamed x24, local copies, waits for them, and re-layouts  3.49 us
  transfers between devices with their start and end apart: 30, of which 15 were waited for; matrix products, arithmetic and copies ran while one was open for 0% of the time, Pallas kernels for 8%

profile of v1, /device:TPU:6, one launch (start us, length us, event | category | flops | bytes accessed | tf_op | source)
XLA Modules:
  0.0 139.9 jit_solution(13354247705268139104)
XLA Ops:
  1.6 2.3 %collective-permute-start = (bf16[64,512]{1,0:T(8,128)(2,1)S(1)}, bf16[64,512]{1,0:T(8,128)(2,1)S(1)}, u32[]{:S(2)}, u32[]{:S(2)}) collective-permute-start(bf16[64,512]{1,0:T(8,128)(2,1)S(1)} %get-tuple-element.128), channel_id=1, source_target_pairs={{0,1},{1,2},{2,3},{3,0},{4,5},{5,6},{6,7},{7,4},{8,9},{9,10},{10,1... | collective-permute-start | bytes 196616 | tf_op jit(solution)/shard_map/ppermute | solution.py:410
  7.3 2.1 %collective-permute-done.1.right_ref = bf16[64,512]{1,0:T(8,128)(2,1)S(1)} collective-permute-done((bf16[64,512]{1,0:T(8,128)(2,1)S(1)}, bf16[64,512]{1,0:T(8,128)(2,1)S(1)}, u32[]{:S(2)}, u32[]{:S(2)}) %collective-permute-start.1) | collective-permute-done | bytes 65568 | tf_op jit(solution)/shard_map/ppermute | solution.py:410
  9.3 2.6 %collective-permute-start.3 = (bf16[256,512]{1,0:T(8,128)(2,1)S(1)}, bf16[256,512]{1,0:T(8,128)(2,1)S(1)}, u32[]{:S(2)}, u32[]{:S(2)}) collective-permute-start(bf16[256,512]{1,0:T(8,128)(2,1)S(1)} %constant_dynamic-update-slice_fusion.17), channel_id=1, source_target_pairs={{0,60},{1,61},{2,62},{3,63},{4,8},{5,9},{6,10},{7,11},{8,4},{9,5},... | collective-permute-start | bytes 786440 | tf_op jit(solution)/shard_map/ppermute | solution.py:410
  14.1 2.2 %collective-permute-done.3.x2 = bf16[256,512]{1,0:T(8,128)(2,1)S(1)} collective-permute-done((bf16[256,512]{1,0:T(8,128)(2,1)S(1)}, bf16[256,512]{1,0:T(8,128)(2,1)S(1)}, u32[]{:S(2)}, u32[]{:S(2)}) %collective-permute-start.3) | collective-permute-done | bytes 262176 | tf_op jit(solution)/shard_map/ppermute | solution.py:410
  16.4 4.0 %shard_map.69 = (bf16[768,1024]{1,0:T(8,128)(2,1)S(1)}, bf16[4,256,768]{2,1,0:T(8,128)(2,1)S(1)}, bf16[128,512]{1,0:T(8,128)(2,1)S(1)}, bf16[512,512]{1,0:T(8,12...) custom-call(s32[7]{0:T(128)S(1)} %stack.23.where_ref, ...), custom_call_target="tpu_custom_call" | custom-call | flops 2147483648 | bytes 4194304 | tf_op jit(solution)/shard_map/pallas_call | solution.py:388
  24.2 3.3 %collective-permute-done.5 = bf16[64,640]{1,0:T(8,128)(2,1)S(1)} collective-permute-done((bf16[64,640]{1,0:T(8,128)(2,1)S(1)}, bf16[64,640]{1,0:T(8,128)(2,1)S(1)}, u32[]{:S(2)}, u32[]{:S(2)}) %collective-permute-start.5) | collective-permute-done | bytes 81952 | tf_op jit(solution)/shard_map/ppermute | solution.py:410
  27.5 2.0 %collective-permute-start.7 = (bf16[256,640]{1,0:T(8,128)(2,1)S(1)}, bf16[256,640]{1,0:T(8,128)(2,1)S(1)}, u32[]{:S(2)}, u32[]{:S(2)}) collective-permute-start(bf16[256,640]{1,0:T(8,128)(2,1)S(1)} %constant_dynamic-update-slice_fusion.p0.g0), channel_id=1, source_target_pairs={{0,60},{1,61},{2,62},{3,63},{4,8},{5,9},{6,10},{7,11},{8,4},{9,5},... | collective-permute-start | bytes 983048 | tf_op jit(solution)/shard_map/ppermute | solution.py:410
  29.5 5.8 %collective-permute-done.7.p2.g2 = bf16[256,640]{1,0:T(8,128)(2,1)S(1)} collective-permute-done((bf16[256,640]{1,0:T(8,128)(2,1)S(1)}, bf16[256,640]{1,0:T(8,128)(2,1)S(1)}, u32[]{:S(2)}, u32[]{:S(2)}) %collective-permute-start.7) | collective-permute-done | bytes 327712 | tf_op jit(solution)/shard_map/ppermute | solution.py:410
  35.3 2.4 %shard_map.72 = (bf16[4,256,768]{2,1,0:T(8,128)(2,1)S(1)}, bf16[512,768]{1,0:T(8,128)(2,1)S(1)}, f32[8,768]{1,0:T(8,128)S(1)}) custom-call(s32[7]{0:T(128)S(1)} %stack.23.where_ref, bf16[256,640]{1,0:T(8,128)(2,1)S(1)} %constant_dynamic-update-slice_fusion.p0.g0, bf16[256,640]{1,0:T(8,128)(2,1)S(1)} %collective-permute-done.6.p1.g1, ...), custom_call_target="tpu_custom_call" | custom-call | flops 268435456 | bytes 4194304 | tf_op jit(solution)/shard_map/pallas_call | solution.py:388
  38.4 5.5 %collective-permute-start.8 = (bf16[128,512]{1,0:T(8,128)(2,1)S(1)}, bf16[128,512]{1,0:T(8,128)(2,1)S(1)}, u32[]{:S(2)}, u32[]{:S(2)}) collective-permute-start(bf16[128,512]{1,0:T(8,128)(2,1)S(1)} %get-tuple-element.85), channel_id=1, source_target_pairs={{0,192},{1,193},{2,194},{3,195},{4,196},{5,197},{6,198},{7,199},{8... | collective-permute-start | bytes 393224 | tf_op jit(solution)/shard_map/ppermute | solution.py:410
  45.1 2.0 %collective-permute-done.8.g_ref.rest_1_ = bf16[128,512]{1,0:T(8,128)(2,1)S(1)} collective-permute-done((bf16[128,512]{1,0:T(8,128)(2,1)S(1)}, bf16[128,512]{1,0:T(8,128)(2,1)S(1)}, u32[]{:S(2)}, u32[]{:S(2)}) %collective-permute-start.8) | collective-permute-done | bytes 131104 | tf_op jit(solution)/shard_map/ppermute | solution.py:410
  49.1 2.4 %collective-permute-done.10 = bf16[64,512]{1,0:T(8,128)(2,1)S(1)} collective-permute-done((bf16[64,512]{1,0:T(8,128)(2,1)S(1)}, bf16[64,512]{1,0:T(8,128)(2,1)S(1)}, u32[]{:S(2)}, u32[]{:S(2)}) %collective-permute-start.10) | collective-permute-done | bytes 65568 | tf_op jit(solution)/shard_map/ppermute | solution.py:410
  53.7 13.2 %collective-permute-start.14 = (bf16[64,512]{1,0:T(8,128)(2,1)S(1)}, bf16[64,512]{1,0:T(8,128)(2,1)S(1)}, u32[]{:S(2)}, u32[]{:S(2)}) collective-permute-start(bf16[64,512]{1,0:T(8,128)(2,1)S(1)} %get-tuple-element.95), channel_id=1, source_target_pairs={{0,193},{1,194},{2,195},{3,192},{4,197},{5,198},{6,199},{7,196},{8... | collective-permute-start | bytes 196616 | tf_op jit(solution)/shard_map/ppermute | solution.py:410
  68.9 4.4 %collective-permute-done.15 = bf16[64,512]{1,0:T(8,128)(2,1)S(1)} collective-permute-done((bf16[64,512]{1,0:T(8,128)(2,1)S(1)}, bf16[64,512]{1,0:T(8,128)(2,1)S(1)}, u32[]{:S(2)}, u32[]{:S(2)}) %collective-permute-start.15) | collective-permute-done | bytes 65568 | tf_op jit(solution)/shard_map/ppermute | solution.py:410
  77.2 12.6 %collective-permute-start.20 = (bf16[64,512]{1,0:T(8,128)(2,1)S(1)}, bf16[64,512]{1,0:T(8,128)(2,1)S(1)}, u32[]{:S(2)}, u32[]{:S(2)}) collective-permute-start(bf16[64,512]{1,0:T(8,128)(2,1)S(1)} %get-tuple-element.106), channel_id=1, source_target_pairs={{0,195},{1,192},{2,193},{3,194},{4,199},{5,196},{6,197},{7,198},{8... | collective-permute-start | bytes 196616 | tf_op jit(solution)/shard_map/ppermute | solution.py:410
  89.8 2.1 %collective-permute-done.18.g_ref = bf16[128,512]{1,0:T(8,128)(2,1)S(1)} collective-permute-done((bf16[128,512]{1,0:T(8,128)(2,1)S(1)}, bf16[128,512]{1,0:T(8,128)(2,1)S(1)}, u32[]{:S(2)}, u32[]{:S(2)}) %collective-permute-start.18) | collective-permute-done | bytes 131104 | tf_op jit(solution)/shard_map/ppermute | solution.py:410
  92.0 2.9 %shard_map.78.dq_ref = bf16[128,512]{1,0:T(8,128)(2,1)S(1)} custom-call(s32[7]{0:T(128)S(1)} %stack.23.where_ref, bf16[128,512]{1,0:T(8,128)(2,1)S(1)} %collective-permute-done.18.g_ref, bf16[512,512]{1,0:T(8,128)(2,1)S(1)} %bitcast.37, bf16[128,512]{1,0:T(8,128)(2,1)S(1)} %get-tuple-element.77.mixed_ref, bf16[768,1024]{1,0:T(8,128)(2,1)S(1)} %get-tuple-element.78.kv_ref, ...), custom_call_target="tpu_custom_call" | custom-call | flops 536870912 | bytes 4194304 | tf_op jit(solution)/shard_map/pallas_call | solution.py:388
  95.1 5.1 %collective-permute-start.22 = (bf16[256,512]{1,0:T(8,128)(2,1)S(1)}, bf16[256,512]{1,0:T(8,128)(2,1)S(1)}, u32[]{:S(2)}, u32[]{:S(2)}) collective-permute-start(bf16[256,512]{1,0:T(8,128)(2,1)S(1)} %get-tuple-element.130.g0), channel_id=1, source_target_pairs={{0,60},{1,61},{2,62},{3,63},{4,8},{5,9},{6,10},{7,11},{8,4},{9,5},... | collective-permute-start | bytes 786440 | tf_op jit(solution)/shard_map/ppermute | solution.py:410
  101.2 3.0 %collective-permute-done.22.g2 = bf16[256,512]{1,0:T(8,128)(2,1)S(1)} collective-permute-done((bf16[256,512]{1,0:T(8,128)(2,1)S(1)}, bf16[256,512]{1,0:T(8,128)(2,1)S(1)}, u32[]{:S(2)}, u32[]{:S(2)}) %collective-permute-start.22) | collective-permute-done | bytes 262176 | tf_op jit(solution)/shard_map/ppermute | solution.py:410
  104.2 2.7 %shard_map.80.d0.kv_ref = bf16[128,1024]{1,0:T(8,128)(2,1)S(1)} custom-call(s32[7]{0:T(128)S(1)} %stack.23.where_ref, bf16[256,512]{1,0:T(8,128)(2,1)S(1)} %get-tuple-element.130.g0, bf16[512,512]{1,0:T(8,128)(2,1)S(1)} %collective-permute-done.21.m.g1, bf16[256,512]{1,0:T(8,128)(2,1)S(1)} %collective-permute-done.22.g2, bf16[512,512]{1,0:T(8,128)(2,1)S(1)} %bitcast.38, ...), custom_call_target="tpu_custom_call" | custom-call | flops 1073741824 | bytes 4194304 | tf_op jit(solution)/shard_map/pallas_call | solution.py:388
  108.1 2.1 %collective-permute-start.25 = (bf16[64,1024]{1,0:T(8,128)(2,1)S(1)}, bf16[64,1024]{1,0:T(8,128)(2,1)S(1)}, u32[]{:S(2)}, u32[]{:S(2)}) collective-permute-start(bf16[64,1024]{1,0:T(8,128)(2,1)S(1)} %get-tuple-element.114), channel_id=1, source_target_pairs={{0,1},{1,2},{2,3},{3,0},{4,5},{5,6},{6,7},{7,4},{8,9},{9,10},{10,1... | collective-permute-start | bytes 393224 | tf_op jit(solution)/shard_map/ppermute | solution.py:410
  112.3 2.6 %collective-permute-done.26.refs_2_ = bf16[64,1024]{1,0:T(8,128)(2,1)S(1)} collective-permute-done((bf16[64,1024]{1,0:T(8,128)(2,1)S(1)}, bf16[64,1024]{1,0:T(8,128)(2,1)S(1)}, u32[]{:S(2)}, u32[]{:S(2)}) %collective-permute-start.26) | collective-permute-done | bytes 131104 | tf_op jit(solution)/shard_map/ppermute | solution.py:410
  117.4 2.0 %shard_map.82 = f32[128,512]{1,0:T(8,128)} custom-call(s32[7]{0:T(128)S(1)} %stack.23.where_ref, bf16[128,512]{1,0:T(8,128)(2,1)S(1)} %shard_map.78.dq_ref, bf16[128,1024]{1,0:T(8,128)(2,1)S(1)} %shard_map.80.d0.kv_ref, bf16[128,512]{1,0:T(8,128)(2,1)S(1)} %collective-permute-done.18.g_ref, bf16[512,1536]{1,0:T(8,128)(2,1)S(1)} %bitcast.29, ...), custom_call_target="tpu_custom_call" | custom-call | flops 268435456 | bytes 4194304 | tf_op jit(solution)/shard_map/pallas_call | solution.py:388
  123.6 15.2 %all_to_all.5.part_ref = bf16[8,8,2048]{2,1,0:T(8,128)(2,1)S(1)} all-to-all(bf16[8,8,2048]{2,1,0:T(8,128)(2,1)S(1)} %bitcast.45), channel_id=1, replica_groups=mesh['pipe'=4,'z'=8,'core'=2,'col'=4] {'z'}, dimensions={0} | all-to-all | bytes 524288 | tf_op jit(solution)/shard_map/all_to_all | solution.py:536
  (87 shorter events, 34.5 us)
Async XLA Ops:
  1.6 5.7 %collective-permute-start = (bf16[64,512]{1,0:T(8,128)(2,1)S(1)}, bf16[64,512]{1,0:T(8,128)(2,1)S(1)}, u32[]{:S(2)}, u32[]{:S(2)}) collective-permute-start(bf16[64,512]{1,0:T(8,128)(2,1)S(1)} %get-tuple-element.128), channel_id=1, source_target_pairs={{0,1},{1,2},{2,3},{3,0},{4,5},{5,6},{6,7},{7,4},{8,9},{9,10},{10,1... | collective-permute-start | bytes 196616 | tf_op jit(solution)/shard_map/ppermute | solution.py:410
  3.9 5.5 %collective-permute-start.1 = (bf16[64,512]{1,0:T(8,128)(2,1)S(1)}, bf16[64,512]{1,0:T(8,128)(2,1)S(1)}, u32[]{:S(2)}, u32[]{:S(2)}) collective-permute-start(bf16[64,512]{1,0:T(8,128)(2,1)S(1)} %get-tuple-element.127), channel_id=1, source_target_pairs={{0,3},{1,0},{2,1},{3,2},{4,7},{5,4},{6,5},{7,6},{8,11},{9,8},{10,9... | collective-permute-start | bytes 196616 | tf_op jit(solution)/shard_map/ppermute | solution.py:410
  9.3 7.0 %collective-permute-start.3 = (bf16[256,512]{1,0:T(8,128)(2,1)S(1)}, bf16[256,512]{1,0:T(8,128)(2,1)S(1)}, u32[]{:S(2)}, u32[]{:S(2)}) collective-permute-start(bf16[256,512]{1,0:T(8,128)(2,1)S(1)} %constant_dynamic-update-slice_fusion.17), channel_id=1, source_target_pairs={{0,60},{1,61},{2,62},{3,63},{4,8},{5,9},{6,10},{7,11},{8,4},{9,5},... | collective-permute-start | bytes 786440 | tf_op jit(solution)/shard_map/ppermute | solution.py:410
  20.4 7.1 %collective-permute-start.4 = (bf16[64,640]{1,0:T(8,128)(2,1)S(1)}, bf16[64,640]{1,0:T(8,128)(2,1)S(1)}, u32[]{:S(2)}, u32[]{:S(2)}) collective-permute-start(bf16[64,640]{1,0:T(8,128)(2,1)S(1)} %get-tuple-element.74), channel_id=1, source_target_pairs={{0,1},{1,2},{2,3},{3,0},{4,5},{5,6},{6,7},{7,4},{8,9},{9,10},{10,1... | collective-permute-start | bytes 245768 | tf_op jit(solution)/shard_map/ppermute | solution.py:410
  21.8 5.7 %collective-permute-start.5 = (bf16[64,640]{1,0:T(8,128)(2,1)S(1)}, bf16[64,640]{1,0:T(8,128)(2,1)S(1)}, u32[]{:S(2)}, u32[]{:S(2)}) collective-permute-start(bf16[64,640]{1,0:T(8,128)(2,1)S(1)} %get-tuple-element.75), channel_id=1, source_target_pairs={{0,3},{1,0},{2,1},{3,2},{4,7},{5,4},{6,5},{7,6},{8,11},{9,8},{10,9... | collective-permute-start | bytes 245768 | tf_op jit(solution)/shard_map/ppermute | solution.py:410
  27.5 7.8 %collective-permute-start.7 = (bf16[256,640]{1,0:T(8,128)(2,1)S(1)}, bf16[256,640]{1,0:T(8,128)(2,1)S(1)}, u32[]{:S(2)}, u32[]{:S(2)}) collective-permute-start(bf16[256,640]{1,0:T(8,128)(2,1)S(1)} %constant_dynamic-update-slice_fusion.p0.g0), channel_id=1, source_target_pairs={{0,60},{1,61},{2,62},{3,63},{4,8},{5,9},{6,10},{7,11},{8,4},{9,5},... | collective-permute-start | bytes 983048 | tf_op jit(solution)/shard_map/ppermute | solution.py:410
  29.5 5.8 %collective-permute-start.6 = (bf16[256,640]{1,0:T(8,128)(2,1)S(1)}, bf16[256,640]{1,0:T(8,128)(2,1)S(1)}, u32[]{:S(2)}, u32[]{:S(2)}) collective-permute-start(bf16[256,640]{1,0:T(8,128)(2,1)S(1)} %constant_dynamic-update-slice_fusion.p0.g0), channel_id=1, source_target_pairs={{0,4},{1,5},{2,6},{3,7},{4,0},{5,1},{6,2},{7,3},{8,12},{9,13},{10,... | collective-permute-start | bytes 983048 | tf_op jit(solution)/shard_map/ppermute | solution.py:410
  38.4 8.7 %collective-permute-start.8 = (bf16[128,512]{1,0:T(8,128)(2,1)S(1)}, bf16[128,512]{1,0:T(8,128)(2,1)S(1)}, u32[]{:S(2)}, u32[]{:S(2)}) collective-permute-start(bf16[128,512]{1,0:T(8,128)(2,1)S(1)} %get-tuple-element.85), channel_id=1, source_target_pairs={{0,192},{1,193},{2,194},{3,195},{4,196},{5,197},{6,198},{7,199},{8... | collective-permute-start | bytes 393224 | tf_op jit(solution)/shard_map/ppermute | solution.py:410
  43.9 5.2 %collective-permute-start.9 = (bf16[64,512]{1,0:T(8,128)(2,1)S(1)}, bf16[64,512]{1,0:T(8,128)(2,1)S(1)}, u32[]{:S(2)}, u32[]{:S(2)}) collective-permute-start(bf16[64,512]{1,0:T(8,128)(2,1)S(1)} %get-tuple-element.86), channel_id=1, source_target_pairs={{0,193},{1,194},{2,195},{3,192},{4,197},{5,198},{6,199},{7,196},{8... | collective-permute-start | bytes 196616 | tf_op jit(solution)/shard_map/ppermute | solution.py:410
  45.1 6.4 %collective-permute-start.10 = (bf16[64,512]{1,0:T(8,128)(2,1)S(1)}, bf16[64,512]{1,0:T(8,128)(2,1)S(1)}, u32[]{:S(2)}, u32[]{:S(2)}) collective-permute-start(bf16[64,512]{1,0:T(8,128)(2,1)S(1)} %get-tuple-element.88), channel_id=1, source_target_pairs={{0,195},{1,192},{2,193},{3,194},{4,199},{5,196},{6,197},{7,198},{8... | collective-permute-start | bytes 196616 | tf_op jit(solution)/shard_map/ppermute | solution.py:410
  53.4 13.8 %collective-permute-start.13 = (bf16[128,512]{1,0:T(8,128)(2,1)S(1)}, bf16[128,512]{1,0:T(8,128)(2,1)S(1)}, u32[]{:S(2)}, u32[]{:S(2)}) collective-permute-start(bf16[128,512]{1,0:T(8,128)(2,1)S(1)} %get-tuple-element.94), channel_id=1, source_target_pairs={{0,192},{1,193},{2,194},{3,195},{4,196},{5,197},{6,198},{7,199},{8... | collective-permute-start | bytes 393224 | tf_op jit(solution)/shard_map/ppermute | solution.py:410
  53.7 15.1 %collective-permute-start.14 = (bf16[64,512]{1,0:T(8,128)(2,1)S(1)}, bf16[64,512]{1,0:T(8,128)(2,1)S(1)}, u32[]{:S(2)}, u32[]{:S(2)}) collective-permute-start(bf16[64,512]{1,0:T(8,128)(2,1)S(1)} %get-tuple-element.95), channel_id=1, source_target_pairs={{0,193},{1,194},{2,195},{3,192},{4,197},{5,198},{6,199},{7,196},{8... | collective-permute-start | bytes 196616 | tf_op jit(solution)/shard_map/ppermute | solution.py:410
  66.9 6.4 %collective-permute-start.15 = (bf16[64,512]{1,0:T(8,128)(2,1)S(1)}, bf16[64,512]{1,0:T(8,128)(2,1)S(1)}, u32[]{:S(2)}, u32[]{:S(2)}) collective-permute-start(bf16[64,512]{1,0:T(8,128)(2,1)S(1)} %get-tuple-element.97), channel_id=1, source_target_pairs={{0,195},{1,192},{2,193},{3,194},{4,199},{5,196},{6,197},{7,198},{8... | collective-permute-start | bytes 196616 | tf_op jit(solution)/shard_map/ppermute | solution.py:410
  75.6 16.4 %collective-permute-start.18 = (bf16[128,512]{1,0:T(8,128)(2,1)S(1)}, bf16[128,512]{1,0:T(8,128)(2,1)S(1)}, u32[]{:S(2)}, u32[]{:S(2)}) collective-permute-start(bf16[128,512]{1,0:T(8,128)(2,1)S(1)} %get-tuple-element.102), channel_id=1, source_target_pairs={{0,192},{1,193},{2,194},{3,195},{4,196},{5,197},{6,198},{7,199},{8... | collective-permute-start | bytes 393224 | tf_op jit(solution)/shard_map/ppermute | solution.py:410
  76.9 17.9 %collective-permute-start.19 = (bf16[64,512]{1,0:T(8,128)(2,1)S(1)}, bf16[64,512]{1,0:T(8,128)(2,1)S(1)}, u32[]{:S(2)}, u32[]{:S(2)}) collective-permute-start(bf16[64,512]{1,0:T(8,128)(2,1)S(1)} %get-tuple-element.103), channel_id=1, source_target_pairs={{0,193},{1,194},{2,195},{3,192},{4,197},{5,198},{6,199},{7,196},{8... | collective-permute-start | bytes 196616 | tf_op jit(solution)/shard_map/ppermute | solution.py:410
  77.2 17.7 %collective-permute-start.20 = (bf16[64,512]{1,0:T(8,128)(2,1)S(1)}, bf16[64,512]{1,0:T(8,128)(2,1)S(1)}, u32[]{:S(2)}, u32[]{:S(2)}) collective-permute-start(bf16[64,512]{1,0:T(8,128)(2,1)S(1)} %get-tuple-element.106), channel_id=1, source_target_pairs={{0,195},{1,192},{2,193},{3,194},{4,199},{5,196},{6,197},{7,198},{8... | collective-permute-start | bytes 196616 | tf_op jit(solution)/shard_map/ppermute | solution.py:410
  95.0 5.2 %collective-permute-start.21 = (bf16[512,512]{1,0:T(8,128)(2,1)S(1)}, bf16[512,512]{1,0:T(8,128)(2,1)S(1)}, u32[]{:S(2)}, u32[]{:S(2)}) collective-permute-start(bf16[512,512]{1,0:T(8,128)(2,1)S(1)} %constant_dynamic-update-slice_fusion.12), channel_id=1, source_target_pairs={{0,4},{1,5},{2,6},{3,7},{4,0},{5,1},{6,2},{7,3},{8,12},{9,13},{10,... | collective-permute-start | bytes 1572872 | tf_op jit(solution)/shard_map/ppermute | solution.py:410
  95.1 9.1 %collective-permute-start.22 = (bf16[256,512]{1,0:T(8,128)(2,1)S(1)}, bf16[256,512]{1,0:T(8,128)(2,1)S(1)}, u32[]{:S(2)}, u32[]{:S(2)}) collective-permute-start(bf16[256,512]{1,0:T(8,128)(2,1)S(1)} %get-tuple-element.130.g0), channel_id=1, source_target_pairs={{0,60},{1,61},{2,62},{3,63},{4,8},{5,9},{6,10},{7,11},{8,4},{9,5},... | collective-permute-start | bytes 786440 | tf_op jit(solution)/shard_map/ppermute | solution.py:410
  107.0 7.9 %collective-permute-start.26 = (bf16[64,1024]{1,0:T(8,128)(2,1)S(1)}, bf16[64,1024]{1,0:T(8,128)(2,1)S(1)}, u32[]{:S(2)}, u32[]{:S(2)}) collective-permute-start(bf16[64,1024]{1,0:T(8,128)(2,1)S(1)} %get-tuple-element.116), channel_id=1, source_target_pairs={{0,2},{1,3},{2,0},{3,1},{4,6},{5,7},{6,4},{7,5},{8,10},{9,11},{10,... | collective-permute-start | bytes 393224 | tf_op jit(solution)/shard_map/ppermute | solution.py:410
  108.1 12.4 %collective-permute-start.25 = (bf16[64,1024]{1,0:T(8,128)(2,1)S(1)}, bf16[64,1024]{1,0:T(8,128)(2,1)S(1)}, u32[]{:S(2)}, u32[]{:S(2)}) collective-permute-start(bf16[64,1024]{1,0:T(8,128)(2,1)S(1)} %get-tuple-element.114), channel_id=1, source_target_pairs={{0,1},{1,2},{2,3},{3,0},{4,5},{5,6},{6,7},{7,4},{8,9},{9,10},{10,1... | collective-permute-start | bytes 393224 | tf_op jit(solution)/shard_map/ppermute | solution.py:410
  110.2 10.4 %collective-permute-start.27 = (bf16[64,1024]{1,0:T(8,128)(2,1)S(1)}, bf16[64,1024]{1,0:T(8,128)(2,1)S(1)}, u32[]{:S(2)}, u32[]{:S(2)}) collective-permute-start(bf16[64,1024]{1,0:T(8,128)(2,1)S(1)} %get-tuple-element.118), channel_id=1, source_target_pairs={{0,3},{1,0},{2,1},{3,2},{4,7},{5,4},{6,5},{7,6},{8,11},{9,8},{10,9... | collective-permute-start | bytes 393224 | tf_op jit(solution)/shard_map/ppermute | solution.py:410
  111.2 9.3 %collective-permute-start.24 = (bf16[64,1024]{1,0:T(8,128)(2,1)S(1)}, bf16[64,1024]{1,0:T(8,128)(2,1)S(1)}, u32[]{:S(2)}, u32[]{:S(2)}) collective-permute-start(bf16[64,1024]{1,0:T(8,128)(2,1)S(1)} %get-tuple-element.111), channel_id=1, source_target_pairs={{0,3},{1,0},{2,1},{3,2},{4,7},{5,4},{6,5},{7,6},{8,11},{9,8},{10,9... | collective-permute-start | bytes 393224 | tf_op jit(solution)/shard_map/ppermute | solution.py:410
  114.9 6.0 %collective-permute-start.28 = (bf16[64,1024]{1,0:T(8,128)(2,1)S(1)}, bf16[64,1024]{1,0:T(8,128)(2,1)S(1)}, u32[]{:S(2)}, u32[]{:S(2)}) collective-permute-start(bf16[64,1024]{1,0:T(8,128)(2,1)S(1)} %get-tuple-element.120), channel_id=1, source_target_pairs={{0,1},{1,2},{2,3},{3,0},{4,5},{5,6},{6,7},{7,4},{8,9},{9,10},{10,1... | collective-permute-start | bytes 393224 | tf_op jit(solution)/shard_map/ppermute | solution.py:410
  116.1 6.8 %collective-permute-start.29 = (bf16[64,1024]{1,0:T(8,128)(2,1)S(1)}, bf16[64,1024]{1,0:T(8,128)(2,1)S(1)}, u32[]{:S(2)}, u32[]{:S(2)}) collective-permute-start(bf16[64,1024]{1,0:T(8,128)(2,1)S(1)} %get-tuple-element.121), channel_id=1, source_target_pairs={{0,2},{1,3},{2,0},{3,1},{4,6},{5,7},{6,4},{7,5},{8,10},{9,11},{10,... | collective-permute-start | bytes 393224 | tf_op jit(solution)/shard_map/ppermute | solution.py:410
  (13 other events, 43.8 us)

commit v2 on v1

--- a/solution.py
+++ b/solution.py
@@ -270,17 +270,19 @@
     @pl.when(active)
     def _():
         for piece, g in enumerate((g0, g1, g2)):
-            d_mixed = nt(wo_ref[...], g[:OWN, :D]).astype(BF16)
+            d_mixed = nt(wo_ref[...], g[:, :D]).astype(BF16)
             dm_ref[:, piece * OWN : (piece + 1) * OWN] = d_mixed
-        for pair in range(PAIRS):
-            at = slice(128 * pair, 128 * pair + 128)
-            value = two_heads(proj_ref[:, 2 * D + 128 * pair : 2 * D + 128 * pair + 128])
+
+        def one_pair(pair, carry):
+            low = pl.multiple_of(128 * pair, 128)
+            at = pl.ds(low, 128)
+            value = two_heads(proj_ref[:, pl.ds(low + 2 * D, 128)])
             grad = dm_ref[at]
             if turn:
                 prod = grad.astype(F32) * delta_ref[at].astype(F32)
                 deltas = [jnp.sum(prod[r : r + 64], axis=0, keepdims=True) for r in (0, 64)]
             else:
-                deltas = [delta_ref[2 * pair + side : 2 * pair + side + 1] for side in range(2)]
+                deltas = [delta_ref[pl.ds(2 * pair + side, 1)] for side in range(2)]
             pressure = nn(value, grad)
             probs = prob_ref[pair]
             d_value = nt(grad, probs)
@@ -292,7 +294,10 @@
                 )
             d_key = nt(query_ref[at], jnp.concatenate(slopes, axis=0))
             kv_ref[:, at] = (turned_block(d_key) * 0.125).astype(BF16)
-            kv_ref[:, D + 128 * pair : D + 128 * pair + 128] = turned_block(d_value).astype(BF16)
+            kv_ref[:, pl.ds(low + D, 128)] = turned_block(d_value).astype(BF16)
+            return carry
+
+        lax.fori_loop(0, PAIRS, one_pair, 0, unroll=2)
         if not last:
             dq_ref, *ins_rest = ins
             outs[0][:, :D] = dq_ref[...]
@@ -336,21 +341,21 @@
             out_ref[:, at] = jnp.concatenate(rows, axis=0).astype(BF16)
 
 
-def early_kernel(where_ref, nt_ref, dq_ref, mixed_ref, g0, m, prev_ref, *refs, turn):
+def early_kernel(where_ref, nt_ref, dq_ref, mixed_ref, g0, g1, m, prev_ref, *refs, turn):
     outs, (left_ref, full_ref, g_ref) = refs[:-3], refs[-3:]
 
     @pl.when(where_ref[5] == turn)
     def _():
         g_ref[:TOK] = g0[:TOK]
-        g_ref[TOK:] = m[:TOK]
+        g_ref[TOK:] = g1[:TOK]
 
     @pl.when(where_ref[5] != turn)
     def _():
         g_ref[...] = prev_ref[...]
 
-    d_query = jnp.concatenate([dq_ref[...], m[OWN : OWN + TOK]], axis=0)
+    d_query = jnp.concatenate([dq_ref[...], m[:TOK]], axis=0)
     left_ref[...] = nn(nt_ref[...], d_query)
-    mixed = jnp.concatenate([mixed_ref[...], m[OWN + TOK :]], axis=0)
+    mixed = jnp.concatenate([mixed_ref[...], m[TOK:]], axis=0)
     full_ref[...] = tn(mixed, g_ref[...])
     split_rows(
         where_ref,
@@ -399,9 +404,9 @@
 def body(sizes, activations, qkv_weight, out_weight, cotangent):
     pipes, chips, cols = sizes
 
-    def routed(block, step, plane=None):
+    def routed(block, step):
         pairs = []
-        for p in range(pipes) if plane is None else (plane,):
+        for p in range(pipes):
             for r in range(2 * chips):
                 for c in range(cols):
                     p2, r2, c2 = step(p, r, c)
@@ -417,12 +422,10 @@
     def mate(p, r, c):
         return p, r ^ 1, c
 
-    def row_rims(pieces, plane=None, extra=()):
+    def row_rims(pieces):
         own = jnp.concatenate(pieces, axis=0)
-        beyond = routed(own, lambda p, r, c: (p, r - 1 + 2 * (r & 1), c), plane)
-        if extra:
-            return own, routed(jnp.concatenate([*pieces, *extra], axis=0), mate), beyond
-        return own, routed(own, mate, plane), beyond
+        beyond = routed(own, lambda p, r, c: (p, r - 1 + 2 * (r & 1), c))
+        return own, routed(own, mate), beyond
 
     pipe, z, core, col = (lax.axis_index(axis) for axis in AXES)
     x = activations.reshape(TOK, D)
@@ -486,7 +489,7 @@
 
     state = ()
     for turn in range(pipes):
-        plane, last = pipes - 1 - turn, turn == pipes - 1
+        last = turn == pipes - 1
         if turn > 0:
             low, low_side, high_side = sends
             gradient = routed(low, lambda p, r, c: (p - 1, r, c))
@@ -494,7 +497,7 @@
             left, d_query = lax.optimization_barrier(
                 (left, query_side(turn, gradient, *((state[0],) if last else ())))
             )
-            gs = row_rims([gradient, left, right], plane, (d_query, mixed) if last else ())
+            gs = row_rims([gradient, left, right])
         fixed = (w_out, mixed_turned if turn else delta, proj, queries, k_probs)
         scratch = [pltpu.VMEM((D, REGION), BF16)]
         if not last:
@@ -507,23 +510,27 @@
             )
             state, sends = outs[:3], outs[3:]
     d_proj, g_low, d_in = state
+    extra, beyond = lax.optimization_barrier(
+        (jnp.concatenate([d_query, mixed], axis=0), gs[2])
+    )
+    gs = (*gs[:2], beyond)
     early = call(
         functools.partial(early_kernel, turn=turn), [((8 * chips, 2 * D), BF16)] * cols,
-        where, n_turned, d_query, mixed, gs[0], gs[1], g_low,
+        where, n_turned, d_query, mixed, gs[0], gs[1], routed(extra, mate), g_low,
         scratch=[pltpu.VMEM((OWN, D), F32), pltpu.VMEM((D, D), F32), pltpu.VMEM((OWN, D), BF16)],
         flops=1 << 28,
     )
-    _, beyond = lax.optimization_barrier((early[0], gs[2]))
-    early, gs = over_cols(early), (*gs[:2], beyond)
     (d_kv,) = call(
         functools.partial(key_kernel, turn=turn, last=True), [((TOK, 2 * D), BF16)],
         where, *gs, *fixed, d_proj, scratch=scratch, flops=1 << 30,
     )
-    late = call(
-        late_kernel, [((8 * chips, 2 * D), BF16)] * cols, where, n_turned, d_kv, routed(d_kv, mate),
+    early = list(early)
+    early[0], d_kv_mate = lax.optimization_barrier((early[0], routed(d_kv, mate)))
+    early = over_cols(early)
+    late = list(call(
+        late_kernel, [((8 * chips, 2 * D), BF16)] * cols, where, n_turned, d_kv, d_kv_mate,
         scratch=[pltpu.VMEM((OWN, 2 * D), F32)], flops=1 << 29,
-    )
-    late = list(late)
+    ))
     late[1], early[2] = lax.optimization_barrier((late[1], early[2]))
     late = over_cols(late)
     (d_in,) = call(

time: 141 us -> 138 us (0.979)
  starting transfers between devices: 58.4 us -> 47.4 us
  waiting for transfers between devices: 35.8 us -> 43 us
    ppermute x30 -> x31, starting transfers between devices: 58.4 us -> 47.4 us  [routed(): return lax.ppermute(block, AXES, pairs)]
    ppermute x30 -> x31, waiting for transfers between devices: 35.8 us -> 43 us  [routed(): return lax.ppermute(block, AXES, pairs)]
    unnamed x24 -> x22, local copies, waits for them, and re-layouts: 3.49 us -> 3.45 us
  transfers between devices with their start and end apart: 30 -> 31, of which waited for: 15 -> 13; matrix products, arithmetic and copies ran while one was open for 0% -> 0% of each run, Pallas kernels for 8% -> 11%
where the time goes in v2:
time: 138 us; the launch traced here: 137 us
  starting transfers between devices  47.4 us (34%)
  waiting for transfers between devices  43 us (31%)
  Pallas kernels  25.2 us (18%)
  blocking collectives  15.7 us (11%)
  local copies, waits for them, and re-layouts  4.5 us (3%)
    ppermute x31, starting transfers between devices, routed(): return lax.ppermute(block, AXES, pairs)  47.4 us
    ppermute x31, waiting for transfers between devices, routed(): return lax.ppermute(block, AXES, pairs)  43 us
    pallas_call x18, Pallas kernels, call(): pl.pallas_call(kernel, out_shape=[jax.ShapeDtypeStruct(s, t) for s, t in...  25.2 us
    all_to_all x1, blocking collectives, body(): part = lax.all_to_all(part, 'z', 0, 0, tiled=True)  15.7 us
    unnamed x22, local copies, waits for them, and re-layouts  3.45 us
  transfers between devices with their start and end apart: 31, of which 13 were waited for; matrix products, arithmetic and copies ran while one was open for 0% of the time, Pallas kernels for 11%

profile of v2, /device:TPU:6, one launch (start us, length us, event | category | flops | bytes accessed | tf_op | source)
XLA Modules:
  0.0 136.7 jit_solution(11890429038088318328)
XLA Ops:
  1.6 2.3 %collective-permute-start = (bf16[64,512]{1,0:T(8,128)(2,1)S(1)}, bf16[64,512]{1,0:T(8,128)(2,1)S(1)}, u32[]{:S(2)}, u32[]{:S(2)}) collective-permute-start(bf16[64,512]{1,0:T(8,128)(2,1)S(1)} %get-tuple-element.132), channel_id=1, source_target_pairs={{0,1},{1,2},{2,3},{3,0},{4,5},{5,6},{6,7},{7,4},{8,9},{9,10},{10,1... | collective-permute-start | bytes 196616 | tf_op jit(solution)/shard_map/ppermute | solution.py:415
  7.3 2.1 %collective-permute-done.1.right_ref = bf16[64,512]{1,0:T(8,128)(2,1)S(1)} collective-permute-done((bf16[64,512]{1,0:T(8,128)(2,1)S(1)}, bf16[64,512]{1,0:T(8,128)(2,1)S(1)}, u32[]{:S(2)}, u32[]{:S(2)}) %collective-permute-start.1) | collective-permute-done | bytes 65568 | tf_op jit(solution)/shard_map/ppermute | solution.py:415
  9.3 2.6 %collective-permute-start.3 = (bf16[256,512]{1,0:T(8,128)(2,1)S(1)}, bf16[256,512]{1,0:T(8,128)(2,1)S(1)}, u32[]{:S(2)}, u32[]{:S(2)}) collective-permute-start(bf16[256,512]{1,0:T(8,128)(2,1)S(1)} %constant_dynamic-update-slice_fusion.12), channel_id=1, source_target_pairs={{0,60},{1,61},{2,62},{3,63},{4,8},{5,9},{6,10},{7,11},{8,4},{9,5},... | collective-permute-start | bytes 786440 | tf_op jit(solution)/shard_map/ppermute | solution.py:415
  14.1 2.2 %collective-permute-done.3.x2 = bf16[256,512]{1,0:T(8,128)(2,1)S(1)} collective-permute-done((bf16[256,512]{1,0:T(8,128)(2,1)S(1)}, bf16[256,512]{1,0:T(8,128)(2,1)S(1)}, u32[]{:S(2)}, u32[]{:S(2)}) %collective-permute-start.3) | collective-permute-done | bytes 262176 | tf_op jit(solution)/shard_map/ppermute | solution.py:415
  16.4 4.0 %shard_map.69 = (bf16[768,1024]{1,0:T(8,128)(2,1)S(1)}, bf16[4,256,768]{2,1,0:T(8,128)(2,1)S(1)}, bf16[128,512]{1,0:T(8,128)(2,1)S(1)}, bf16[512,512]{1,0:T(8,12...) custom-call(s32[7]{0:T(128)S(1)} %stack.23.where_ref, ...), custom_call_target="tpu_custom_call" | custom-call | flops 2147483648 | bytes 4194304 | tf_op jit(solution)/shard_map/pallas_call | solution.py:393
  24.2 3.3 %collective-permute-done.5 = bf16[64,640]{1,0:T(8,128)(2,1)S(1)} collective-permute-done((bf16[64,640]{1,0:T(8,128)(2,1)S(1)}, bf16[64,640]{1,0:T(8,128)(2,1)S(1)}, u32[]{:S(2)}, u32[]{:S(2)}) %collective-permute-start.5) | collective-permute-done | bytes 81952 | tf_op jit(solution)/shard_map/ppermute | solution.py:415
  29.5 5.8 %collective-permute-done.7.p2.g2 = bf16[256,640]{1,0:T(8,128)(2,1)S(1)} collective-permute-done((bf16[256,640]{1,0:T(8,128)(2,1)S(1)}, bf16[256,640]{1,0:T(8,128)(2,1)S(1)}, u32[]{:S(2)}, u32[]{:S(2)}) %collective-permute-start.7) | collective-permute-done | bytes 327712 | tf_op jit(solution)/shard_map/ppermute | solution.py:415
  35.3 2.4 %shard_map.72 = (bf16[4,256,768]{2,1,0:T(8,128)(2,1)S(1)}, bf16[512,768]{1,0:T(8,128)(2,1)S(1)}, f32[8,768]{1,0:T(8,128)S(1)}) custom-call(s32[7]{0:T(128)S(1)} %stack.23.where_ref, bf16[256,640]{1,0:T(8,128)(2,1)S(1)} %constant_dynamic-update-slice_fusion.p0.g0, bf16[256,640]{1,0:T(8,128)(2,1)S(1)} %collective-permute-done.6.p1.g1, ...), custom_call_target="tpu_custom_call" | custom-call | flops 268435456 | bytes 4194304 | tf_op jit(solution)/shard_map/pallas_call | solution.py:393
  38.4 5.9 %collective-permute-start.8 = (bf16[128,512]{1,0:T(8,128)(2,1)S(1)}, bf16[128,512]{1,0:T(8,128)(2,1)S(1)}, u32[]{:S(2)}, u32[]{:S(2)}) collective-permute-start(bf16[128,512]{1,0:T(8,128)(2,1)S(1)} %get-tuple-element.88), channel_id=1, source_target_pairs={{0,192},{1,193},{2,194},{3,195},{4,196},{5,197},{6,198},{7,199},{8... | collective-permute-start | bytes 393224 | tf_op jit(solution)/shard_map/ppermute | solution.py:415
  49.5 2.4 %collective-permute-done.10 = bf16[64,512]{1,0:T(8,128)(2,1)S(1)} collective-permute-done((bf16[64,512]{1,0:T(8,128)(2,1)S(1)}, bf16[64,512]{1,0:T(8,128)(2,1)S(1)}, u32[]{:S(2)}, u32[]{:S(2)}) %collective-permute-start.10) | collective-permute-done | bytes 65568 | tf_op jit(solution)/shard_map/ppermute | solution.py:415
  53.7 5.2 %collective-permute-done.12.g2 = bf16[256,512]{1,0:T(8,128)(2,1)S(1)} collective-permute-done((bf16[256,512]{1,0:T(8,128)(2,1)S(1)}, bf16[256,512]{1,0:T(8,128)(2,1)S(1)}, u32[]{:S(2)}, u32[]{:S(2)}) %collective-permute-start.12) | collective-permute-done | bytes 262176 | tf_op jit(solution)/shard_map/ppermute | solution.py:415
  61.0 5.0 %collective-permute-start.14 = (bf16[64,512]{1,0:T(8,128)(2,1)S(1)}, bf16[64,512]{1,0:T(8,128)(2,1)S(1)}, u32[]{:S(2)}, u32[]{:S(2)}) collective-permute-start(bf16[64,512]{1,0:T(8,128)(2,1)S(1)} %get-tuple-element.98), channel_id=1, source_target_pairs={{0,193},{1,194},{2,195},{3,192},{4,197},{5,198},{6,199},{7,196},{8... | collective-permute-start | bytes 196616 | tf_op jit(solution)/shard_map/ppermute | solution.py:415
  68.0 4.4 %collective-permute-done.15 = bf16[64,512]{1,0:T(8,128)(2,1)S(1)} collective-permute-done((bf16[64,512]{1,0:T(8,128)(2,1)S(1)}, bf16[64,512]{1,0:T(8,128)(2,1)S(1)}, u32[]{:S(2)}, u32[]{:S(2)}) %collective-permute-start.15) | collective-permute-done | bytes 65568 | tf_op jit(solution)/shard_map/ppermute | solution.py:415
  74.0 5.4 %collective-permute-done.17.g2 = bf16[256,512]{1,0:T(8,128)(2,1)S(1)} collective-permute-done((bf16[256,512]{1,0:T(8,128)(2,1)S(1)}, bf16[256,512]{1,0:T(8,128)(2,1)S(1)}, u32[]{:S(2)}, u32[]{:S(2)}) %collective-permute-start.17) | collective-permute-done | bytes 262176 | tf_op jit(solution)/shard_map/ppermute | solution.py:415
  81.9 4.5 %collective-permute-start.20 = (bf16[64,512]{1,0:T(8,128)(2,1)S(1)}, bf16[64,512]{1,0:T(8,128)(2,1)S(1)}, u32[]{:S(2)}, u32[]{:S(2)}) collective-permute-start(bf16[64,512]{1,0:T(8,128)(2,1)S(1)} %get-tuple-element.109), channel_id=1, source_target_pairs={{0,195},{1,192},{2,193},{3,194},{4,199},{5,196},{6,197},{7,198},{8... | collective-permute-start | bytes 196616 | tf_op jit(solution)/shard_map/ppermute | solution.py:415
  86.5 2.9 %shard_map.78.dq_ref = bf16[128,512]{1,0:T(8,128)(2,1)S(1)} custom-call(s32[7]{0:T(128)S(1)} %stack.23.where_ref, bf16[128,512]{1,0:T(8,128)(2,1)S(1)} %collective-permute-done.18.g_ref, bf16[512,512]{1,0:T(8,128)(2,1)S(1)} %bitcast.37, bf16[128,512]{1,0:T(8,128)(2,1)S(1)} %get-tuple-element.80.mixed_ref, bf16[768,1024]{1,0:T(8,128)(2,1)S(1)} %get-tuple-element.81.kv_ref, ...), custom_call_target="tpu_custom_call" | custom-call | flops 536870912 | bytes 4194304 | tf_op jit(solution)/shard_map/pallas_call | solution.py:393
  89.5 4.7 %collective-permute-start.22 = (bf16[256,512]{1,0:T(8,128)(2,1)S(1)}, bf16[256,512]{1,0:T(8,128)(2,1)S(1)}, u32[]{:S(2)}, u32[]{:S(2)}) collective-permute-start(bf16[256,512]{1,0:T(8,128)(2,1)S(1)} %constant_dynamic-update-slice_fusion.9.g0), channel_id=1, source_target_pairs={{0,60},{1,61},{2,62},{3,63},{4,8},{5,9},{6,10},{7,11},{8,4},{9,5},... | collective-permute-start | bytes 786440 | tf_op jit(solution)/shard_map/ppermute | solution.py:415
  94.2 4.0 %collective-permute-done.22.g2 = bf16[256,512]{1,0:T(8,128)(2,1)S(1)} collective-permute-done((bf16[256,512]{1,0:T(8,128)(2,1)S(1)}, bf16[256,512]{1,0:T(8,128)(2,1)S(1)}, u32[]{:S(2)}, u32[]{:S(2)}) %collective-permute-start.22) | collective-permute-done | bytes 262176 | tf_op jit(solution)/shard_map/ppermute | solution.py:415
  98.3 3.0 %shard_map.79.d0.kv_ref = bf16[128,1024]{1,0:T(8,128)(2,1)S(1)} custom-call(s32[7]{0:T(128)S(1)} %stack.23.where_ref, bf16[256,512]{1,0:T(8,128)(2,1)S(1)} %constant_dynamic-update-slice_fusion.9.g0, bf16[256,512]{1,0:T(8,128)(2,1)S(1)} %collective-permute-done.21.g1, bf16[256,512]{1,0:T(8,128)(2,1)S(1)} %collective-permute-done.22.g2, ...), custom_call_target="tpu_custom_call" | custom-call | flops 1073741824 | bytes 4194304 | tf_op jit(solution)/shard_map/pallas_call | solution.py:393
  102.9 2.1 %collective-permute-start.27 = (bf16[64,1024]{1,0:T(8,128)(2,1)S(1)}, bf16[64,1024]{1,0:T(8,128)(2,1)S(1)}, u32[]{:S(2)}, u32[]{:S(2)}) collective-permute-start(bf16[64,1024]{1,0:T(8,128)(2,1)S(1)} %get-tuple-element.122), channel_id=1, source_target_pairs={{0,2},{1,3},{2,0},{3,1},{4,6},{5,7},{6,4},{7,5},{8,10},{9,11},{10,... | collective-permute-start | bytes 393224 | tf_op jit(solution)/shard_map/ppermute | solution.py:415
  105.0 2.4 %collective-permute-start.26 = (bf16[64,1024]{1,0:T(8,128)(2,1)S(1)}, bf16[64,1024]{1,0:T(8,128)(2,1)S(1)}, u32[]{:S(2)}, u32[]{:S(2)}) collective-permute-start(bf16[64,1024]{1,0:T(8,128)(2,1)S(1)} %get-tuple-element.120), channel_id=1, source_target_pairs={{0,1},{1,2},{2,3},{3,0},{4,5},{5,6},{6,7},{7,4},{8,9},{9,10},{10,1... | collective-permute-start | bytes 393224 | tf_op jit(solution)/shard_map/ppermute | solution.py:415
  109.6 3.6 %collective-permute-start.30 = (bf16[64,1024]{1,0:T(8,128)(2,1)S(1)}, bf16[64,1024]{1,0:T(8,128)(2,1)S(1)}, u32[]{:S(2)}, u32[]{:S(2)}) collective-permute-start(bf16[64,1024]{1,0:T(8,128)(2,1)S(1)} %get-tuple-element.127), channel_id=1, source_target_pairs={{0,2},{1,3},{2,0},{3,1},{4,6},{5,7},{6,4},{7,5},{8,10},{9,11},{10,... | collective-permute-start | bytes 393224 | tf_op jit(solution)/shard_map/ppermute | solution.py:415
  115.5 3.6 %collective-permute-done.25.refs_7_ = bf16[64,1024]{1,0:T(8,128)(2,1)S(1)} collective-permute-done((bf16[64,1024]{1,0:T(8,128)(2,1)S(1)}, bf16[64,1024]{1,0:T(8,128)(2,1)S(1)}, u32[]{:S(2)}, u32[]{:S(2)}) %collective-permute-start.25) | collective-permute-done | bytes 131104 | tf_op jit(solution)/shard_map/ppermute | solution.py:415
  119.8 15.7 %all_to_all.5.part_ref = bf16[8,8,2048]{2,1,0:T(8,128)(2,1)S(1)} all-to-all(bf16[8,8,2048]{2,1,0:T(8,128)(2,1)S(1)} %bitcast.45), channel_id=1, replica_groups=mesh['pipe'=4,'z'=8,'core'=2,'col'=4] {'z'}, dimensions={0} | all-to-all | bytes 524288 | tf_op jit(solution)/shard_map/all_to_all | solution.py:543
  (88 shorter events, 36.3 us)
Async XLA Ops:
  1.6 5.7 %collective-permute-start = (bf16[64,512]{1,0:T(8,128)(2,1)S(1)}, bf16[64,512]{1,0:T(8,128)(2,1)S(1)}, u32[]{:S(2)}, u32[]{:S(2)}) collective-permute-start(bf16[64,512]{1,0:T(8,128)(2,1)S(1)} %get-tuple-element.132), channel_id=1, source_target_pairs={{0,1},{1,2},{2,3},{3,0},{4,5},{5,6},{6,7},{7,4},{8,9},{9,10},{10,1... | collective-permute-start | bytes 196616 | tf_op jit(solution)/shard_map/ppermute | solution.py:415
  9.3 7.0 %collective-permute-start.3 = (bf16[256,512]{1,0:T(8,128)(2,1)S(1)}, bf16[256,512]{1,0:T(8,128)(2,1)S(1)}, u32[]{:S(2)}, u32[]{:S(2)}) collective-permute-start(bf16[256,512]{1,0:T(8,128)(2,1)S(1)} %constant_dynamic-update-slice_fusion.12), channel_id=1, source_target_pairs={{0,60},{1,61},{2,62},{3,63},{4,8},{5,9},{6,10},{7,11},{8,4},{9,5},... | collective-permute-start | bytes 786440 | tf_op jit(solution)/shard_map/ppermute | solution.py:415
  20.4 7.1 %collective-permute-start.4 = (bf16[64,640]{1,0:T(8,128)(2,1)S(1)}, bf16[64,640]{1,0:T(8,128)(2,1)S(1)}, u32[]{:S(2)}, u32[]{:S(2)}) collective-permute-start(bf16[64,640]{1,0:T(8,128)(2,1)S(1)} %get-tuple-element.77), channel_id=1, source_target_pairs={{0,1},{1,2},{2,3},{3,0},{4,5},{5,6},{6,7},{7,4},{8,9},{9,10},{10,1... | collective-permute-start | bytes 245768 | tf_op jit(solution)/shard_map/ppermute | solution.py:415
  21.8 5.7 %collective-permute-start.5 = (bf16[64,640]{1,0:T(8,128)(2,1)S(1)}, bf16[64,640]{1,0:T(8,128)(2,1)S(1)}, u32[]{:S(2)}, u32[]{:S(2)}) collective-permute-start(bf16[64,640]{1,0:T(8,128)(2,1)S(1)} %get-tuple-element.78), channel_id=1, source_target_pairs={{0,3},{1,0},{2,1},{3,2},{4,7},{5,4},{6,5},{7,6},{8,11},{9,8},{10,9... | collective-permute-start | bytes 245768 | tf_op jit(solution)/shard_map/ppermute | solution.py:415
  27.5 7.8 %collective-permute-start.7 = (bf16[256,640]{1,0:T(8,128)(2,1)S(1)}, bf16[256,640]{1,0:T(8,128)(2,1)S(1)}, u32[]{:S(2)}, u32[]{:S(2)}) collective-permute-start(bf16[256,640]{1,0:T(8,128)(2,1)S(1)} %constant_dynamic-update-slice_fusion.p0.g0), channel_id=1, source_target_pairs={{0,60},{1,61},{2,62},{3,63},{4,8},{5,9},{6,10},{7,11},{8,4},{9,5},... | collective-permute-start | bytes 983048 | tf_op jit(solution)/shard_map/ppermute | solution.py:415
  29.5 5.8 %collective-permute-start.6 = (bf16[256,640]{1,0:T(8,128)(2,1)S(1)}, bf16[256,640]{1,0:T(8,128)(2,1)S(1)}, u32[]{:S(2)}, u32[]{:S(2)}) collective-permute-start(bf16[256,640]{1,0:T(8,128)(2,1)S(1)} %constant_dynamic-update-slice_fusion.p0.g0), channel_id=1, source_target_pairs={{0,4},{1,5},{2,6},{3,7},{4,0},{5,1},{6,2},{7,3},{8,12},{9,13},{10,... | collective-permute-start | bytes 983048 | tf_op jit(solution)/shard_map/ppermute | solution.py:415
  38.4 9.1 %collective-permute-start.8 = (bf16[128,512]{1,0:T(8,128)(2,1)S(1)}, bf16[128,512]{1,0:T(8,128)(2,1)S(1)}, u32[]{:S(2)}, u32[]{:S(2)}) collective-permute-start(bf16[128,512]{1,0:T(8,128)(2,1)S(1)} %get-tuple-element.88), channel_id=1, source_target_pairs={{0,192},{1,193},{2,194},{3,195},{4,196},{5,197},{6,198},{7,199},{8... | collective-permute-start | bytes 393224 | tf_op jit(solution)/shard_map/ppermute | solution.py:415
  45.5 6.4 %collective-permute-start.10 = (bf16[64,512]{1,0:T(8,128)(2,1)S(1)}, bf16[64,512]{1,0:T(8,128)(2,1)S(1)}, u32[]{:S(2)}, u32[]{:S(2)}) collective-permute-start(bf16[64,512]{1,0:T(8,128)(2,1)S(1)} %get-tuple-element.91), channel_id=1, source_target_pairs={{0,195},{1,192},{2,193},{3,194},{4,199},{5,196},{6,197},{7,198},{8... | collective-permute-start | bytes 196616 | tf_op jit(solution)/shard_map/ppermute | solution.py:415
  51.9 7.0 %collective-permute-start.12 = (bf16[256,512]{1,0:T(8,128)(2,1)S(1)}, bf16[256,512]{1,0:T(8,128)(2,1)S(1)}, u32[]{:S(2)}, u32[]{:S(2)}) collective-permute-start(bf16[256,512]{1,0:T(8,128)(2,1)S(1)} %constant_dynamic-update-slice_fusion.3.g0), channel_id=1, source_target_pairs={{0,60},{1,61},{2,62},{3,63},{4,8},{5,9},{6,10},{7,11},{8,4},{9,5},... | collective-permute-start | bytes 786440 | tf_op jit(solution)/shard_map/ppermute | solution.py:415
  59.5 6.7 %collective-permute-start.13 = (bf16[128,512]{1,0:T(8,128)(2,1)S(1)}, bf16[128,512]{1,0:T(8,128)(2,1)S(1)}, u32[]{:S(2)}, u32[]{:S(2)}) collective-permute-start(bf16[128,512]{1,0:T(8,128)(2,1)S(1)} %get-tuple-element.97), channel_id=1, source_target_pairs={{0,192},{1,193},{2,194},{3,195},{4,196},{5,197},{6,198},{7,199},{8... | collective-permute-start | bytes 393224 | tf_op jit(solution)/shard_map/ppermute | solution.py:415
  61.0 6.9 %collective-permute-start.14 = (bf16[64,512]{1,0:T(8,128)(2,1)S(1)}, bf16[64,512]{1,0:T(8,128)(2,1)S(1)}, u32[]{:S(2)}, u32[]{:S(2)}) collective-permute-start(bf16[64,512]{1,0:T(8,128)(2,1)S(1)} %get-tuple-element.98), channel_id=1, source_target_pairs={{0,193},{1,194},{2,195},{3,192},{4,197},{5,198},{6,199},{7,196},{8... | collective-permute-start | bytes 196616 | tf_op jit(solution)/shard_map/ppermute | solution.py:415
  66.0 6.4 %collective-permute-start.15 = (bf16[64,512]{1,0:T(8,128)(2,1)S(1)}, bf16[64,512]{1,0:T(8,128)(2,1)S(1)}, u32[]{:S(2)}, u32[]{:S(2)}) collective-permute-start(bf16[64,512]{1,0:T(8,128)(2,1)S(1)} %get-tuple-element.100), channel_id=1, source_target_pairs={{0,195},{1,192},{2,193},{3,194},{4,199},{5,196},{6,197},{7,198},{8... | collective-permute-start | bytes 196616 | tf_op jit(solution)/shard_map/ppermute | solution.py:415
  72.4 7.0 %collective-permute-start.17 = (bf16[256,512]{1,0:T(8,128)(2,1)S(1)}, bf16[256,512]{1,0:T(8,128)(2,1)S(1)}, u32[]{:S(2)}, u32[]{:S(2)}) collective-permute-start(bf16[256,512]{1,0:T(8,128)(2,1)S(1)} %constant_dynamic-update-slice_fusion.6.g0), channel_id=1, source_target_pairs={{0,60},{1,61},{2,62},{3,63},{4,8},{5,9},{6,10},{7,11},{8,4},{9,5},... | collective-permute-start | bytes 786440 | tf_op jit(solution)/shard_map/ppermute | solution.py:415
  80.3 6.2 %collective-permute-start.18 = (bf16[128,512]{1,0:T(8,128)(2,1)S(1)}, bf16[128,512]{1,0:T(8,128)(2,1)S(1)}, u32[]{:S(2)}, u32[]{:S(2)}) collective-permute-start(bf16[128,512]{1,0:T(8,128)(2,1)S(1)} %get-tuple-element.105), channel_id=1, source_target_pairs={{0,192},{1,193},{2,194},{3,195},{4,196},{5,197},{6,198},{7,199},{8... | collective-permute-start | bytes 393224 | tf_op jit(solution)/shard_map/ppermute | solution.py:415
  81.6 7.7 %collective-permute-start.19 = (bf16[64,512]{1,0:T(8,128)(2,1)S(1)}, bf16[64,512]{1,0:T(8,128)(2,1)S(1)}, u32[]{:S(2)}, u32[]{:S(2)}) collective-permute-start(bf16[64,512]{1,0:T(8,128)(2,1)S(1)} %get-tuple-element.106), channel_id=1, source_target_pairs={{0,193},{1,194},{2,195},{3,192},{4,197},{5,198},{6,199},{7,196},{8... | collective-permute-start | bytes 196616 | tf_op jit(solution)/shard_map/ppermute | solution.py:415
  81.9 7.5 %collective-permute-start.20 = (bf16[64,512]{1,0:T(8,128)(2,1)S(1)}, bf16[64,512]{1,0:T(8,128)(2,1)S(1)}, u32[]{:S(2)}, u32[]{:S(2)}) collective-permute-start(bf16[64,512]{1,0:T(8,128)(2,1)S(1)} %get-tuple-element.109), channel_id=1, source_target_pairs={{0,195},{1,192},{2,193},{3,194},{4,199},{5,196},{6,197},{7,198},{8... | collective-permute-start | bytes 196616 | tf_op jit(solution)/shard_map/ppermute | solution.py:415
  89.5 8.8 %collective-permute-start.22 = (bf16[256,512]{1,0:T(8,128)(2,1)S(1)}, bf16[256,512]{1,0:T(8,128)(2,1)S(1)}, u32[]{:S(2)}, u32[]{:S(2)}) collective-permute-start(bf16[256,512]{1,0:T(8,128)(2,1)S(1)} %constant_dynamic-update-slice_fusion.9.g0), channel_id=1, source_target_pairs={{0,60},{1,61},{2,62},{3,63},{4,8},{5,9},{6,10},{7,11},{8,4},{9,5},... | collective-permute-start | bytes 786440 | tf_op jit(solution)/shard_map/ppermute | solution.py:415
  101.3 6.2 %collective-permute-start.24 = (bf16[128,1024]{1,0:T(8,128)(2,1)S(1)}, bf16[128,1024]{1,0:T(8,128)(2,1)S(1)}, u32[]{:S(2)}, u32[]{:S(2)}) collective-permute-start(bf16[128,1024]{1,0:T(8,128)(2,1)S(1)} %shard_map.79.d0.kv_ref), channel_id=1, source_target_pairs={{0,4},{1,5},{2,6},{3,7},{4,0},{5,1},{6,2},{7,3},{8,12},{9,13},{10,... | collective-permute-start | bytes 786440 | tf_op jit(solution)/shard_map/ppermute | solution.py:415
  102.9 10.3 %collective-permute-start.27 = (bf16[64,1024]{1,0:T(8,128)(2,1)S(1)}, bf16[64,1024]{1,0:T(8,128)(2,1)S(1)}, u32[]{:S(2)}, u32[]{:S(2)}) collective-permute-start(bf16[64,1024]{1,0:T(8,128)(2,1)S(1)} %get-tuple-element.122), channel_id=1, source_target_pairs={{0,2},{1,3},{2,0},{3,1},{4,6},{5,7},{6,4},{7,5},{8,10},{9,11},{10,... | collective-permute-start | bytes 393224 | tf_op jit(solution)/shard_map/ppermute | solution.py:415
  105.0 14.1 %collective-permute-start.26 = (bf16[64,1024]{1,0:T(8,128)(2,1)S(1)}, bf16[64,1024]{1,0:T(8,128)(2,1)S(1)}, u32[]{:S(2)}, u32[]{:S(2)}) collective-permute-start(bf16[64,1024]{1,0:T(8,128)(2,1)S(1)} %get-tuple-element.120), channel_id=1, source_target_pairs={{0,1},{1,2},{2,3},{3,0},{4,5},{5,6},{6,7},{7,4},{8,9},{9,10},{10,1... | collective-permute-start | bytes 393224 | tf_op jit(solution)/shard_map/ppermute | solution.py:415
  107.4 11.7 %collective-permute-start.28 = (bf16[64,1024]{1,0:T(8,128)(2,1)S(1)}, bf16[64,1024]{1,0:T(8,128)(2,1)S(1)}, u32[]{:S(2)}, u32[]{:S(2)}) collective-permute-start(bf16[64,1024]{1,0:T(8,128)(2,1)S(1)} %get-tuple-element.124), channel_id=1, source_target_pairs={{0,3},{1,0},{2,1},{3,2},{4,7},{5,4},{6,5},{7,6},{8,11},{9,8},{10,9... | collective-permute-start | bytes 393224 | tf_op jit(solution)/shard_map/ppermute | solution.py:415
  108.4 10.7 %collective-permute-start.25 = (bf16[64,1024]{1,0:T(8,128)(2,1)S(1)}, bf16[64,1024]{1,0:T(8,128)(2,1)S(1)}, u32[]{:S(2)}, u32[]{:S(2)}) collective-permute-start(bf16[64,1024]{1,0:T(8,128)(2,1)S(1)} %get-tuple-element.116), channel_id=1, source_target_pairs={{0,3},{1,0},{2,1},{3,2},{4,7},{5,4},{6,5},{7,6},{8,11},{9,8},{10,9... | collective-permute-start | bytes 393224 | tf_op jit(solution)/shard_map/ppermute | solution.py:415
  109.6 9.5 %collective-permute-start.30 = (bf16[64,1024]{1,0:T(8,128)(2,1)S(1)}, bf16[64,1024]{1,0:T(8,128)(2,1)S(1)}, u32[]{:S(2)}, u32[]{:S(2)}) collective-permute-start(bf16[64,1024]{1,0:T(8,128)(2,1)S(1)} %get-tuple-element.127), channel_id=1, source_target_pairs={{0,2},{1,3},{2,0},{3,1},{4,6},{5,7},{6,4},{7,5},{8,10},{9,11},{10,... | collective-permute-start | bytes 393224 | tf_op jit(solution)/shard_map/ppermute | solution.py:415
  113.2 6.0 %collective-permute-start.29 = (bf16[64,1024]{1,0:T(8,128)(2,1)S(1)}, bf16[64,1024]{1,0:T(8,128)(2,1)S(1)}, u32[]{:S(2)}, u32[]{:S(2)}) collective-permute-start(bf16[64,1024]{1,0:T(8,128)(2,1)S(1)} %get-tuple-element.126), channel_id=1, source_target_pairs={{0,1},{1,2},{2,3},{3,0},{4,5},{5,6},{6,7},{7,4},{8,9},{9,10},{10,1... | collective-permute-start | bytes 393224 | tf_op jit(solution)/shard_map/ppermute | solution.py:415
  (14 other events, 66.4 us)

commit v3 on v2

--- a/solution.py
+++ b/solution.py
@@ -297,7 +297,7 @@
             kv_ref[:, pl.ds(low + D, 128)] = turned_block(d_value).astype(BF16)
             return carry
 
-        lax.fori_loop(0, PAIRS, one_pair, 0, unroll=2)
+        lax.fori_loop(0, PAIRS, one_pair, 0, unroll=4 if last else 2)
         if not last:
             dq_ref, *ins_rest = ins
             outs[0][:, :D] = dq_ref[...]
@@ -510,10 +510,7 @@
             )
             state, sends = outs[:3], outs[3:]
     d_proj, g_low, d_in = state
-    extra, beyond = lax.optimization_barrier(
-        (jnp.concatenate([d_query, mixed], axis=0), gs[2])
-    )
-    gs = (*gs[:2], beyond)
+    extra = jnp.concatenate([d_query, mixed], axis=0)
     early = call(
         functools.partial(early_kernel, turn=turn), [((8 * chips, 2 * D), BF16)] * cols,
         where, n_turned, d_query, mixed, gs[0], gs[1], routed(extra, mate), g_low,

time: 138 us -> 139 us (level)
  no operation moved by 1% of the time
where the time goes in v3:
time: 139 us; the launch traced here: 137 us
  starting transfers between devices  47.4 us (34%)
  waiting for transfers between devices  42.9 us (31%)
  Pallas kernels  24.9 us (18%)
  blocking collectives  16.2 us (12%)
  local copies, waits for them, and re-layouts  4.5 us (3%)
    ppermute x31, starting transfers between devices, routed(): return lax.ppermute(block, AXES, pairs)  47.4 us
    ppermute x31, waiting for transfers between devices, routed(): return lax.ppermute(block, AXES, pairs)  42.9 us
    pallas_call x18, Pallas kernels, call(): pl.pallas_call(kernel, out_shape=[jax.ShapeDtypeStruct(s, t) for s, t in...  24.9 us
    all_to_all x1, blocking collectives, body(): part = lax.all_to_all(part, 'z', 0, 0, tiled=True)  16.2 us
    unnamed x22, local copies, waits for them, and re-layouts  3.45 us
  transfers between devices with their start and end apart: 31, of which 13 were waited for; matrix products, arithmetic and copies ran while one was open for 0% of the time, Pallas kernels for 11%

profile of v3, /device:TPU:6, one launch (start us, length us, event | category | flops | bytes accessed | tf_op | source)
XLA Modules:
  0.0 136.9 jit_solution(13659887163153234295)
XLA Ops:
  1.6 2.3 %collective-permute-start = (bf16[64,512]{1,0:T(8,128)(2,1)S(1)}, bf16[64,512]{1,0:T(8,128)(2,1)S(1)}, u32[]{:S(2)}, u32[]{:S(2)}) collective-permute-start(bf16[64,512]{1,0:T(8,128)(2,1)S(1)} %get-tuple-element.128), channel_id=1, source_target_pairs={{0,1},{1,2},{2,3},{3,0},{4,5},{5,6},{6,7},{7,4},{8,9},{9,10},{10,1... | collective-permute-start | bytes 196616 | tf_op jit(solution)/shard_map/ppermute | solution.py:415
  7.3 2.1 %collective-permute-done.1.right_ref = bf16[64,512]{1,0:T(8,128)(2,1)S(1)} collective-permute-done((bf16[64,512]{1,0:T(8,128)(2,1)S(1)}, bf16[64,512]{1,0:T(8,128)(2,1)S(1)}, u32[]{:S(2)}, u32[]{:S(2)}) %collective-permute-start.1) | collective-permute-done | bytes 65568 | tf_op jit(solution)/shard_map/ppermute | solution.py:415
  9.3 2.6 %collective-permute-start.3 = (bf16[256,512]{1,0:T(8,128)(2,1)S(1)}, bf16[256,512]{1,0:T(8,128)(2,1)S(1)}, u32[]{:S(2)}, u32[]{:S(2)}) collective-permute-start(bf16[256,512]{1,0:T(8,128)(2,1)S(1)} %constant_dynamic-update-slice_fusion.12), channel_id=1, source_target_pairs={{0,60},{1,61},{2,62},{3,63},{4,8},{5,9},{6,10},{7,11},{8,4},{9,5},... | collective-permute-start | bytes 786440 | tf_op jit(solution)/shard_map/ppermute | solution.py:415
  14.1 2.2 %collective-permute-done.3.x2 = bf16[256,512]{1,0:T(8,128)(2,1)S(1)} collective-permute-done((bf16[256,512]{1,0:T(8,128)(2,1)S(1)}, bf16[256,512]{1,0:T(8,128)(2,1)S(1)}, u32[]{:S(2)}, u32[]{:S(2)}) %collective-permute-start.3) | collective-permute-done | bytes 262176 | tf_op jit(solution)/shard_map/ppermute | solution.py:415
  16.4 4.0 %shard_map.69 = (bf16[768,1024]{1,0:T(8,128)(2,1)S(1)}, bf16[4,256,768]{2,1,0:T(8,128)(2,1)S(1)}, bf16[128,512]{1,0:T(8,128)(2,1)S(1)}, bf16[512,512]{1,0:T(8,12...) custom-call(s32[7]{0:T(128)S(1)} %stack.23.where_ref, ...), custom_call_target="tpu_custom_call" | custom-call | flops 2147483648 | bytes 4194304 | tf_op jit(solution)/shard_map/pallas_call | solution.py:393
  24.2 3.3 %collective-permute-done.5 = bf16[64,640]{1,0:T(8,128)(2,1)S(1)} collective-permute-done((bf16[64,640]{1,0:T(8,128)(2,1)S(1)}, bf16[64,640]{1,0:T(8,128)(2,1)S(1)}, u32[]{:S(2)}, u32[]{:S(2)}) %collective-permute-start.5) | collective-permute-done | bytes 81952 | tf_op jit(solution)/shard_map/ppermute | solution.py:415
  29.5 5.8 %collective-permute-done.7.p2.g2 = bf16[256,640]{1,0:T(8,128)(2,1)S(1)} collective-permute-done((bf16[256,640]{1,0:T(8,128)(2,1)S(1)}, bf16[256,640]{1,0:T(8,128)(2,1)S(1)}, u32[]{:S(2)}, u32[]{:S(2)}) %collective-permute-start.7) | collective-permute-done | bytes 327712 | tf_op jit(solution)/shard_map/ppermute | solution.py:415
  35.3 2.4 %shard_map.72 = (bf16[4,256,768]{2,1,0:T(8,128)(2,1)S(1)}, bf16[512,768]{1,0:T(8,128)(2,1)S(1)}, f32[8,768]{1,0:T(8,128)S(1)}) custom-call(s32[7]{0:T(128)S(1)} %stack.23.where_ref, bf16[256,640]{1,0:T(8,128)(2,1)S(1)} %constant_dynamic-update-slice_fusion.p0.g0, bf16[256,640]{1,0:T(8,128)(2,1)S(1)} %collective-permute-done.6.p1.g1, ...), custom_call_target="tpu_custom_call" | custom-call | flops 268435456 | bytes 4194304 | tf_op jit(solution)/shard_map/pallas_call | solution.py:393
  38.4 5.9 %collective-permute-start.8 = (bf16[128,512]{1,0:T(8,128)(2,1)S(1)}, bf16[128,512]{1,0:T(8,128)(2,1)S(1)}, u32[]{:S(2)}, u32[]{:S(2)}) collective-permute-start(bf16[128,512]{1,0:T(8,128)(2,1)S(1)} %get-tuple-element.86), channel_id=1, source_target_pairs={{0,192},{1,193},{2,194},{3,195},{4,196},{5,197},{6,198},{7,199},{8... | collective-permute-start | bytes 393224 | tf_op jit(solution)/shard_map/ppermute | solution.py:415
  49.5 2.4 %collective-permute-done.10 = bf16[64,512]{1,0:T(8,128)(2,1)S(1)} collective-permute-done((bf16[64,512]{1,0:T(8,128)(2,1)S(1)}, bf16[64,512]{1,0:T(8,128)(2,1)S(1)}, u32[]{:S(2)}, u32[]{:S(2)}) %collective-permute-start.10) | collective-permute-done | bytes 65568 | tf_op jit(solution)/shard_map/ppermute | solution.py:415
  53.7 5.2 %collective-permute-done.12.g2 = bf16[256,512]{1,0:T(8,128)(2,1)S(1)} collective-permute-done((bf16[256,512]{1,0:T(8,128)(2,1)S(1)}, bf16[256,512]{1,0:T(8,128)(2,1)S(1)}, u32[]{:S(2)}, u32[]{:S(2)}) %collective-permute-start.12) | collective-permute-done | bytes 262176 | tf_op jit(solution)/shard_map/ppermute | solution.py:415
  61.0 5.0 %collective-permute-start.14 = (bf16[64,512]{1,0:T(8,128)(2,1)S(1)}, bf16[64,512]{1,0:T(8,128)(2,1)S(1)}, u32[]{:S(2)}, u32[]{:S(2)}) collective-permute-start(bf16[64,512]{1,0:T(8,128)(2,1)S(1)} %get-tuple-element.96), channel_id=1, source_target_pairs={{0,193},{1,194},{2,195},{3,192},{4,197},{5,198},{6,199},{7,196},{8... | collective-permute-start | bytes 196616 | tf_op jit(solution)/shard_map/ppermute | solution.py:415
  68.0 4.4 %collective-permute-done.15 = bf16[64,512]{1,0:T(8,128)(2,1)S(1)} collective-permute-done((bf16[64,512]{1,0:T(8,128)(2,1)S(1)}, bf16[64,512]{1,0:T(8,128)(2,1)S(1)}, u32[]{:S(2)}, u32[]{:S(2)}) %collective-permute-start.15) | collective-permute-done | bytes 65568 | tf_op jit(solution)/shard_map/ppermute | solution.py:415
  74.0 5.4 %collective-permute-done.17.g2 = bf16[256,512]{1,0:T(8,128)(2,1)S(1)} collective-permute-done((bf16[256,512]{1,0:T(8,128)(2,1)S(1)}, bf16[256,512]{1,0:T(8,128)(2,1)S(1)}, u32[]{:S(2)}, u32[]{:S(2)}) %collective-permute-start.17) | collective-permute-done | bytes 262176 | tf_op jit(solution)/shard_map/ppermute | solution.py:415
  81.9 4.5 %collective-permute-start.20 = (bf16[64,512]{1,0:T(8,128)(2,1)S(1)}, bf16[64,512]{1,0:T(8,128)(2,1)S(1)}, u32[]{:S(2)}, u32[]{:S(2)}) collective-permute-start(bf16[64,512]{1,0:T(8,128)(2,1)S(1)} %get-tuple-element.107), channel_id=1, source_target_pairs={{0,195},{1,192},{2,193},{3,194},{4,199},{5,196},{6,197},{7,198},{8... | collective-permute-start | bytes 196616 | tf_op jit(solution)/shard_map/ppermute | solution.py:415
  86.5 2.9 %shard_map.78.dq_ref = bf16[128,512]{1,0:T(8,128)(2,1)S(1)} custom-call(s32[7]{0:T(128)S(1)} %stack.23.where_ref, bf16[128,512]{1,0:T(8,128)(2,1)S(1)} %collective-permute-done.18.g_ref, bf16[512,512]{1,0:T(8,128)(2,1)S(1)} %bitcast.37, bf16[128,512]{1,0:T(8,128)(2,1)S(1)} %get-tuple-element.78.mixed_ref, bf16[768,1024]{1,0:T(8,128)(2,1)S(1)} %get-tuple-element.79.kv_ref, ...), custom_call_target="tpu_custom_call" | custom-call | flops 536870912 | bytes 4194304 | tf_op jit(solution)/shard_map/pallas_call | solution.py:393
  89.5 4.7 %collective-permute-start.22 = (bf16[256,512]{1,0:T(8,128)(2,1)S(1)}, bf16[256,512]{1,0:T(8,128)(2,1)S(1)}, u32[]{:S(2)}, u32[]{:S(2)}) collective-permute-start(bf16[256,512]{1,0:T(8,128)(2,1)S(1)} %constant_dynamic-update-slice_fusion.9.g0), channel_id=1, source_target_pairs={{0,60},{1,61},{2,62},{3,63},{4,8},{5,9},{6,10},{7,11},{8,4},{9,5},... | collective-permute-start | bytes 786440 | tf_op jit(solution)/shard_map/ppermute | solution.py:415
  94.8 3.4 %collective-permute-done.22.g2 = bf16[256,512]{1,0:T(8,128)(2,1)S(1)} collective-permute-done((bf16[256,512]{1,0:T(8,128)(2,1)S(1)}, bf16[256,512]{1,0:T(8,128)(2,1)S(1)}, u32[]{:S(2)}, u32[]{:S(2)}) %collective-permute-start.22) | collective-permute-done | bytes 262176 | tf_op jit(solution)/shard_map/ppermute | solution.py:415
  98.3 2.7 %shard_map.79.d0.kv_ref = bf16[128,1024]{1,0:T(8,128)(2,1)S(1)} custom-call(s32[7]{0:T(128)S(1)} %stack.23.where_ref, bf16[256,512]{1,0:T(8,128)(2,1)S(1)} %constant_dynamic-update-slice_fusion.9.g0, bf16[256,512]{1,0:T(8,128)(2,1)S(1)} %collective-permute-done.21.g1, bf16[256,512]{1,0:T(8,128)(2,1)S(1)} %collective-permute-done.22.g2, ...), custom_call_target="tpu_custom_call" | custom-call | flops 1073741824 | bytes 4194304 | tf_op jit(solution)/shard_map/pallas_call | solution.py:393
  102.1 2.1 %collective-permute-start.27 = (bf16[64,1024]{1,0:T(8,128)(2,1)S(1)}, bf16[64,1024]{1,0:T(8,128)(2,1)S(1)}, u32[]{:S(2)}, u32[]{:S(2)}) collective-permute-start(bf16[64,1024]{1,0:T(8,128)(2,1)S(1)} %get-tuple-element.118), channel_id=1, source_target_pairs={{0,2},{1,3},{2,0},{3,1},{4,6},{5,7},{6,4},{7,5},{8,10},{9,11},{10,... | collective-permute-start | bytes 393224 | tf_op jit(solution)/shard_map/ppermute | solution.py:415
  104.2 2.4 %collective-permute-start.26 = (bf16[64,1024]{1,0:T(8,128)(2,1)S(1)}, bf16[64,1024]{1,0:T(8,128)(2,1)S(1)}, u32[]{:S(2)}, u32[]{:S(2)}) collective-permute-start(bf16[64,1024]{1,0:T(8,128)(2,1)S(1)} %get-tuple-element.116), channel_id=1, source_target_pairs={{0,1},{1,2},{2,3},{3,0},{4,5},{5,6},{6,7},{7,4},{8,9},{9,10},{10,1... | collective-permute-start | bytes 393224 | tf_op jit(solution)/shard_map/ppermute | solution.py:415
  108.8 3.6 %collective-permute-start.30 = (bf16[64,1024]{1,0:T(8,128)(2,1)S(1)}, bf16[64,1024]{1,0:T(8,128)(2,1)S(1)}, u32[]{:S(2)}, u32[]{:S(2)}) collective-permute-start(bf16[64,1024]{1,0:T(8,128)(2,1)S(1)} %get-tuple-element.123), channel_id=1, source_target_pairs={{0,2},{1,3},{2,0},{3,1},{4,6},{5,7},{6,4},{7,5},{8,10},{9,11},{10,... | collective-permute-start | bytes 393224 | tf_op jit(solution)/shard_map/ppermute | solution.py:415
  114.7 4.1 %collective-permute-done.25.refs_7_ = bf16[64,1024]{1,0:T(8,128)(2,1)S(1)} collective-permute-done((bf16[64,1024]{1,0:T(8,128)(2,1)S(1)}, bf16[64,1024]{1,0:T(8,128)(2,1)S(1)}, u32[]{:S(2)}, u32[]{:S(2)}) %collective-permute-start.25) | collective-permute-done | bytes 131104 | tf_op jit(solution)/shard_map/ppermute | solution.py:415
  119.5 16.2 %all_to_all.5.part_ref = bf16[8,8,2048]{2,1,0:T(8,128)(2,1)S(1)} all-to-all(bf16[8,8,2048]{2,1,0:T(8,128)(2,1)S(1)} %bitcast.45), channel_id=1, replica_groups=mesh['pipe'=4,'z'=8,'core'=2,'col'=4] {'z'}, dimensions={0} | all-to-all | bytes 524288 | tf_op jit(solution)/shard_map/all_to_all | solution.py:540
  (88 shorter events, 36.4 us)
Async XLA Ops:
  1.6 5.7 %collective-permute-start = (bf16[64,512]{1,0:T(8,128)(2,1)S(1)}, bf16[64,512]{1,0:T(8,128)(2,1)S(1)}, u32[]{:S(2)}, u32[]{:S(2)}) collective-permute-start(bf16[64,512]{1,0:T(8,128)(2,1)S(1)} %get-tuple-element.128), channel_id=1, source_target_pairs={{0,1},{1,2},{2,3},{3,0},{4,5},{5,6},{6,7},{7,4},{8,9},{9,10},{10,1... | collective-permute-start | bytes 196616 | tf_op jit(solution)/shard_map/ppermute | solution.py:415
  9.3 7.0 %collective-permute-start.3 = (bf16[256,512]{1,0:T(8,128)(2,1)S(1)}, bf16[256,512]{1,0:T(8,128)(2,1)S(1)}, u32[]{:S(2)}, u32[]{:S(2)}) collective-permute-start(bf16[256,512]{1,0:T(8,128)(2,1)S(1)} %constant_dynamic-update-slice_fusion.12), channel_id=1, source_target_pairs={{0,60},{1,61},{2,62},{3,63},{4,8},{5,9},{6,10},{7,11},{8,4},{9,5},... | collective-permute-start | bytes 786440 | tf_op jit(solution)/shard_map/ppermute | solution.py:415
  20.4 7.1 %collective-permute-start.4 = (bf16[64,640]{1,0:T(8,128)(2,1)S(1)}, bf16[64,640]{1,0:T(8,128)(2,1)S(1)}, u32[]{:S(2)}, u32[]{:S(2)}) collective-permute-start(bf16[64,640]{1,0:T(8,128)(2,1)S(1)} %get-tuple-element.75), channel_id=1, source_target_pairs={{0,1},{1,2},{2,3},{3,0},{4,5},{5,6},{6,7},{7,4},{8,9},{9,10},{10,1... | collective-permute-start | bytes 245768 | tf_op jit(solution)/shard_map/ppermute | solution.py:415
  27.5 7.8 %collective-permute-start.7 = (bf16[256,640]{1,0:T(8,128)(2,1)S(1)}, bf16[256,640]{1,0:T(8,128)(2,1)S(1)}, u32[]{:S(2)}, u32[]{:S(2)}) collective-permute-start(bf16[256,640]{1,0:T(8,128)(2,1)S(1)} %constant_dynamic-update-slice_fusion.p0.g0), channel_id=1, source_target_pairs={{0,60},{1,61},{2,62},{3,63},{4,8},{5,9},{6,10},{7,11},{8,4},{9,5},... | collective-permute-start | bytes 983048 | tf_op jit(solution)/shard_map/ppermute | solution.py:415
  29.5 5.8 %collective-permute-start.6 = (bf16[256,640]{1,0:T(8,128)(2,1)S(1)}, bf16[256,640]{1,0:T(8,128)(2,1)S(1)}, u32[]{:S(2)}, u32[]{:S(2)}) collective-permute-start(bf16[256,640]{1,0:T(8,128)(2,1)S(1)} %constant_dynamic-update-slice_fusion.p0.g0), channel_id=1, source_target_pairs={{0,4},{1,5},{2,6},{3,7},{4,0},{5,1},{6,2},{7,3},{8,12},{9,13},{10,... | collective-permute-start | bytes 983048 | tf_op jit(solution)/shard_map/ppermute | solution.py:415
  38.4 9.1 %collective-permute-start.8 = (bf16[128,512]{1,0:T(8,128)(2,1)S(1)}, bf16[128,512]{1,0:T(8,128)(2,1)S(1)}, u32[]{:S(2)}, u32[]{:S(2)}) collective-permute-start(bf16[128,512]{1,0:T(8,128)(2,1)S(1)} %get-tuple-element.86), channel_id=1, source_target_pairs={{0,192},{1,193},{2,194},{3,195},{4,196},{5,197},{6,198},{7,199},{8... | collective-permute-start | bytes 393224 | tf_op jit(solution)/shard_map/ppermute | solution.py:415
  45.5 6.4 %collective-permute-start.10 = (bf16[64,512]{1,0:T(8,128)(2,1)S(1)}, bf16[64,512]{1,0:T(8,128)(2,1)S(1)}, u32[]{:S(2)}, u32[]{:S(2)}) collective-permute-start(bf16[64,512]{1,0:T(8,128)(2,1)S(1)} %get-tuple-element.89), channel_id=1, source_target_pairs={{0,195},{1,192},{2,193},{3,194},{4,199},{5,196},{6,197},{7,198},{8... | collective-permute-start | bytes 196616 | tf_op jit(solution)/shard_map/ppermute | solution.py:415
  51.9 7.0 %collective-permute-start.12 = (bf16[256,512]{1,0:T(8,128)(2,1)S(1)}, bf16[256,512]{1,0:T(8,128)(2,1)S(1)}, u32[]{:S(2)}, u32[]{:S(2)}) collective-permute-start(bf16[256,512]{1,0:T(8,128)(2,1)S(1)} %constant_dynamic-update-slice_fusion.3.g0), channel_id=1, source_target_pairs={{0,60},{1,61},{2,62},{3,63},{4,8},{5,9},{6,10},{7,11},{8,4},{9,5},... | collective-permute-start | bytes 786440 | tf_op jit(solution)/shard_map/ppermute | solution.py:415
  59.5 6.7 %collective-permute-start.13 = (bf16[128,512]{1,0:T(8,128)(2,1)S(1)}, bf16[128,512]{1,0:T(8,128)(2,1)S(1)}, u32[]{:S(2)}, u32[]{:S(2)}) collective-permute-start(bf16[128,512]{1,0:T(8,128)(2,1)S(1)} %get-tuple-element.95), channel_id=1, source_target_pairs={{0,192},{1,193},{2,194},{3,195},{4,196},{5,197},{6,198},{7,199},{8... | collective-permute-start | bytes 393224 | tf_op jit(solution)/shard_map/ppermute | solution.py:415
  61.0 6.9 %collective-permute-start.14 = (bf16[64,512]{1,0:T(8,128)(2,1)S(1)}, bf16[64,512]{1,0:T(8,128)(2,1)S(1)}, u32[]{:S(2)}, u32[]{:S(2)}) collective-permute-start(bf16[64,512]{1,0:T(8,128)(2,1)S(1)} %get-tuple-element.96), channel_id=1, source_target_pairs={{0,193},{1,194},{2,195},{3,192},{4,197},{5,198},{6,199},{7,196},{8... | collective-permute-start | bytes 196616 | tf_op jit(solution)/shard_map/ppermute | solution.py:415
  66.0 6.4 %collective-permute-start.15 = (bf16[64,512]{1,0:T(8,128)(2,1)S(1)}, bf16[64,512]{1,0:T(8,128)(2,1)S(1)}, u32[]{:S(2)}, u32[]{:S(2)}) collective-permute-start(bf16[64,512]{1,0:T(8,128)(2,1)S(1)} %get-tuple-element.98), channel_id=1, source_target_pairs={{0,195},{1,192},{2,193},{3,194},{4,199},{5,196},{6,197},{7,198},{8... | collective-permute-start | bytes 196616 | tf_op jit(solution)/shard_map/ppermute | solution.py:415
  72.4 7.0 %collective-permute-start.17 = (bf16[256,512]{1,0:T(8,128)(2,1)S(1)}, bf16[256,512]{1,0:T(8,128)(2,1)S(1)}, u32[]{:S(2)}, u32[]{:S(2)}) collective-permute-start(bf16[256,512]{1,0:T(8,128)(2,1)S(1)} %constant_dynamic-update-slice_fusion.6.g0), channel_id=1, source_target_pairs={{0,60},{1,61},{2,62},{3,63},{4,8},{5,9},{6,10},{7,11},{8,4},{9,5},... | collective-permute-start | bytes 786440 | tf_op jit(solution)/shard_map/ppermute | solution.py:415
  80.3 6.2 %collective-permute-start.18 = (bf16[128,512]{1,0:T(8,128)(2,1)S(1)}, bf16[128,512]{1,0:T(8,128)(2,1)S(1)}, u32[]{:S(2)}, u32[]{:S(2)}) collective-permute-start(bf16[128,512]{1,0:T(8,128)(2,1)S(1)} %get-tuple-element.103), channel_id=1, source_target_pairs={{0,192},{1,193},{2,194},{3,195},{4,196},{5,197},{6,198},{7,199},{8... | collective-permute-start | bytes 393224 | tf_op jit(solution)/shard_map/ppermute | solution.py:415
  81.6 7.7 %collective-permute-start.19 = (bf16[64,512]{1,0:T(8,128)(2,1)S(1)}, bf16[64,512]{1,0:T(8,128)(2,1)S(1)}, u32[]{:S(2)}, u32[]{:S(2)}) collective-permute-start(bf16[64,512]{1,0:T(8,128)(2,1)S(1)} %get-tuple-element.104), channel_id=1, source_target_pairs={{0,193},{1,194},{2,195},{3,192},{4,197},{5,198},{6,199},{7,196},{8... | collective-permute-start | bytes 196616 | tf_op jit(solution)/shard_map/ppermute | solution.py:415
  81.9 7.5 %collective-permute-start.20 = (bf16[64,512]{1,0:T(8,128)(2,1)S(1)}, bf16[64,512]{1,0:T(8,128)(2,1)S(1)}, u32[]{:S(2)}, u32[]{:S(2)}) collective-permute-start(bf16[64,512]{1,0:T(8,128)(2,1)S(1)} %get-tuple-element.107), channel_id=1, source_target_pairs={{0,195},{1,192},{2,193},{3,194},{4,199},{5,196},{6,197},{7,198},{8... | collective-permute-start | bytes 196616 | tf_op jit(solution)/shard_map/ppermute | solution.py:415
  89.5 8.8 %collective-permute-start.22 = (bf16[256,512]{1,0:T(8,128)(2,1)S(1)}, bf16[256,512]{1,0:T(8,128)(2,1)S(1)}, u32[]{:S(2)}, u32[]{:S(2)}) collective-permute-start(bf16[256,512]{1,0:T(8,128)(2,1)S(1)} %constant_dynamic-update-slice_fusion.9.g0), channel_id=1, source_target_pairs={{0,60},{1,61},{2,62},{3,63},{4,8},{5,9},{6,10},{7,11},{8,4},{9,5},... | collective-permute-start | bytes 786440 | tf_op jit(solution)/shard_map/ppermute | solution.py:415
  94.2 6.8 %collective-permute-start.23 = (bf16[256,512]{1,0:T(8,128)(2,1)S(1)}, bf16[256,512]{1,0:T(8,128)(2,1)S(1)}, u32[]{:S(2)}, u32[]{:S(2)}) collective-permute-start(bf16[256,512]{1,0:T(8,128)(2,1)S(1)} %pad_maximum_fusion), channel_id=1, source_target_pairs={{0,4},{1,5},{2,6},{3,7},{4,0},{5,1},{6,2},{7,3},{8,12},{9,13},{10,... | collective-permute-start | bytes 786440 | tf_op jit(solution)/shard_map/ppermute | solution.py:415
  101.0 5.7 %collective-permute-start.24 = (bf16[128,1024]{1,0:T(8,128)(2,1)S(1)}, bf16[128,1024]{1,0:T(8,128)(2,1)S(1)}, u32[]{:S(2)}, u32[]{:S(2)}) collective-permute-start(bf16[128,1024]{1,0:T(8,128)(2,1)S(1)} %shard_map.79.d0.kv_ref), channel_id=1, source_target_pairs={{0,4},{1,5},{2,6},{3,7},{4,0},{5,1},{6,2},{7,3},{8,12},{9,13},{10,... | collective-permute-start | bytes 786440 | tf_op jit(solution)/shard_map/ppermute | solution.py:415
  102.1 10.3 %collective-permute-start.27 = (bf16[64,1024]{1,0:T(8,128)(2,1)S(1)}, bf16[64,1024]{1,0:T(8,128)(2,1)S(1)}, u32[]{:S(2)}, u32[]{:S(2)}) collective-permute-start(bf16[64,1024]{1,0:T(8,128)(2,1)S(1)} %get-tuple-element.118), channel_id=1, source_target_pairs={{0,2},{1,3},{2,0},{3,1},{4,6},{5,7},{6,4},{7,5},{8,10},{9,11},{10,... | collective-permute-start | bytes 393224 | tf_op jit(solution)/shard_map/ppermute | solution.py:415
  104.2 14.5 %collective-permute-start.26 = (bf16[64,1024]{1,0:T(8,128)(2,1)S(1)}, bf16[64,1024]{1,0:T(8,128)(2,1)S(1)}, u32[]{:S(2)}, u32[]{:S(2)}) collective-permute-start(bf16[64,1024]{1,0:T(8,128)(2,1)S(1)} %get-tuple-element.116), channel_id=1, source_target_pairs={{0,1},{1,2},{2,3},{3,0},{4,5},{5,6},{6,7},{7,4},{8,9},{9,10},{10,1... | collective-permute-start | bytes 393224 | tf_op jit(solution)/shard_map/ppermute | solution.py:415
  106.6 12.2 %collective-permute-start.28 = (bf16[64,1024]{1,0:T(8,128)(2,1)S(1)}, bf16[64,1024]{1,0:T(8,128)(2,1)S(1)}, u32[]{:S(2)}, u32[]{:S(2)}) collective-permute-start(bf16[64,1024]{1,0:T(8,128)(2,1)S(1)} %get-tuple-element.120), channel_id=1, source_target_pairs={{0,3},{1,0},{2,1},{3,2},{4,7},{5,4},{6,5},{7,6},{8,11},{9,8},{10,9... | collective-permute-start | bytes 393224 | tf_op jit(solution)/shard_map/ppermute | solution.py:415
  107.7 11.1 %collective-permute-start.25 = (bf16[64,1024]{1,0:T(8,128)(2,1)S(1)}, bf16[64,1024]{1,0:T(8,128)(2,1)S(1)}, u32[]{:S(2)}, u32[]{:S(2)}) collective-permute-start(bf16[64,1024]{1,0:T(8,128)(2,1)S(1)} %get-tuple-element.112), channel_id=1, source_target_pairs={{0,3},{1,0},{2,1},{3,2},{4,7},{5,4},{6,5},{7,6},{8,11},{9,8},{10,9... | collective-permute-start | bytes 393224 | tf_op jit(solution)/shard_map/ppermute | solution.py:415
  108.8 10.0 %collective-permute-start.30 = (bf16[64,1024]{1,0:T(8,128)(2,1)S(1)}, bf16[64,1024]{1,0:T(8,128)(2,1)S(1)}, u32[]{:S(2)}, u32[]{:S(2)}) collective-permute-start(bf16[64,1024]{1,0:T(8,128)(2,1)S(1)} %get-tuple-element.123), channel_id=1, source_target_pairs={{0,2},{1,3},{2,0},{3,1},{4,6},{5,7},{6,4},{7,5},{8,10},{9,11},{10,... | collective-permute-start | bytes 393224 | tf_op jit(solution)/shard_map/ppermute | solution.py:415
  112.4 6.4 %collective-permute-start.29 = (bf16[64,1024]{1,0:T(8,128)(2,1)S(1)}, bf16[64,1024]{1,0:T(8,128)(2,1)S(1)}, u32[]{:S(2)}, u32[]{:S(2)}) collective-permute-start(bf16[64,1024]{1,0:T(8,128)(2,1)S(1)} %get-tuple-element.122), channel_id=1, source_target_pairs={{0,1},{1,2},{2,3},{3,0},{4,5},{5,6},{6,7},{7,4},{8,9},{9,10},{10,1... | collective-permute-start | bytes 393224 | tf_op jit(solution)/shard_map/ppermute | solution.py:415
  (14 other events, 68.4 us)

commit v4 on v3

--- a/solution.py
+++ b/solution.py
@@ -494,10 +494,8 @@
             low, low_side, high_side = sends
             gradient = routed(low, lambda p, r, c: (p - 1, r, c))
             left, right = col_rims(low_side, high_side, 1)
-            left, d_query = lax.optimization_barrier(
-                (left, query_side(turn, gradient, *((state[0],) if last else ())))
-            )
             gs = row_rims([gradient, left, right])
+            d_query = query_side(turn, gradient, *((state[0],) if last else ()))
         fixed = (w_out, mixed_turned if turn else delta, proj, queries, k_probs)
         scratch = [pltpu.VMEM((D, REGION), BF16)]
         if not last:

time: 139 us -> 136 us (0.978)
  starting transfers between devices: 47.4 us -> 41.5 us
  blocking collectives: 16.2 us -> 18.2 us
    ppermute x31, starting transfers between devices: 47.4 us -> 41.5 us  [routed(): return lax.ppermute(block, AXES, pairs)]
    all_to_all x1, blocking collectives: 16.2 us -> 18.2 us  [body(): part = lax.all_to_all(part, 'z', 0, 0, tiled=True)]
  transfers between devices with their start and end apart: 31 -> 31, of which waited for: 13 -> 16; matrix products, arithmetic and copies ran while one was open for 0% -> 0% of each run, Pallas kernels for 11% -> 11%
where the time goes in v4:
time: 136 us; the launch traced here: 134 us
  waiting for transfers between devices  43.8 us (32%)
  starting transfers between devices  41.5 us (31%)
  Pallas kernels  24.9 us (18%)
  blocking collectives  18.2 us (13%)
  local copies, waits for them, and re-layouts  4.5 us (3%)
    ppermute x31, waiting for transfers between devices, routed(): return lax.ppermute(block, AXES, pairs)  43.8 us
    ppermute x31, starting transfers between devices, routed(): return lax.ppermute(block, AXES, pairs)  41.5 us
    pallas_call x18, Pallas kernels, call(): pl.pallas_call(kernel, out_shape=[jax.ShapeDtypeStruct(s, t) for s, t in...  24.9 us
    all_to_all x1, blocking collectives, body(): part = lax.all_to_all(part, 'z', 0, 0, tiled=True)  18.2 us
    unnamed x22, local copies, waits for them, and re-layouts  3.44 us
  transfers between devices with their start and end apart: 31, of which 16 were waited for; matrix products, arithmetic and copies ran while one was open for 0% of the time, Pallas kernels for 11%

profile of v4, /device:TPU:6, one launch (start us, length us, event | category | flops | bytes accessed | tf_op | source)
XLA Modules:
  0.0 133.8 jit_solution(5768466990053379694)
XLA Ops:
  1.6 2.3 %collective-permute-start = (bf16[64,512]{1,0:T(8,128)(2,1)S(1)}, bf16[64,512]{1,0:T(8,128)(2,1)S(1)}, u32[]{:S(2)}, u32[]{:S(2)}) collective-permute-start(bf16[64,512]{1,0:T(8,128)(2,1)S(1)} %get-tuple-element.116), channel_id=1, source_target_pairs={{0,1},{1,2},{2,3},{3,0},{4,5},{5,6},{6,7},{7,4},{8,9},{9,10},{10,1... | collective-permute-start | bytes 196616 | tf_op jit(solution)/shard_map/ppermute | solution.py:415
  7.3 2.1 %collective-permute-done.1.right_ref = bf16[64,512]{1,0:T(8,128)(2,1)S(1)} collective-permute-done((bf16[64,512]{1,0:T(8,128)(2,1)S(1)}, bf16[64,512]{1,0:T(8,128)(2,1)S(1)}, u32[]{:S(2)}, u32[]{:S(2)}) %collective-permute-start.1) | collective-permute-done | bytes 65568 | tf_op jit(solution)/shard_map/ppermute | solution.py:415
  9.3 2.6 %collective-permute-start.3 = (bf16[256,512]{1,0:T(8,128)(2,1)S(1)}, bf16[256,512]{1,0:T(8,128)(2,1)S(1)}, u32[]{:S(2)}, u32[]{:S(2)}) collective-permute-start(bf16[256,512]{1,0:T(8,128)(2,1)S(1)} %constant_dynamic-update-slice_fusion.12), channel_id=1, source_target_pairs={{0,60},{1,61},{2,62},{3,63},{4,8},{5,9},{6,10},{7,11},{8,4},{9,5},... | collective-permute-start | bytes 786440 | tf_op jit(solution)/shard_map/ppermute | solution.py:415
  14.1 2.2 %collective-permute-done.3.x2 = bf16[256,512]{1,0:T(8,128)(2,1)S(1)} collective-permute-done((bf16[256,512]{1,0:T(8,128)(2,1)S(1)}, bf16[256,512]{1,0:T(8,128)(2,1)S(1)}, u32[]{:S(2)}, u32[]{:S(2)}) %collective-permute-start.3) | collective-permute-done | bytes 262176 | tf_op jit(solution)/shard_map/ppermute | solution.py:415
  16.4 4.0 %shard_map.69 = (bf16[768,1024]{1,0:T(8,128)(2,1)S(1)}, bf16[4,256,768]{2,1,0:T(8,128)(2,1)S(1)}, bf16[128,512]{1,0:T(8,128)(2,1)S(1)}, bf16[512,512]{1,0:T(8,12...) custom-call(s32[7]{0:T(128)S(1)} %stack.23.where_ref, ...), custom_call_target="tpu_custom_call" | custom-call | flops 2147483648 | bytes 4194304 | tf_op jit(solution)/shard_map/pallas_call | solution.py:393
  24.2 3.3 %collective-permute-done.5 = bf16[64,640]{1,0:T(8,128)(2,1)S(1)} collective-permute-done((bf16[64,640]{1,0:T(8,128)(2,1)S(1)}, bf16[64,640]{1,0:T(8,128)(2,1)S(1)}, u32[]{:S(2)}, u32[]{:S(2)}) %collective-permute-start.5) | collective-permute-done | bytes 81952 | tf_op jit(solution)/shard_map/ppermute | solution.py:415
  29.5 5.8 %collective-permute-done.7.p2.g2 = bf16[256,640]{1,0:T(8,128)(2,1)S(1)} collective-permute-done((bf16[256,640]{1,0:T(8,128)(2,1)S(1)}, bf16[256,640]{1,0:T(8,128)(2,1)S(1)}, u32[]{:S(2)}, u32[]{:S(2)}) %collective-permute-start.7) | collective-permute-done | bytes 327712 | tf_op jit(solution)/shard_map/ppermute | solution.py:415
  35.3 2.4 %shard_map.72 = (bf16[4,256,768]{2,1,0:T(8,128)(2,1)S(1)}, bf16[512,768]{1,0:T(8,128)(2,1)S(1)}, f32[8,768]{1,0:T(8,128)S(1)}) custom-call(s32[7]{0:T(128)S(1)} %stack.23.where_ref, bf16[256,640]{1,0:T(8,128)(2,1)S(1)} %constant_dynamic-update-slice_fusion.p0.g0, bf16[256,640]{1,0:T(8,128)(2,1)S(1)} %collective-permute-done.6.p1.g1, ...), custom_call_target="tpu_custom_call" | custom-call | flops 268435456 | bytes 4194304 | tf_op jit(solution)/shard_map/pallas_call | solution.py:393
  38.4 5.9 %collective-permute-start.8 = (bf16[128,512]{1,0:T(8,128)(2,1)S(1)}, bf16[128,512]{1,0:T(8,128)(2,1)S(1)}, u32[]{:S(2)}, u32[]{:S(2)}) collective-permute-start(bf16[128,512]{1,0:T(8,128)(2,1)S(1)} %get-tuple-element.80), channel_id=1, source_target_pairs={{0,192},{1,193},{2,194},{3,195},{4,196},{5,197},{6,198},{7,199},{8... | collective-permute-start | bytes 393224 | tf_op jit(solution)/shard_map/ppermute | solution.py:415
  45.5 2.0 %collective-permute-done.8.g_ref.rest_1_ = bf16[128,512]{1,0:T(8,128)(2,1)S(1)} collective-permute-done((bf16[128,512]{1,0:T(8,128)(2,1)S(1)}, bf16[128,512]{1,0:T(8,128)(2,1)S(1)}, u32[]{:S(2)}, u32[]{:S(2)}) %collective-permute-start.8) | collective-permute-done | bytes 131104 | tf_op jit(solution)/shard_map/ppermute | solution.py:415
  49.5 2.4 %collective-permute-done.10 = bf16[64,512]{1,0:T(8,128)(2,1)S(1)} collective-permute-done((bf16[64,512]{1,0:T(8,128)(2,1)S(1)}, bf16[64,512]{1,0:T(8,128)(2,1)S(1)}, u32[]{:S(2)}, u32[]{:S(2)}) %collective-permute-start.10) | collective-permute-done | bytes 65568 | tf_op jit(solution)/shard_map/ppermute | solution.py:415
  54.3 4.6 %collective-permute-done.12.g2 = bf16[256,512]{1,0:T(8,128)(2,1)S(1)} collective-permute-done((bf16[256,512]{1,0:T(8,128)(2,1)S(1)}, bf16[256,512]{1,0:T(8,128)(2,1)S(1)}, u32[]{:S(2)}, u32[]{:S(2)}) %collective-permute-start.12) | collective-permute-done | bytes 262176 | tf_op jit(solution)/shard_map/ppermute | solution.py:415
  60.5 4.4 %collective-permute-start.14 = (bf16[64,512]{1,0:T(8,128)(2,1)S(1)}, bf16[64,512]{1,0:T(8,128)(2,1)S(1)}, u32[]{:S(2)}, u32[]{:S(2)}) collective-permute-start(bf16[64,512]{1,0:T(8,128)(2,1)S(1)} %get-tuple-element.88), channel_id=1, source_target_pairs={{0,193},{1,194},{2,195},{3,192},{4,197},{5,198},{6,199},{7,196},{8... | collective-permute-start | bytes 196616 | tf_op jit(solution)/shard_map/ppermute | solution.py:415
  66.8 4.5 %collective-permute-done.15 = bf16[64,512]{1,0:T(8,128)(2,1)S(1)} collective-permute-done((bf16[64,512]{1,0:T(8,128)(2,1)S(1)}, bf16[64,512]{1,0:T(8,128)(2,1)S(1)}, u32[]{:S(2)}, u32[]{:S(2)}) %collective-permute-start.15) | collective-permute-done | bytes 65568 | tf_op jit(solution)/shard_map/ppermute | solution.py:415
  71.9 6.3 %collective-permute-done.17.g2 = bf16[256,512]{1,0:T(8,128)(2,1)S(1)} collective-permute-done((bf16[256,512]{1,0:T(8,128)(2,1)S(1)}, bf16[256,512]{1,0:T(8,128)(2,1)S(1)}, u32[]{:S(2)}, u32[]{:S(2)}) %collective-permute-start.17) | collective-permute-done | bytes 262176 | tf_op jit(solution)/shard_map/ppermute | solution.py:415
  80.6 4.3 %collective-permute-start.20 = (bf16[64,512]{1,0:T(8,128)(2,1)S(1)}, bf16[64,512]{1,0:T(8,128)(2,1)S(1)}, u32[]{:S(2)}, u32[]{:S(2)}) collective-permute-start(bf16[64,512]{1,0:T(8,128)(2,1)S(1)} %get-tuple-element.95), channel_id=1, source_target_pairs={{0,195},{1,192},{2,193},{3,194},{4,199},{5,196},{6,197},{7,198},{8... | collective-permute-start | bytes 196616 | tf_op jit(solution)/shard_map/ppermute | solution.py:415
  87.0 2.4 %collective-permute-start.22 = (bf16[256,512]{1,0:T(8,128)(2,1)S(1)}, bf16[256,512]{1,0:T(8,128)(2,1)S(1)}, u32[]{:S(2)}, u32[]{:S(2)}) collective-permute-start(bf16[256,512]{1,0:T(8,128)(2,1)S(1)} %constant_dynamic-update-slice_fusion.9.g0), channel_id=1, source_target_pairs={{0,60},{1,61},{2,62},{3,63},{4,8},{5,9},{6,10},{7,11},{8,4},{9,5},... | collective-permute-start | bytes 786440 | tf_op jit(solution)/shard_map/ppermute | solution.py:415
  89.4 2.9 %shard_map.79.dq_ref = bf16[128,512]{1,0:T(8,128)(2,1)S(1)} custom-call(s32[7]{0:T(128)S(1)} %stack.23.where_ref, bf16[128,512]{1,0:T(8,128)(2,1)S(1)} %collective-permute-done.18.g_ref, bf16[512,512]{1,0:T(8,128)(2,1)S(1)} %bitcast.37, bf16[128,512]{1,0:T(8,128)(2,1)S(1)} %get-tuple-element.72.mixed_ref, bf16[768,1024]{1,0:T(8,128)(2,1)S(1)} %get-tuple-element.73.kv_ref, ...), custom_call_target="tpu_custom_call" | custom-call | flops 536870912 | bytes 4194304 | tf_op jit(solution)/shard_map/pallas_call | solution.py:393
  94.0 2.7 %shard_map.78.d0.kv_ref = bf16[128,1024]{1,0:T(8,128)(2,1)S(1)} custom-call(s32[7]{0:T(128)S(1)} %stack.23.where_ref, bf16[256,512]{1,0:T(8,128)(2,1)S(1)} %constant_dynamic-update-slice_fusion.9.g0, bf16[256,512]{1,0:T(8,128)(2,1)S(1)} %collective-permute-done.21.g1, bf16[256,512]{1,0:T(8,128)(2,1)S(1)} %collective-permute-done.22.g2, ...), custom_call_target="tpu_custom_call" | custom-call | flops 1073741824 | bytes 4194304 | tf_op jit(solution)/shard_map/pallas_call | solution.py:393
  98.7 2.2 %collective-permute-start.26 = (bf16[64,1024]{1,0:T(8,128)(2,1)S(1)}, bf16[64,1024]{1,0:T(8,128)(2,1)S(1)}, u32[]{:S(2)}, u32[]{:S(2)}) collective-permute-start(bf16[64,1024]{1,0:T(8,128)(2,1)S(1)} %get-tuple-element.104), channel_id=1, source_target_pairs={{0,1},{1,2},{2,3},{3,0},{4,5},{5,6},{6,7},{7,4},{8,9},{9,10},{10,1... | collective-permute-start | bytes 393224 | tf_op jit(solution)/shard_map/ppermute | solution.py:415
  102.0 2.1 %collective-permute-start.25 = (bf16[64,1024]{1,0:T(8,128)(2,1)S(1)}, bf16[64,1024]{1,0:T(8,128)(2,1)S(1)}, u32[]{:S(2)}, u32[]{:S(2)}) collective-permute-start(bf16[64,1024]{1,0:T(8,128)(2,1)S(1)} %get-tuple-element.100), channel_id=1, source_target_pairs={{0,3},{1,0},{2,1},{3,2},{4,7},{5,4},{6,5},{7,6},{8,11},{9,8},{10,9... | collective-permute-start | bytes 393224 | tf_op jit(solution)/shard_map/ppermute | solution.py:415
  104.1 2.5 %collective-permute-start.30 = (bf16[64,1024]{1,0:T(8,128)(2,1)S(1)}, bf16[64,1024]{1,0:T(8,128)(2,1)S(1)}, u32[]{:S(2)}, u32[]{:S(2)}) collective-permute-start(bf16[64,1024]{1,0:T(8,128)(2,1)S(1)} %get-tuple-element.111), channel_id=1, source_target_pairs={{0,2},{1,3},{2,0},{3,1},{4,6},{5,7},{6,4},{7,5},{8,10},{9,11},{10,... | collective-permute-start | bytes 393224 | tf_op jit(solution)/shard_map/ppermute | solution.py:415
  111.4 2.4 %collective-permute-done.30.refs_6_ = bf16[64,1024]{1,0:T(8,128)(2,1)S(1)} collective-permute-done((bf16[64,1024]{1,0:T(8,128)(2,1)S(1)}, bf16[64,1024]{1,0:T(8,128)(2,1)S(1)}, u32[]{:S(2)}, u32[]{:S(2)}) %collective-permute-start.30) | collective-permute-done | bytes 131104 | tf_op jit(solution)/shard_map/ppermute | solution.py:415
  114.4 18.2 %all_to_all.5.part_ref = bf16[8,8,2048]{2,1,0:T(8,128)(2,1)S(1)} all-to-all(bf16[8,8,2048]{2,1,0:T(8,128)(2,1)S(1)} %bitcast.45), channel_id=1, replica_groups=mesh['pipe'=4,'z'=8,'core'=2,'col'=4] {'z'}, dimensions={0} | all-to-all | bytes 524288 | tf_op jit(solution)/shard_map/all_to_all | solution.py:538
  (88 shorter events, 38.6 us)
Async XLA Ops:
  1.6 5.7 %collective-permute-start = (bf16[64,512]{1,0:T(8,128)(2,1)S(1)}, bf16[64,512]{1,0:T(8,128)(2,1)S(1)}, u32[]{:S(2)}, u32[]{:S(2)}) collective-permute-start(bf16[64,512]{1,0:T(8,128)(2,1)S(1)} %get-tuple-element.116), channel_id=1, source_target_pairs={{0,1},{1,2},{2,3},{3,0},{4,5},{5,6},{6,7},{7,4},{8,9},{9,10},{10,1... | collective-permute-start | bytes 196616 | tf_op jit(solution)/shard_map/ppermute | solution.py:415
  3.9 5.5 %collective-permute-start.1 = (bf16[64,512]{1,0:T(8,128)(2,1)S(1)}, bf16[64,512]{1,0:T(8,128)(2,1)S(1)}, u32[]{:S(2)}, u32[]{:S(2)}) collective-permute-start(bf16[64,512]{1,0:T(8,128)(2,1)S(1)} %get-tuple-element.115), channel_id=1, source_target_pairs={{0,3},{1,0},{2,1},{3,2},{4,7},{5,4},{6,5},{7,6},{8,11},{9,8},{10,9... | collective-permute-start | bytes 196616 | tf_op jit(solution)/shard_map/ppermute | solution.py:415
  9.3 7.0 %collective-permute-start.3 = (bf16[256,512]{1,0:T(8,128)(2,1)S(1)}, bf16[256,512]{1,0:T(8,128)(2,1)S(1)}, u32[]{:S(2)}, u32[]{:S(2)}) collective-permute-start(bf16[256,512]{1,0:T(8,128)(2,1)S(1)} %constant_dynamic-update-slice_fusion.12), channel_id=1, source_target_pairs={{0,60},{1,61},{2,62},{3,63},{4,8},{5,9},{6,10},{7,11},{8,4},{9,5},... | collective-permute-start | bytes 786440 | tf_op jit(solution)/shard_map/ppermute | solution.py:415
  20.4 7.1 %collective-permute-start.4 = (bf16[64,640]{1,0:T(8,128)(2,1)S(1)}, bf16[64,640]{1,0:T(8,128)(2,1)S(1)}, u32[]{:S(2)}, u32[]{:S(2)}) collective-permute-start(bf16[64,640]{1,0:T(8,128)(2,1)S(1)} %get-tuple-element.69), channel_id=1, source_target_pairs={{0,1},{1,2},{2,3},{3,0},{4,5},{5,6},{6,7},{7,4},{8,9},{9,10},{10,1... | collective-permute-start | bytes 245768 | tf_op jit(solution)/shard_map/ppermute | solution.py:415
  21.8 5.7 %collective-permute-start.5 = (bf16[64,640]{1,0:T(8,128)(2,1)S(1)}, bf16[64,640]{1,0:T(8,128)(2,1)S(1)}, u32[]{:S(2)}, u32[]{:S(2)}) collective-permute-start(bf16[64,640]{1,0:T(8,128)(2,1)S(1)} %get-tuple-element.70), channel_id=1, source_target_pairs={{0,3},{1,0},{2,1},{3,2},{4,7},{5,4},{6,5},{7,6},{8,11},{9,8},{10,9... | collective-permute-start | bytes 245768 | tf_op jit(solution)/shard_map/ppermute | solution.py:415
  27.5 7.8 %collective-permute-start.7 = (bf16[256,640]{1,0:T(8,128)(2,1)S(1)}, bf16[256,640]{1,0:T(8,128)(2,1)S(1)}, u32[]{:S(2)}, u32[]{:S(2)}) collective-permute-start(bf16[256,640]{1,0:T(8,128)(2,1)S(1)} %constant_dynamic-update-slice_fusion.p0.g0), channel_id=1, source_target_pairs={{0,60},{1,61},{2,62},{3,63},{4,8},{5,9},{6,10},{7,11},{8,4},{9,5},... | collective-permute-start | bytes 983048 | tf_op jit(solution)/shard_map/ppermute | solution.py:415
  29.5 5.8 %collective-permute-start.6 = (bf16[256,640]{1,0:T(8,128)(2,1)S(1)}, bf16[256,640]{1,0:T(8,128)(2,1)S(1)}, u32[]{:S(2)}, u32[]{:S(2)}) collective-permute-start(bf16[256,640]{1,0:T(8,128)(2,1)S(1)} %constant_dynamic-update-slice_fusion.p0.g0), channel_id=1, source_target_pairs={{0,4},{1,5},{2,6},{3,7},{4,0},{5,1},{6,2},{7,3},{8,12},{9,13},{10,... | collective-permute-start | bytes 983048 | tf_op jit(solution)/shard_map/ppermute | solution.py:415
  38.4 9.1 %collective-permute-start.8 = (bf16[128,512]{1,0:T(8,128)(2,1)S(1)}, bf16[128,512]{1,0:T(8,128)(2,1)S(1)}, u32[]{:S(2)}, u32[]{:S(2)}) collective-permute-start(bf16[128,512]{1,0:T(8,128)(2,1)S(1)} %get-tuple-element.80), channel_id=1, source_target_pairs={{0,192},{1,193},{2,194},{3,195},{4,196},{5,197},{6,198},{7,199},{8... | collective-permute-start | bytes 393224 | tf_op jit(solution)/shard_map/ppermute | solution.py:415
  45.5 6.4 %collective-permute-start.10 = (bf16[64,512]{1,0:T(8,128)(2,1)S(1)}, bf16[64,512]{1,0:T(8,128)(2,1)S(1)}, u32[]{:S(2)}, u32[]{:S(2)}) collective-permute-start(bf16[64,512]{1,0:T(8,128)(2,1)S(1)} %get-tuple-element.82), channel_id=1, source_target_pairs={{0,195},{1,192},{2,193},{3,194},{4,199},{5,196},{6,197},{7,198},{8... | collective-permute-start | bytes 196616 | tf_op jit(solution)/shard_map/ppermute | solution.py:415
  51.9 7.0 %collective-permute-start.12 = (bf16[256,512]{1,0:T(8,128)(2,1)S(1)}, bf16[256,512]{1,0:T(8,128)(2,1)S(1)}, u32[]{:S(2)}, u32[]{:S(2)}) collective-permute-start(bf16[256,512]{1,0:T(8,128)(2,1)S(1)} %constant_dynamic-update-slice_fusion.3.g0), channel_id=1, source_target_pairs={{0,60},{1,61},{2,62},{3,63},{4,8},{5,9},{6,10},{7,11},{8,4},{9,5},... | collective-permute-start | bytes 786440 | tf_op jit(solution)/shard_map/ppermute | solution.py:415
  59.5 5.5 %collective-permute-start.13 = (bf16[128,512]{1,0:T(8,128)(2,1)S(1)}, bf16[128,512]{1,0:T(8,128)(2,1)S(1)}, u32[]{:S(2)}, u32[]{:S(2)}) collective-permute-start(bf16[128,512]{1,0:T(8,128)(2,1)S(1)} %get-tuple-element.87), channel_id=1, source_target_pairs={{0,192},{1,193},{2,194},{3,195},{4,196},{5,197},{6,198},{7,199},{8... | collective-permute-start | bytes 393224 | tf_op jit(solution)/shard_map/ppermute | solution.py:415
  60.5 6.3 %collective-permute-start.14 = (bf16[64,512]{1,0:T(8,128)(2,1)S(1)}, bf16[64,512]{1,0:T(8,128)(2,1)S(1)}, u32[]{:S(2)}, u32[]{:S(2)}) collective-permute-start(bf16[64,512]{1,0:T(8,128)(2,1)S(1)} %get-tuple-element.88), channel_id=1, source_target_pairs={{0,193},{1,194},{2,195},{3,192},{4,197},{5,198},{6,199},{7,196},{8... | collective-permute-start | bytes 196616 | tf_op jit(solution)/shard_map/ppermute | solution.py:415
  64.9 6.4 %collective-permute-start.15 = (bf16[64,512]{1,0:T(8,128)(2,1)S(1)}, bf16[64,512]{1,0:T(8,128)(2,1)S(1)}, u32[]{:S(2)}, u32[]{:S(2)}) collective-permute-start(bf16[64,512]{1,0:T(8,128)(2,1)S(1)} %get-tuple-element.89), channel_id=1, source_target_pairs={{0,195},{1,192},{2,193},{3,194},{4,199},{5,196},{6,197},{7,198},{8... | collective-permute-start | bytes 196616 | tf_op jit(solution)/shard_map/ppermute | solution.py:415
  71.3 7.0 %collective-permute-start.17 = (bf16[256,512]{1,0:T(8,128)(2,1)S(1)}, bf16[256,512]{1,0:T(8,128)(2,1)S(1)}, u32[]{:S(2)}, u32[]{:S(2)}) collective-permute-start(bf16[256,512]{1,0:T(8,128)(2,1)S(1)} %constant_dynamic-update-slice_fusion.6.g0), channel_id=1, source_target_pairs={{0,60},{1,61},{2,62},{3,63},{4,8},{5,9},{6,10},{7,11},{8,4},{9,5},... | collective-permute-start | bytes 786440 | tf_op jit(solution)/shard_map/ppermute | solution.py:415
  71.4 6.9 %collective-permute-start.16 = (bf16[256,512]{1,0:T(8,128)(2,1)S(1)}, bf16[256,512]{1,0:T(8,128)(2,1)S(1)}, u32[]{:S(2)}, u32[]{:S(2)}) collective-permute-start(bf16[256,512]{1,0:T(8,128)(2,1)S(1)} %constant_dynamic-update-slice_fusion.6.g0), channel_id=1, source_target_pairs={{0,4},{1,5},{2,6},{3,7},{4,0},{5,1},{6,2},{7,3},{8,12},{9,13},{10,... | collective-permute-start | bytes 786440 | tf_op jit(solution)/shard_map/ppermute | solution.py:415
  79.1 5.8 %collective-permute-start.18 = (bf16[128,512]{1,0:T(8,128)(2,1)S(1)}, bf16[128,512]{1,0:T(8,128)(2,1)S(1)}, u32[]{:S(2)}, u32[]{:S(2)}) collective-permute-start(bf16[128,512]{1,0:T(8,128)(2,1)S(1)} %get-tuple-element.93), channel_id=1, source_target_pairs={{0,192},{1,193},{2,194},{3,195},{4,196},{5,197},{6,198},{7,199},{8... | collective-permute-start | bytes 393224 | tf_op jit(solution)/shard_map/ppermute | solution.py:415
  80.6 6.4 %collective-permute-start.20 = (bf16[64,512]{1,0:T(8,128)(2,1)S(1)}, bf16[64,512]{1,0:T(8,128)(2,1)S(1)}, u32[]{:S(2)}, u32[]{:S(2)}) collective-permute-start(bf16[64,512]{1,0:T(8,128)(2,1)S(1)} %get-tuple-element.95), channel_id=1, source_target_pairs={{0,195},{1,192},{2,193},{3,194},{4,199},{5,196},{6,197},{7,198},{8... | collective-permute-start | bytes 196616 | tf_op jit(solution)/shard_map/ppermute | solution.py:415
  87.0 7.0 %collective-permute-start.22 = (bf16[256,512]{1,0:T(8,128)(2,1)S(1)}, bf16[256,512]{1,0:T(8,128)(2,1)S(1)}, u32[]{:S(2)}, u32[]{:S(2)}) collective-permute-start(bf16[256,512]{1,0:T(8,128)(2,1)S(1)} %constant_dynamic-update-slice_fusion.9.g0), channel_id=1, source_target_pairs={{0,60},{1,61},{2,62},{3,63},{4,8},{5,9},{6,10},{7,11},{8,4},{9,5},... | collective-permute-start | bytes 786440 | tf_op jit(solution)/shard_map/ppermute | solution.py:415
  97.9 8.8 %collective-permute-start.27 = (bf16[64,1024]{1,0:T(8,128)(2,1)S(1)}, bf16[64,1024]{1,0:T(8,128)(2,1)S(1)}, u32[]{:S(2)}, u32[]{:S(2)}) collective-permute-start(bf16[64,1024]{1,0:T(8,128)(2,1)S(1)} %get-tuple-element.106), channel_id=1, source_target_pairs={{0,2},{1,3},{2,0},{3,1},{4,6},{5,7},{6,4},{7,5},{8,10},{9,11},{10,... | collective-permute-start | bytes 393224 | tf_op jit(solution)/shard_map/ppermute | solution.py:415
  98.7 12.7 %collective-permute-start.26 = (bf16[64,1024]{1,0:T(8,128)(2,1)S(1)}, bf16[64,1024]{1,0:T(8,128)(2,1)S(1)}, u32[]{:S(2)}, u32[]{:S(2)}) collective-permute-start(bf16[64,1024]{1,0:T(8,128)(2,1)S(1)} %get-tuple-element.104), channel_id=1, source_target_pairs={{0,1},{1,2},{2,3},{3,0},{4,5},{5,6},{6,7},{7,4},{8,9},{9,10},{10,1... | collective-permute-start | bytes 393224 | tf_op jit(solution)/shard_map/ppermute | solution.py:415
  100.8 10.5 %collective-permute-start.28 = (bf16[64,1024]{1,0:T(8,128)(2,1)S(1)}, bf16[64,1024]{1,0:T(8,128)(2,1)S(1)}, u32[]{:S(2)}, u32[]{:S(2)}) collective-permute-start(bf16[64,1024]{1,0:T(8,128)(2,1)S(1)} %get-tuple-element.108), channel_id=1, source_target_pairs={{0,3},{1,0},{2,1},{3,2},{4,7},{5,4},{6,5},{7,6},{8,11},{9,8},{10,9... | collective-permute-start | bytes 393224 | tf_op jit(solution)/shard_map/ppermute | solution.py:415
  102.0 9.4 %collective-permute-start.25 = (bf16[64,1024]{1,0:T(8,128)(2,1)S(1)}, bf16[64,1024]{1,0:T(8,128)(2,1)S(1)}, u32[]{:S(2)}, u32[]{:S(2)}) collective-permute-start(bf16[64,1024]{1,0:T(8,128)(2,1)S(1)} %get-tuple-element.100), channel_id=1, source_target_pairs={{0,3},{1,0},{2,1},{3,2},{4,7},{5,4},{6,5},{7,6},{8,11},{9,8},{10,9... | collective-permute-start | bytes 393224 | tf_op jit(solution)/shard_map/ppermute | solution.py:415
  104.1 9.6 %collective-permute-start.30 = (bf16[64,1024]{1,0:T(8,128)(2,1)S(1)}, bf16[64,1024]{1,0:T(8,128)(2,1)S(1)}, u32[]{:S(2)}, u32[]{:S(2)}) collective-permute-start(bf16[64,1024]{1,0:T(8,128)(2,1)S(1)} %get-tuple-element.111), channel_id=1, source_target_pairs={{0,2},{1,3},{2,0},{3,1},{4,6},{5,7},{6,4},{7,5},{8,10},{9,11},{10,... | collective-permute-start | bytes 393224 | tf_op jit(solution)/shard_map/ppermute | solution.py:415
  106.6 7.1 %collective-permute-start.29 = (bf16[64,1024]{1,0:T(8,128)(2,1)S(1)}, bf16[64,1024]{1,0:T(8,128)(2,1)S(1)}, u32[]{:S(2)}, u32[]{:S(2)}) collective-permute-start(bf16[64,1024]{1,0:T(8,128)(2,1)S(1)} %get-tuple-element.110), channel_id=1, source_target_pairs={{0,1},{1,2},{2,3},{3,0},{4,5},{5,6},{6,7},{7,4},{8,9},{9,10},{10,1... | collective-permute-start | bytes 393224 | tf_op jit(solution)/shard_map/ppermute | solution.py:415
  (14 other events, 66.0 us)

commit v5 on v4

--- a/solution.py
+++ b/solution.py
@@ -118,19 +118,18 @@
     ok = window(where_ref, False)
     ok2 = jnp.concatenate([ok, ok], axis=0)
     lane = lax.broadcasted_iota(jnp.int32, (TOK, 128), 1)
-    stats = jnp.zeros((TOK, 128), F32)
-    for pair in range(PAIRS):
-        at = slice(128 * pair, 128 * pair + 128)
+
+    def one_pair(pair, stats):
+        low = pl.multiple_of(128 * pair, 128)
+        at = pl.ds(low, 128)
         query = two_heads(proj_ref[:, at] * 0.125)
-        scores = nt(query, kv_ref[:, at])
-        scores = jnp.where(ok2, scores, -1e30)
+        scores = jnp.where(ok2, nt(query, kv_ref[:, at]), -1e30)
         highest = jnp.max(scores, axis=-1, keepdims=True)
         grown = jnp.exp(scores - highest)
         total = jnp.sum(grown, axis=-1, keepdims=True)
         probs = (grown * (1.0 / total)).astype(BF16)
         prob_ref[pair] = probs
-        value = kv_ref[:, D + 128 * pair : D + 128 * pair + 128]
-        mixed = one_block(nn(probs, value)).astype(BF16)
+        mixed = one_block(nn(probs, kv_ref[:, pl.ds(low + D, 128)])).astype(BF16)
         mixed_ref[:, at] = mixed
         log_total = highest + jnp.log(total)
         delta = two_sums(dm_ref[:, at], mixed)
@@ -141,6 +140,9 @@
                 for head in range(2):
                     chosen = lane == first + 8 * part + 2 * pair + head
                     stats = jnp.where(chosen, piece[TOK * head : TOK * head + TOK], stats)
+        return stats
+
+    stats = lax.fori_loop(0, PAIRS, one_pair, jnp.zeros((TOK, 128), F32), unroll=2)
     starts = where_ref[5] == 0
     pack_ref[:, D:] = stats.astype(BF16)
 
@@ -242,7 +244,7 @@
             dq_ref[:, at] = (one_block(nn(slopes, kv_ref[:, at])) * 0.125).astype(BF16)
             return carry
 
-        lax.fori_loop(0, PAIRS, one_pair, 0)
+        lax.fori_loop(0, PAIRS, one_pair, 0, unroll=2)
 
 
 def turned_block(stacked):

time: 136 us -> 136 us (level)
  transfers between devices with their start and end apart: 31 -> 31, of which waited for: 16 -> 16; matrix products, arithmetic and copies ran while one was open for 0% -> 0% of each run, Pallas kernels for 11% -> 10%
where the time goes in v5:
time: 136 us; the launch traced here: 134 us
  waiting for transfers between devices  45 us (33%)
  starting transfers between devices  40.7 us (30%)
  Pallas kernels  24.6 us (18%)
  blocking collectives  18.2 us (13%)
  local copies, waits for them, and re-layouts  4.5 us (3%)
    ppermute x31, waiting for transfers between devices, routed(): return lax.ppermute(block, AXES, pairs)  45 us
    ppermute x31, starting transfers between devices, routed(): return lax.ppermute(block, AXES, pairs)  40.7 us
    pallas_call x18, Pallas kernels, call(): pl.pallas_call(kernel, out_shape=[jax.ShapeDtypeStruct(s, t) for s, t in...  24.6 us
    all_to_all x1, blocking collectives, body(): part = lax.all_to_all(part, 'z', 0, 0, tiled=True)  18.2 us
    unnamed x22, local copies, waits for them, and re-layouts  3.44 us
  transfers between devices with their start and end apart: 31, of which 16 were waited for; matrix products, arithmetic and copies ran while one was open for 0% of the time, Pallas kernels for 10%

profile of v5, /device:TPU:6, one launch (start us, length us, event | category | flops | bytes accessed | tf_op | source)
XLA Modules:
  0.0 134.0 jit_solution(13634219521454875109)
XLA Ops:
  1.6 2.3 %collective-permute-start = (bf16[64,512]{1,0:T(8,128)(2,1)S(1)}, bf16[64,512]{1,0:T(8,128)(2,1)S(1)}, u32[]{:S(2)}, u32[]{:S(2)}) collective-permute-start(bf16[64,512]{1,0:T(8,128)(2,1)S(1)} %get-tuple-element.116), channel_id=1, source_target_pairs={{0,1},{1,2},{2,3},{3,0},{4,5},{5,6},{6,7},{7,4},{8,9},{9,10},{10,1... | collective-permute-start | bytes 196616 | tf_op jit(solution)/shard_map/ppermute | solution.py:417
  7.3 2.1 %collective-permute-done.1.right_ref = bf16[64,512]{1,0:T(8,128)(2,1)S(1)} collective-permute-done((bf16[64,512]{1,0:T(8,128)(2,1)S(1)}, bf16[64,512]{1,0:T(8,128)(2,1)S(1)}, u32[]{:S(2)}, u32[]{:S(2)}) %collective-permute-start.1) | collective-permute-done | bytes 65568 | tf_op jit(solution)/shard_map/ppermute | solution.py:417
  9.3 2.6 %collective-permute-start.3 = (bf16[256,512]{1,0:T(8,128)(2,1)S(1)}, bf16[256,512]{1,0:T(8,128)(2,1)S(1)}, u32[]{:S(2)}, u32[]{:S(2)}) collective-permute-start(bf16[256,512]{1,0:T(8,128)(2,1)S(1)} %constant_dynamic-update-slice_fusion.12), channel_id=1, source_target_pairs={{0,60},{1,61},{2,62},{3,63},{4,8},{5,9},{6,10},{7,11},{8,4},{9,5},... | collective-permute-start | bytes 786440 | tf_op jit(solution)/shard_map/ppermute | solution.py:417
  14.1 2.2 %collective-permute-done.3.x2 = bf16[256,512]{1,0:T(8,128)(2,1)S(1)} collective-permute-done((bf16[256,512]{1,0:T(8,128)(2,1)S(1)}, bf16[256,512]{1,0:T(8,128)(2,1)S(1)}, u32[]{:S(2)}, u32[]{:S(2)}) %collective-permute-start.3) | collective-permute-done | bytes 262176 | tf_op jit(solution)/shard_map/ppermute | solution.py:417
  16.4 4.7 %shard_map.69 = (bf16[768,1024]{1,0:T(8,128)(2,1)S(1)}, bf16[4,256,768]{2,1,0:T(8,128)(2,1)S(1)}, bf16[128,512]{1,0:T(8,128)(2,1)S(1)}, bf16[512,512]{1,0:T(8,12...) custom-call(s32[7]{0:T(128)S(1)} %stack.23.where_ref, ...), custom_call_target="tpu_custom_call" | custom-call | flops 2147483648 | bytes 4194304 | tf_op jit(solution)/shard_map/pallas_call | solution.py:395
  24.9 3.2 %collective-permute-done.5 = bf16[64,640]{1,0:T(8,128)(2,1)S(1)} collective-permute-done((bf16[64,640]{1,0:T(8,128)(2,1)S(1)}, bf16[64,640]{1,0:T(8,128)(2,1)S(1)}, u32[]{:S(2)}, u32[]{:S(2)}) %collective-permute-start.5) | collective-permute-done | bytes 81952 | tf_op jit(solution)/shard_map/ppermute | solution.py:417
  28.2 2.0 %collective-permute-start.7 = (bf16[256,640]{1,0:T(8,128)(2,1)S(1)}, bf16[256,640]{1,0:T(8,128)(2,1)S(1)}, u32[]{:S(2)}, u32[]{:S(2)}) collective-permute-start(bf16[256,640]{1,0:T(8,128)(2,1)S(1)} %constant_dynamic-update-slice_fusion.p0.g0), channel_id=1, source_target_pairs={{0,60},{1,61},{2,62},{3,63},{4,8},{5,9},{6,10},{7,11},{8,4},{9,5},... | collective-permute-start | bytes 983048 | tf_op jit(solution)/shard_map/ppermute | solution.py:417
  30.2 5.8 %collective-permute-done.7.p2.g2 = bf16[256,640]{1,0:T(8,128)(2,1)S(1)} collective-permute-done((bf16[256,640]{1,0:T(8,128)(2,1)S(1)}, bf16[256,640]{1,0:T(8,128)(2,1)S(1)}, u32[]{:S(2)}, u32[]{:S(2)}) %collective-permute-start.7) | collective-permute-done | bytes 327712 | tf_op jit(solution)/shard_map/ppermute | solution.py:417
  36.0 2.4 %shard_map.72 = (bf16[4,256,768]{2,1,0:T(8,128)(2,1)S(1)}, bf16[512,768]{1,0:T(8,128)(2,1)S(1)}, f32[8,768]{1,0:T(8,128)S(1)}) custom-call(s32[7]{0:T(128)S(1)} %stack.23.where_ref, bf16[256,640]{1,0:T(8,128)(2,1)S(1)} %constant_dynamic-update-slice_fusion.p0.g0, bf16[256,640]{1,0:T(8,128)(2,1)S(1)} %collective-permute-done.6.p1.g1, ...), custom_call_target="tpu_custom_call" | custom-call | flops 268435456 | bytes 4194304 | tf_op jit(solution)/shard_map/pallas_call | solution.py:395
  38.9 6.1 %collective-permute-start.8 = (bf16[128,512]{1,0:T(8,128)(2,1)S(1)}, bf16[128,512]{1,0:T(8,128)(2,1)S(1)}, u32[]{:S(2)}, u32[]{:S(2)}) collective-permute-start(bf16[128,512]{1,0:T(8,128)(2,1)S(1)} %get-tuple-element.80), channel_id=1, source_target_pairs={{0,192},{1,193},{2,194},{3,195},{4,196},{5,197},{6,198},{7,199},{8... | collective-permute-start | bytes 393224 | tf_op jit(solution)/shard_map/ppermute | solution.py:417
  45.7 2.6 %collective-permute-done.8.g_ref.rest_1_ = bf16[128,512]{1,0:T(8,128)(2,1)S(1)} collective-permute-done((bf16[128,512]{1,0:T(8,128)(2,1)S(1)}, bf16[128,512]{1,0:T(8,128)(2,1)S(1)}, u32[]{:S(2)}, u32[]{:S(2)}) %collective-permute-start.8) | collective-permute-done | bytes 131104 | tf_op jit(solution)/shard_map/ppermute | solution.py:417
  54.4 4.6 %collective-permute-done.12.g2 = bf16[256,512]{1,0:T(8,128)(2,1)S(1)} collective-permute-done((bf16[256,512]{1,0:T(8,128)(2,1)S(1)}, bf16[256,512]{1,0:T(8,128)(2,1)S(1)}, u32[]{:S(2)}, u32[]{:S(2)}) %collective-permute-start.12) | collective-permute-done | bytes 262176 | tf_op jit(solution)/shard_map/ppermute | solution.py:417
  61.2 3.9 %collective-permute-start.14 = (bf16[64,512]{1,0:T(8,128)(2,1)S(1)}, bf16[64,512]{1,0:T(8,128)(2,1)S(1)}, u32[]{:S(2)}, u32[]{:S(2)}) collective-permute-start(bf16[64,512]{1,0:T(8,128)(2,1)S(1)} %get-tuple-element.88), channel_id=1, source_target_pairs={{0,193},{1,194},{2,195},{3,192},{4,197},{5,198},{6,199},{7,196},{8... | collective-permute-start | bytes 196616 | tf_op jit(solution)/shard_map/ppermute | solution.py:417
  67.0 4.5 %collective-permute-done.15 = bf16[64,512]{1,0:T(8,128)(2,1)S(1)} collective-permute-done((bf16[64,512]{1,0:T(8,128)(2,1)S(1)}, bf16[64,512]{1,0:T(8,128)(2,1)S(1)}, u32[]{:S(2)}, u32[]{:S(2)}) %collective-permute-start.15) | collective-permute-done | bytes 65568 | tf_op jit(solution)/shard_map/ppermute | solution.py:417
  72.1 6.3 %collective-permute-done.17.g2 = bf16[256,512]{1,0:T(8,128)(2,1)S(1)} collective-permute-done((bf16[256,512]{1,0:T(8,128)(2,1)S(1)}, bf16[256,512]{1,0:T(8,128)(2,1)S(1)}, u32[]{:S(2)}, u32[]{:S(2)}) %collective-permute-start.17) | collective-permute-done | bytes 262176 | tf_op jit(solution)/shard_map/ppermute | solution.py:417
  80.8 4.0 %collective-permute-start.20 = (bf16[64,512]{1,0:T(8,128)(2,1)S(1)}, bf16[64,512]{1,0:T(8,128)(2,1)S(1)}, u32[]{:S(2)}, u32[]{:S(2)}) collective-permute-start(bf16[64,512]{1,0:T(8,128)(2,1)S(1)} %get-tuple-element.95), channel_id=1, source_target_pairs={{0,195},{1,192},{2,193},{3,194},{4,199},{5,196},{6,197},{7,198},{8... | collective-permute-start | bytes 196616 | tf_op jit(solution)/shard_map/ppermute | solution.py:417
  87.2 2.1 %collective-permute-start.22 = (bf16[256,512]{1,0:T(8,128)(2,1)S(1)}, bf16[256,512]{1,0:T(8,128)(2,1)S(1)}, u32[]{:S(2)}, u32[]{:S(2)}) collective-permute-start(bf16[256,512]{1,0:T(8,128)(2,1)S(1)} %constant_dynamic-update-slice_fusion.9.g0), channel_id=1, source_target_pairs={{0,60},{1,61},{2,62},{3,63},{4,8},{5,9},{6,10},{7,11},{8,4},{9,5},... | collective-permute-start | bytes 786440 | tf_op jit(solution)/shard_map/ppermute | solution.py:417
  89.3 2.4 %shard_map.79.dq_ref = bf16[128,512]{1,0:T(8,128)(2,1)S(1)} custom-call(s32[7]{0:T(128)S(1)} %stack.23.where_ref, bf16[128,512]{1,0:T(8,128)(2,1)S(1)} %collective-permute-done.18.g_ref, bf16[512,512]{1,0:T(8,128)(2,1)S(1)} %bitcast.37, bf16[128,512]{1,0:T(8,128)(2,1)S(1)} %get-tuple-element.72.mixed_ref, bf16[768,1024]{1,0:T(8,128)(2,1)S(1)} %get-tuple-element.73.kv_ref, ...), custom_call_target="tpu_custom_call" | custom-call | flops 536870912 | bytes 4194304 | tf_op jit(solution)/shard_map/pallas_call | solution.py:395
  94.2 2.7 %shard_map.78.d0.kv_ref = bf16[128,1024]{1,0:T(8,128)(2,1)S(1)} custom-call(s32[7]{0:T(128)S(1)} %stack.23.where_ref, bf16[256,512]{1,0:T(8,128)(2,1)S(1)} %constant_dynamic-update-slice_fusion.9.g0, bf16[256,512]{1,0:T(8,128)(2,1)S(1)} %collective-permute-done.21.g1, bf16[256,512]{1,0:T(8,128)(2,1)S(1)} %collective-permute-done.22.g2, ...), custom_call_target="tpu_custom_call" | custom-call | flops 1073741824 | bytes 4194304 | tf_op jit(solution)/shard_map/pallas_call | solution.py:395
  98.7 2.4 %collective-permute-start.26 = (bf16[64,1024]{1,0:T(8,128)(2,1)S(1)}, bf16[64,1024]{1,0:T(8,128)(2,1)S(1)}, u32[]{:S(2)}, u32[]{:S(2)}) collective-permute-start(bf16[64,1024]{1,0:T(8,128)(2,1)S(1)} %get-tuple-element.104), channel_id=1, source_target_pairs={{0,1},{1,2},{2,3},{3,0},{4,5},{5,6},{6,7},{7,4},{8,9},{9,10},{10,1... | collective-permute-start | bytes 393224 | tf_op jit(solution)/shard_map/ppermute | solution.py:417
  102.0 2.0 %collective-permute-start.25 = (bf16[64,1024]{1,0:T(8,128)(2,1)S(1)}, bf16[64,1024]{1,0:T(8,128)(2,1)S(1)}, u32[]{:S(2)}, u32[]{:S(2)}) collective-permute-start(bf16[64,1024]{1,0:T(8,128)(2,1)S(1)} %get-tuple-element.100), channel_id=1, source_target_pairs={{0,3},{1,0},{2,1},{3,2},{4,7},{5,4},{6,5},{7,6},{8,11},{9,8},{10,9... | collective-permute-start | bytes 393224 | tf_op jit(solution)/shard_map/ppermute | solution.py:417
  104.1 2.7 %collective-permute-start.30 = (bf16[64,1024]{1,0:T(8,128)(2,1)S(1)}, bf16[64,1024]{1,0:T(8,128)(2,1)S(1)}, u32[]{:S(2)}, u32[]{:S(2)}) collective-permute-start(bf16[64,1024]{1,0:T(8,128)(2,1)S(1)} %get-tuple-element.111), channel_id=1, source_target_pairs={{0,2},{1,3},{2,0},{3,1},{4,6},{5,7},{6,4},{7,5},{8,10},{9,11},{10,... | collective-permute-start | bytes 393224 | tf_op jit(solution)/shard_map/ppermute | solution.py:417
  111.6 2.4 %collective-permute-done.30.refs_6_ = bf16[64,1024]{1,0:T(8,128)(2,1)S(1)} collective-permute-done((bf16[64,1024]{1,0:T(8,128)(2,1)S(1)}, bf16[64,1024]{1,0:T(8,128)(2,1)S(1)}, u32[]{:S(2)}, u32[]{:S(2)}) %collective-permute-start.30) | collective-permute-done | bytes 131104 | tf_op jit(solution)/shard_map/ppermute | solution.py:417
  114.6 18.2 %all_to_all.5.part_ref = bf16[8,8,2048]{2,1,0:T(8,128)(2,1)S(1)} all-to-all(bf16[8,8,2048]{2,1,0:T(8,128)(2,1)S(1)} %bitcast.45), channel_id=1, replica_groups=mesh['pipe'=4,'z'=8,'core'=2,'col'=4] {'z'}, dimensions={0} | all-to-all | bytes 524288 | tf_op jit(solution)/shard_map/all_to_all | solution.py:540
  (88 shorter events, 38.9 us)
Async XLA Ops:
  1.6 5.7 %collective-permute-start = (bf16[64,512]{1,0:T(8,128)(2,1)S(1)}, bf16[64,512]{1,0:T(8,128)(2,1)S(1)}, u32[]{:S(2)}, u32[]{:S(2)}) collective-permute-start(bf16[64,512]{1,0:T(8,128)(2,1)S(1)} %get-tuple-element.116), channel_id=1, source_target_pairs={{0,1},{1,2},{2,3},{3,0},{4,5},{5,6},{6,7},{7,4},{8,9},{9,10},{10,1... | collective-permute-start | bytes 196616 | tf_op jit(solution)/shard_map/ppermute | solution.py:417
  3.9 5.5 %collective-permute-start.1 = (bf16[64,512]{1,0:T(8,128)(2,1)S(1)}, bf16[64,512]{1,0:T(8,128)(2,1)S(1)}, u32[]{:S(2)}, u32[]{:S(2)}) collective-permute-start(bf16[64,512]{1,0:T(8,128)(2,1)S(1)} %get-tuple-element.115), channel_id=1, source_target_pairs={{0,3},{1,0},{2,1},{3,2},{4,7},{5,4},{6,5},{7,6},{8,11},{9,8},{10,9... | collective-permute-start | bytes 196616 | tf_op jit(solution)/shard_map/ppermute | solution.py:417
  9.3 7.0 %collective-permute-start.3 = (bf16[256,512]{1,0:T(8,128)(2,1)S(1)}, bf16[256,512]{1,0:T(8,128)(2,1)S(1)}, u32[]{:S(2)}, u32[]{:S(2)}) collective-permute-start(bf16[256,512]{1,0:T(8,128)(2,1)S(1)} %constant_dynamic-update-slice_fusion.12), channel_id=1, source_target_pairs={{0,60},{1,61},{2,62},{3,63},{4,8},{5,9},{6,10},{7,11},{8,4},{9,5},... | collective-permute-start | bytes 786440 | tf_op jit(solution)/shard_map/ppermute | solution.py:417
  21.1 7.1 %collective-permute-start.4 = (bf16[64,640]{1,0:T(8,128)(2,1)S(1)}, bf16[64,640]{1,0:T(8,128)(2,1)S(1)}, u32[]{:S(2)}, u32[]{:S(2)}) collective-permute-start(bf16[64,640]{1,0:T(8,128)(2,1)S(1)} %get-tuple-element.69), channel_id=1, source_target_pairs={{0,1},{1,2},{2,3},{3,0},{4,5},{5,6},{6,7},{7,4},{8,9},{9,10},{10,1... | collective-permute-start | bytes 245768 | tf_op jit(solution)/shard_map/ppermute | solution.py:417
  22.5 5.7 %collective-permute-start.5 = (bf16[64,640]{1,0:T(8,128)(2,1)S(1)}, bf16[64,640]{1,0:T(8,128)(2,1)S(1)}, u32[]{:S(2)}, u32[]{:S(2)}) collective-permute-start(bf16[64,640]{1,0:T(8,128)(2,1)S(1)} %get-tuple-element.70), channel_id=1, source_target_pairs={{0,3},{1,0},{2,1},{3,2},{4,7},{5,4},{6,5},{7,6},{8,11},{9,8},{10,9... | collective-permute-start | bytes 245768 | tf_op jit(solution)/shard_map/ppermute | solution.py:417
  28.2 7.8 %collective-permute-start.7 = (bf16[256,640]{1,0:T(8,128)(2,1)S(1)}, bf16[256,640]{1,0:T(8,128)(2,1)S(1)}, u32[]{:S(2)}, u32[]{:S(2)}) collective-permute-start(bf16[256,640]{1,0:T(8,128)(2,1)S(1)} %constant_dynamic-update-slice_fusion.p0.g0), channel_id=1, source_target_pairs={{0,60},{1,61},{2,62},{3,63},{4,8},{5,9},{6,10},{7,11},{8,4},{9,5},... | collective-permute-start | bytes 983048 | tf_op jit(solution)/shard_map/ppermute | solution.py:417
  30.2 5.8 %collective-permute-start.6 = (bf16[256,640]{1,0:T(8,128)(2,1)S(1)}, bf16[256,640]{1,0:T(8,128)(2,1)S(1)}, u32[]{:S(2)}, u32[]{:S(2)}) collective-permute-start(bf16[256,640]{1,0:T(8,128)(2,1)S(1)} %constant_dynamic-update-slice_fusion.p0.g0), channel_id=1, source_target_pairs={{0,4},{1,5},{2,6},{3,7},{4,0},{5,1},{6,2},{7,3},{8,12},{9,13},{10,... | collective-permute-start | bytes 983048 | tf_op jit(solution)/shard_map/ppermute | solution.py:417
  38.9 9.3 %collective-permute-start.8 = (bf16[128,512]{1,0:T(8,128)(2,1)S(1)}, bf16[128,512]{1,0:T(8,128)(2,1)S(1)}, u32[]{:S(2)}, u32[]{:S(2)}) collective-permute-start(bf16[128,512]{1,0:T(8,128)(2,1)S(1)} %get-tuple-element.80), channel_id=1, source_target_pairs={{0,192},{1,193},{2,194},{3,195},{4,196},{5,197},{6,198},{7,199},{8... | collective-permute-start | bytes 393224 | tf_op jit(solution)/shard_map/ppermute | solution.py:417
  45.7 6.4 %collective-permute-start.10 = (bf16[64,512]{1,0:T(8,128)(2,1)S(1)}, bf16[64,512]{1,0:T(8,128)(2,1)S(1)}, u32[]{:S(2)}, u32[]{:S(2)}) collective-permute-start(bf16[64,512]{1,0:T(8,128)(2,1)S(1)} %get-tuple-element.82), channel_id=1, source_target_pairs={{0,195},{1,192},{2,193},{3,194},{4,199},{5,196},{6,197},{7,198},{8... | collective-permute-start | bytes 196616 | tf_op jit(solution)/shard_map/ppermute | solution.py:417
  52.0 7.0 %collective-permute-start.12 = (bf16[256,512]{1,0:T(8,128)(2,1)S(1)}, bf16[256,512]{1,0:T(8,128)(2,1)S(1)}, u32[]{:S(2)}, u32[]{:S(2)}) collective-permute-start(bf16[256,512]{1,0:T(8,128)(2,1)S(1)} %constant_dynamic-update-slice_fusion.3.g0), channel_id=1, source_target_pairs={{0,60},{1,61},{2,62},{3,63},{4,8},{5,9},{6,10},{7,11},{8,4},{9,5},... | collective-permute-start | bytes 786440 | tf_op jit(solution)/shard_map/ppermute | solution.py:417
  59.7 5.5 %collective-permute-start.13 = (bf16[128,512]{1,0:T(8,128)(2,1)S(1)}, bf16[128,512]{1,0:T(8,128)(2,1)S(1)}, u32[]{:S(2)}, u32[]{:S(2)}) collective-permute-start(bf16[128,512]{1,0:T(8,128)(2,1)S(1)} %get-tuple-element.87), channel_id=1, source_target_pairs={{0,192},{1,193},{2,194},{3,195},{4,196},{5,197},{6,198},{7,199},{8... | collective-permute-start | bytes 393224 | tf_op jit(solution)/shard_map/ppermute | solution.py:417
  61.2 5.8 %collective-permute-start.14 = (bf16[64,512]{1,0:T(8,128)(2,1)S(1)}, bf16[64,512]{1,0:T(8,128)(2,1)S(1)}, u32[]{:S(2)}, u32[]{:S(2)}) collective-permute-start(bf16[64,512]{1,0:T(8,128)(2,1)S(1)} %get-tuple-element.88), channel_id=1, source_target_pairs={{0,193},{1,194},{2,195},{3,192},{4,197},{5,198},{6,199},{7,196},{8... | collective-permute-start | bytes 196616 | tf_op jit(solution)/shard_map/ppermute | solution.py:417
  65.1 6.4 %collective-permute-start.15 = (bf16[64,512]{1,0:T(8,128)(2,1)S(1)}, bf16[64,512]{1,0:T(8,128)(2,1)S(1)}, u32[]{:S(2)}, u32[]{:S(2)}) collective-permute-start(bf16[64,512]{1,0:T(8,128)(2,1)S(1)} %get-tuple-element.89), channel_id=1, source_target_pairs={{0,195},{1,192},{2,193},{3,194},{4,199},{5,196},{6,197},{7,198},{8... | collective-permute-start | bytes 196616 | tf_op jit(solution)/shard_map/ppermute | solution.py:417
  71.5 7.0 %collective-permute-start.17 = (bf16[256,512]{1,0:T(8,128)(2,1)S(1)}, bf16[256,512]{1,0:T(8,128)(2,1)S(1)}, u32[]{:S(2)}, u32[]{:S(2)}) collective-permute-start(bf16[256,512]{1,0:T(8,128)(2,1)S(1)} %constant_dynamic-update-slice_fusion.6.g0), channel_id=1, source_target_pairs={{0,60},{1,61},{2,62},{3,63},{4,8},{5,9},{6,10},{7,11},{8,4},{9,5},... | collective-permute-start | bytes 786440 | tf_op jit(solution)/shard_map/ppermute | solution.py:417
  71.6 6.9 %collective-permute-start.16 = (bf16[256,512]{1,0:T(8,128)(2,1)S(1)}, bf16[256,512]{1,0:T(8,128)(2,1)S(1)}, u32[]{:S(2)}, u32[]{:S(2)}) collective-permute-start(bf16[256,512]{1,0:T(8,128)(2,1)S(1)} %constant_dynamic-update-slice_fusion.6.g0), channel_id=1, source_target_pairs={{0,4},{1,5},{2,6},{3,7},{4,0},{5,1},{6,2},{7,3},{8,12},{9,13},{10,... | collective-permute-start | bytes 786440 | tf_op jit(solution)/shard_map/ppermute | solution.py:417
  79.1 5.7 %collective-permute-start.18 = (bf16[128,512]{1,0:T(8,128)(2,1)S(1)}, bf16[128,512]{1,0:T(8,128)(2,1)S(1)}, u32[]{:S(2)}, u32[]{:S(2)}) collective-permute-start(bf16[128,512]{1,0:T(8,128)(2,1)S(1)} %get-tuple-element.93), channel_id=1, source_target_pairs={{0,192},{1,193},{2,194},{3,195},{4,196},{5,197},{6,198},{7,199},{8... | collective-permute-start | bytes 393224 | tf_op jit(solution)/shard_map/ppermute | solution.py:417
  80.8 6.4 %collective-permute-start.20 = (bf16[64,512]{1,0:T(8,128)(2,1)S(1)}, bf16[64,512]{1,0:T(8,128)(2,1)S(1)}, u32[]{:S(2)}, u32[]{:S(2)}) collective-permute-start(bf16[64,512]{1,0:T(8,128)(2,1)S(1)} %get-tuple-element.95), channel_id=1, source_target_pairs={{0,195},{1,192},{2,193},{3,194},{4,199},{5,196},{6,197},{7,198},{8... | collective-permute-start | bytes 196616 | tf_op jit(solution)/shard_map/ppermute | solution.py:417
  87.2 7.0 %collective-permute-start.22 = (bf16[256,512]{1,0:T(8,128)(2,1)S(1)}, bf16[256,512]{1,0:T(8,128)(2,1)S(1)}, u32[]{:S(2)}, u32[]{:S(2)}) collective-permute-start(bf16[256,512]{1,0:T(8,128)(2,1)S(1)} %constant_dynamic-update-slice_fusion.9.g0), channel_id=1, source_target_pairs={{0,60},{1,61},{2,62},{3,63},{4,8},{5,9},{6,10},{7,11},{8,4},{9,5},... | collective-permute-start | bytes 786440 | tf_op jit(solution)/shard_map/ppermute | solution.py:417
  98.0 8.8 %collective-permute-start.27 = (bf16[64,1024]{1,0:T(8,128)(2,1)S(1)}, bf16[64,1024]{1,0:T(8,128)(2,1)S(1)}, u32[]{:S(2)}, u32[]{:S(2)}) collective-permute-start(bf16[64,1024]{1,0:T(8,128)(2,1)S(1)} %get-tuple-element.106), channel_id=1, source_target_pairs={{0,2},{1,3},{2,0},{3,1},{4,6},{5,7},{6,4},{7,5},{8,10},{9,11},{10,... | collective-permute-start | bytes 393224 | tf_op jit(solution)/shard_map/ppermute | solution.py:417
  98.7 12.9 %collective-permute-start.26 = (bf16[64,1024]{1,0:T(8,128)(2,1)S(1)}, bf16[64,1024]{1,0:T(8,128)(2,1)S(1)}, u32[]{:S(2)}, u32[]{:S(2)}) collective-permute-start(bf16[64,1024]{1,0:T(8,128)(2,1)S(1)} %get-tuple-element.104), channel_id=1, source_target_pairs={{0,1},{1,2},{2,3},{3,0},{4,5},{5,6},{6,7},{7,4},{8,9},{9,10},{10,1... | collective-permute-start | bytes 393224 | tf_op jit(solution)/shard_map/ppermute | solution.py:417
  101.0 10.5 %collective-permute-start.28 = (bf16[64,1024]{1,0:T(8,128)(2,1)S(1)}, bf16[64,1024]{1,0:T(8,128)(2,1)S(1)}, u32[]{:S(2)}, u32[]{:S(2)}) collective-permute-start(bf16[64,1024]{1,0:T(8,128)(2,1)S(1)} %get-tuple-element.108), channel_id=1, source_target_pairs={{0,3},{1,0},{2,1},{3,2},{4,7},{5,4},{6,5},{7,6},{8,11},{9,8},{10,9... | collective-permute-start | bytes 393224 | tf_op jit(solution)/shard_map/ppermute | solution.py:417
  102.0 9.5 %collective-permute-start.25 = (bf16[64,1024]{1,0:T(8,128)(2,1)S(1)}, bf16[64,1024]{1,0:T(8,128)(2,1)S(1)}, u32[]{:S(2)}, u32[]{:S(2)}) collective-permute-start(bf16[64,1024]{1,0:T(8,128)(2,1)S(1)} %get-tuple-element.100), channel_id=1, source_target_pairs={{0,3},{1,0},{2,1},{3,2},{4,7},{5,4},{6,5},{7,6},{8,11},{9,8},{10,9... | collective-permute-start | bytes 393224 | tf_op jit(solution)/shard_map/ppermute | solution.py:417
  104.1 9.9 %collective-permute-start.30 = (bf16[64,1024]{1,0:T(8,128)(2,1)S(1)}, bf16[64,1024]{1,0:T(8,128)(2,1)S(1)}, u32[]{:S(2)}, u32[]{:S(2)}) collective-permute-start(bf16[64,1024]{1,0:T(8,128)(2,1)S(1)} %get-tuple-element.111), channel_id=1, source_target_pairs={{0,2},{1,3},{2,0},{3,1},{4,6},{5,7},{6,4},{7,5},{8,10},{9,11},{10,... | collective-permute-start | bytes 393224 | tf_op jit(solution)/shard_map/ppermute | solution.py:417
  106.8 7.1 %collective-permute-start.29 = (bf16[64,1024]{1,0:T(8,128)(2,1)S(1)}, bf16[64,1024]{1,0:T(8,128)(2,1)S(1)}, u32[]{:S(2)}, u32[]{:S(2)}) collective-permute-start(bf16[64,1024]{1,0:T(8,128)(2,1)S(1)} %get-tuple-element.110), channel_id=1, source_target_pairs={{0,1},{1,2},{2,3},{3,0},{4,5},{5,6},{6,7},{7,4},{8,9},{9,10},{10,1... | collective-permute-start | bytes 393224 | tf_op jit(solution)/shard_map/ppermute | solution.py:417
  (14 other events, 66.6 us)

commit v6 on v4

--- a/solution.py
+++ b/solution.py
@@ -242,7 +242,7 @@
             dq_ref[:, at] = (one_block(nn(slopes, kv_ref[:, at])) * 0.125).astype(BF16)
             return carry
 
-        lax.fori_loop(0, PAIRS, one_pair, 0)
+        lax.fori_loop(0, PAIRS, one_pair, 0, unroll=2 if turn else 1)
 
 
 def turned_block(stacked):
@@ -297,7 +297,7 @@
             kv_ref[:, pl.ds(low + D, 128)] = turned_block(d_value).astype(BF16)
             return carry
 
-        lax.fori_loop(0, PAIRS, one_pair, 0, unroll=4 if last else 2)
+        lax.fori_loop(0, PAIRS, one_pair, 0, unroll=2)
         if not last:
             dq_ref, *ins_rest = ins
             outs[0][:, :D] = dq_ref[...]

time: 136 us -> 136 us (level)
  no operation moved by 1% of the time
where the time goes in v6:
time: 136 us; the launch traced here: 134 us
  waiting for transfers between devices  44.3 us (33%)
  starting transfers between devices  41.5 us (31%)
  Pallas kernels  24.7 us (18%)
  blocking collectives  18.2 us (13%)
  local copies, waits for them, and re-layouts  4.5 us (3%)
    ppermute x31, waiting for transfers between devices, routed(): return lax.ppermute(block, AXES, pairs)  44.3 us
    ppermute x31, starting transfers between devices, routed(): return lax.ppermute(block, AXES, pairs)  41.5 us
    pallas_call x18, Pallas kernels, call(): pl.pallas_call(kernel, out_shape=[jax.ShapeDtypeStruct(s, t) for s, t in...  24.7 us
    all_to_all x1, blocking collectives, body(): part = lax.all_to_all(part, 'z', 0, 0, tiled=True)  18.2 us
    unnamed x22, local copies, waits for them, and re-layouts  3.44 us
  transfers between devices with their start and end apart: 31, of which 16 were waited for; matrix products, arithmetic and copies ran while one was open for 0% of the time, Pallas kernels for 11%

profile of v6, /device:TPU:6, one launch (start us, length us, event | category | flops | bytes accessed | tf_op | source)
XLA Modules:
  0.0 134.2 jit_solution(6543191955213475642)
XLA Ops:
  1.6 2.3 %collective-permute-start = (bf16[64,512]{1,0:T(8,128)(2,1)S(1)}, bf16[64,512]{1,0:T(8,128)(2,1)S(1)}, u32[]{:S(2)}, u32[]{:S(2)}) collective-permute-start(bf16[64,512]{1,0:T(8,128)(2,1)S(1)} %get-tuple-element.116), channel_id=1, source_target_pairs={{0,1},{1,2},{2,3},{3,0},{4,5},{5,6},{6,7},{7,4},{8,9},{9,10},{10,1... | collective-permute-start | bytes 196616 | tf_op jit(solution)/shard_map/ppermute | solution.py:415
  7.3 2.1 %collective-permute-done.1.right_ref = bf16[64,512]{1,0:T(8,128)(2,1)S(1)} collective-permute-done((bf16[64,512]{1,0:T(8,128)(2,1)S(1)}, bf16[64,512]{1,0:T(8,128)(2,1)S(1)}, u32[]{:S(2)}, u32[]{:S(2)}) %collective-permute-start.1) | collective-permute-done | bytes 65568 | tf_op jit(solution)/shard_map/ppermute | solution.py:415
  9.3 2.6 %collective-permute-start.3 = (bf16[256,512]{1,0:T(8,128)(2,1)S(1)}, bf16[256,512]{1,0:T(8,128)(2,1)S(1)}, u32[]{:S(2)}, u32[]{:S(2)}) collective-permute-start(bf16[256,512]{1,0:T(8,128)(2,1)S(1)} %constant_dynamic-update-slice_fusion.12), channel_id=1, source_target_pairs={{0,60},{1,61},{2,62},{3,63},{4,8},{5,9},{6,10},{7,11},{8,4},{9,5},... | collective-permute-start | bytes 786440 | tf_op jit(solution)/shard_map/ppermute | solution.py:415
  14.1 2.2 %collective-permute-done.3.x2 = bf16[256,512]{1,0:T(8,128)(2,1)S(1)} collective-permute-done((bf16[256,512]{1,0:T(8,128)(2,1)S(1)}, bf16[256,512]{1,0:T(8,128)(2,1)S(1)}, u32[]{:S(2)}, u32[]{:S(2)}) %collective-permute-start.3) | collective-permute-done | bytes 262176 | tf_op jit(solution)/shard_map/ppermute | solution.py:415
  16.4 4.0 %shard_map.69 = (bf16[768,1024]{1,0:T(8,128)(2,1)S(1)}, bf16[4,256,768]{2,1,0:T(8,128)(2,1)S(1)}, bf16[128,512]{1,0:T(8,128)(2,1)S(1)}, bf16[512,512]{1,0:T(8,12...) custom-call(s32[7]{0:T(128)S(1)} %stack.23.where_ref, ...), custom_call_target="tpu_custom_call" | custom-call | flops 2147483648 | bytes 4194304 | tf_op jit(solution)/shard_map/pallas_call | solution.py:393
  24.2 3.3 %collective-permute-done.5 = bf16[64,640]{1,0:T(8,128)(2,1)S(1)} collective-permute-done((bf16[64,640]{1,0:T(8,128)(2,1)S(1)}, bf16[64,640]{1,0:T(8,128)(2,1)S(1)}, u32[]{:S(2)}, u32[]{:S(2)}) %collective-permute-start.5) | collective-permute-done | bytes 81952 | tf_op jit(solution)/shard_map/ppermute | solution.py:415
  29.5 5.8 %collective-permute-done.7.p2.g2 = bf16[256,640]{1,0:T(8,128)(2,1)S(1)} collective-permute-done((bf16[256,640]{1,0:T(8,128)(2,1)S(1)}, bf16[256,640]{1,0:T(8,128)(2,1)S(1)}, u32[]{:S(2)}, u32[]{:S(2)}) %collective-permute-start.7) | collective-permute-done | bytes 327712 | tf_op jit(solution)/shard_map/ppermute | solution.py:415
  35.3 2.4 %shard_map.72 = (bf16[4,256,768]{2,1,0:T(8,128)(2,1)S(1)}, bf16[512,768]{1,0:T(8,128)(2,1)S(1)}, f32[8,768]{1,0:T(8,128)S(1)}) custom-call(s32[7]{0:T(128)S(1)} %stack.23.where_ref, bf16[256,640]{1,0:T(8,128)(2,1)S(1)} %constant_dynamic-update-slice_fusion.p0.g0, bf16[256,640]{1,0:T(8,128)(2,1)S(1)} %collective-permute-done.6.p1.g1, ...), custom_call_target="tpu_custom_call" | custom-call | flops 268435456 | bytes 4194304 | tf_op jit(solution)/shard_map/pallas_call | solution.py:393
  38.4 5.9 %collective-permute-start.8 = (bf16[128,512]{1,0:T(8,128)(2,1)S(1)}, bf16[128,512]{1,0:T(8,128)(2,1)S(1)}, u32[]{:S(2)}, u32[]{:S(2)}) collective-permute-start(bf16[128,512]{1,0:T(8,128)(2,1)S(1)} %get-tuple-element.80), channel_id=1, source_target_pairs={{0,192},{1,193},{2,194},{3,195},{4,196},{5,197},{6,198},{7,199},{8... | collective-permute-start | bytes 393224 | tf_op jit(solution)/shard_map/ppermute | solution.py:415
  45.5 2.0 %collective-permute-done.8.g_ref.rest_1_ = bf16[128,512]{1,0:T(8,128)(2,1)S(1)} collective-permute-done((bf16[128,512]{1,0:T(8,128)(2,1)S(1)}, bf16[128,512]{1,0:T(8,128)(2,1)S(1)}, u32[]{:S(2)}, u32[]{:S(2)}) %collective-permute-start.8) | collective-permute-done | bytes 131104 | tf_op jit(solution)/shard_map/ppermute | solution.py:415
  49.5 2.4 %collective-permute-done.10 = bf16[64,512]{1,0:T(8,128)(2,1)S(1)} collective-permute-done((bf16[64,512]{1,0:T(8,128)(2,1)S(1)}, bf16[64,512]{1,0:T(8,128)(2,1)S(1)}, u32[]{:S(2)}, u32[]{:S(2)}) %collective-permute-start.10) | collective-permute-done | bytes 65568 | tf_op jit(solution)/shard_map/ppermute | solution.py:415
  54.3 4.6 %collective-permute-done.12.g2 = bf16[256,512]{1,0:T(8,128)(2,1)S(1)} collective-permute-done((bf16[256,512]{1,0:T(8,128)(2,1)S(1)}, bf16[256,512]{1,0:T(8,128)(2,1)S(1)}, u32[]{:S(2)}, u32[]{:S(2)}) %collective-permute-start.12) | collective-permute-done | bytes 262176 | tf_op jit(solution)/shard_map/ppermute | solution.py:415
  60.5 4.4 %collective-permute-start.14 = (bf16[64,512]{1,0:T(8,128)(2,1)S(1)}, bf16[64,512]{1,0:T(8,128)(2,1)S(1)}, u32[]{:S(2)}, u32[]{:S(2)}) collective-permute-start(bf16[64,512]{1,0:T(8,128)(2,1)S(1)} %get-tuple-element.88), channel_id=1, source_target_pairs={{0,193},{1,194},{2,195},{3,192},{4,197},{5,198},{6,199},{7,196},{8... | collective-permute-start | bytes 196616 | tf_op jit(solution)/shard_map/ppermute | solution.py:415
  66.8 4.5 %collective-permute-done.15 = bf16[64,512]{1,0:T(8,128)(2,1)S(1)} collective-permute-done((bf16[64,512]{1,0:T(8,128)(2,1)S(1)}, bf16[64,512]{1,0:T(8,128)(2,1)S(1)}, u32[]{:S(2)}, u32[]{:S(2)}) %collective-permute-start.15) | collective-permute-done | bytes 65568 | tf_op jit(solution)/shard_map/ppermute | solution.py:415
  71.9 6.3 %collective-permute-done.17.g2 = bf16[256,512]{1,0:T(8,128)(2,1)S(1)} collective-permute-done((bf16[256,512]{1,0:T(8,128)(2,1)S(1)}, bf16[256,512]{1,0:T(8,128)(2,1)S(1)}, u32[]{:S(2)}, u32[]{:S(2)}) %collective-permute-start.17) | collective-permute-done | bytes 262176 | tf_op jit(solution)/shard_map/ppermute | solution.py:415
  80.6 4.3 %collective-permute-start.20 = (bf16[64,512]{1,0:T(8,128)(2,1)S(1)}, bf16[64,512]{1,0:T(8,128)(2,1)S(1)}, u32[]{:S(2)}, u32[]{:S(2)}) collective-permute-start(bf16[64,512]{1,0:T(8,128)(2,1)S(1)} %get-tuple-element.95), channel_id=1, source_target_pairs={{0,195},{1,192},{2,193},{3,194},{4,199},{5,196},{6,197},{7,198},{8... | collective-permute-start | bytes 196616 | tf_op jit(solution)/shard_map/ppermute | solution.py:415
  87.0 2.4 %collective-permute-start.22 = (bf16[256,512]{1,0:T(8,128)(2,1)S(1)}, bf16[256,512]{1,0:T(8,128)(2,1)S(1)}, u32[]{:S(2)}, u32[]{:S(2)}) collective-permute-start(bf16[256,512]{1,0:T(8,128)(2,1)S(1)} %constant_dynamic-update-slice_fusion.9.g0), channel_id=1, source_target_pairs={{0,60},{1,61},{2,62},{3,63},{4,8},{5,9},{6,10},{7,11},{8,4},{9,5},... | collective-permute-start | bytes 786440 | tf_op jit(solution)/shard_map/ppermute | solution.py:415
  89.4 2.4 %shard_map.79.dq_ref = bf16[128,512]{1,0:T(8,128)(2,1)S(1)} custom-call(s32[7]{0:T(128)S(1)} %stack.23.where_ref, bf16[128,512]{1,0:T(8,128)(2,1)S(1)} %collective-permute-done.18.g_ref, bf16[512,512]{1,0:T(8,128)(2,1)S(1)} %bitcast.37, bf16[128,512]{1,0:T(8,128)(2,1)S(1)} %get-tuple-element.72.mixed_ref, bf16[768,1024]{1,0:T(8,128)(2,1)S(1)} %get-tuple-element.73.kv_ref, ...), custom_call_target="tpu_custom_call" | custom-call | flops 536870912 | bytes 4194304 | tf_op jit(solution)/shard_map/pallas_call | solution.py:393
  94.0 3.0 %shard_map.78.d0.kv_ref = bf16[128,1024]{1,0:T(8,128)(2,1)S(1)} custom-call(s32[7]{0:T(128)S(1)} %stack.23.where_ref, bf16[256,512]{1,0:T(8,128)(2,1)S(1)} %constant_dynamic-update-slice_fusion.9.g0, bf16[256,512]{1,0:T(8,128)(2,1)S(1)} %collective-permute-done.21.g1, bf16[256,512]{1,0:T(8,128)(2,1)S(1)} %collective-permute-done.22.g2, ...), custom_call_target="tpu_custom_call" | custom-call | flops 1073741824 | bytes 4194304 | tf_op jit(solution)/shard_map/pallas_call | solution.py:393
  99.0 2.2 %collective-permute-start.26 = (bf16[64,1024]{1,0:T(8,128)(2,1)S(1)}, bf16[64,1024]{1,0:T(8,128)(2,1)S(1)}, u32[]{:S(2)}, u32[]{:S(2)}) collective-permute-start(bf16[64,1024]{1,0:T(8,128)(2,1)S(1)} %get-tuple-element.104), channel_id=1, source_target_pairs={{0,1},{1,2},{2,3},{3,0},{4,5},{5,6},{6,7},{7,4},{8,9},{9,10},{10,1... | collective-permute-start | bytes 393224 | tf_op jit(solution)/shard_map/ppermute | solution.py:415
  102.3 2.1 %collective-permute-start.25 = (bf16[64,1024]{1,0:T(8,128)(2,1)S(1)}, bf16[64,1024]{1,0:T(8,128)(2,1)S(1)}, u32[]{:S(2)}, u32[]{:S(2)}) collective-permute-start(bf16[64,1024]{1,0:T(8,128)(2,1)S(1)} %get-tuple-element.100), channel_id=1, source_target_pairs={{0,3},{1,0},{2,1},{3,2},{4,7},{5,4},{6,5},{7,6},{8,11},{9,8},{10,9... | collective-permute-start | bytes 393224 | tf_op jit(solution)/shard_map/ppermute | solution.py:415
  104.4 2.5 %collective-permute-start.30 = (bf16[64,1024]{1,0:T(8,128)(2,1)S(1)}, bf16[64,1024]{1,0:T(8,128)(2,1)S(1)}, u32[]{:S(2)}, u32[]{:S(2)}) collective-permute-start(bf16[64,1024]{1,0:T(8,128)(2,1)S(1)} %get-tuple-element.111), channel_id=1, source_target_pairs={{0,2},{1,3},{2,0},{3,1},{4,6},{5,7},{6,4},{7,5},{8,10},{9,11},{10,... | collective-permute-start | bytes 393224 | tf_op jit(solution)/shard_map/ppermute | solution.py:415
  111.7 2.4 %collective-permute-done.30.refs_6_ = bf16[64,1024]{1,0:T(8,128)(2,1)S(1)} collective-permute-done((bf16[64,1024]{1,0:T(8,128)(2,1)S(1)}, bf16[64,1024]{1,0:T(8,128)(2,1)S(1)}, u32[]{:S(2)}, u32[]{:S(2)}) %collective-permute-start.30) | collective-permute-done | bytes 131104 | tf_op jit(solution)/shard_map/ppermute | solution.py:415
  114.7 18.2 %all_to_all.5.part_ref = bf16[8,8,2048]{2,1,0:T(8,128)(2,1)S(1)} all-to-all(bf16[8,8,2048]{2,1,0:T(8,128)(2,1)S(1)} %bitcast.45), channel_id=1, replica_groups=mesh['pipe'=4,'z'=8,'core'=2,'col'=4] {'z'}, dimensions={0} | all-to-all | bytes 524288 | tf_op jit(solution)/shard_map/all_to_all | solution.py:538
  (88 shorter events, 39.1 us)
Async XLA Ops:
  1.6 5.7 %collective-permute-start = (bf16[64,512]{1,0:T(8,128)(2,1)S(1)}, bf16[64,512]{1,0:T(8,128)(2,1)S(1)}, u32[]{:S(2)}, u32[]{:S(2)}) collective-permute-start(bf16[64,512]{1,0:T(8,128)(2,1)S(1)} %get-tuple-element.116), channel_id=1, source_target_pairs={{0,1},{1,2},{2,3},{3,0},{4,5},{5,6},{6,7},{7,4},{8,9},{9,10},{10,1... | collective-permute-start | bytes 196616 | tf_op jit(solution)/shard_map/ppermute | solution.py:415
  3.9 5.5 %collective-permute-start.1 = (bf16[64,512]{1,0:T(8,128)(2,1)S(1)}, bf16[64,512]{1,0:T(8,128)(2,1)S(1)}, u32[]{:S(2)}, u32[]{:S(2)}) collective-permute-start(bf16[64,512]{1,0:T(8,128)(2,1)S(1)} %get-tuple-element.115), channel_id=1, source_target_pairs={{0,3},{1,0},{2,1},{3,2},{4,7},{5,4},{6,5},{7,6},{8,11},{9,8},{10,9... | collective-permute-start | bytes 196616 | tf_op jit(solution)/shard_map/ppermute | solution.py:415
  9.3 7.0 %collective-permute-start.3 = (bf16[256,512]{1,0:T(8,128)(2,1)S(1)}, bf16[256,512]{1,0:T(8,128)(2,1)S(1)}, u32[]{:S(2)}, u32[]{:S(2)}) collective-permute-start(bf16[256,512]{1,0:T(8,128)(2,1)S(1)} %constant_dynamic-update-slice_fusion.12), channel_id=1, source_target_pairs={{0,60},{1,61},{2,62},{3,63},{4,8},{5,9},{6,10},{7,11},{8,4},{9,5},... | collective-permute-start | bytes 786440 | tf_op jit(solution)/shard_map/ppermute | solution.py:415
  20.4 7.1 %collective-permute-start.4 = (bf16[64,640]{1,0:T(8,128)(2,1)S(1)}, bf16[64,640]{1,0:T(8,128)(2,1)S(1)}, u32[]{:S(2)}, u32[]{:S(2)}) collective-permute-start(bf16[64,640]{1,0:T(8,128)(2,1)S(1)} %get-tuple-element.69), channel_id=1, source_target_pairs={{0,1},{1,2},{2,3},{3,0},{4,5},{5,6},{6,7},{7,4},{8,9},{9,10},{10,1... | collective-permute-start | bytes 245768 | tf_op jit(solution)/shard_map/ppermute | solution.py:415
  21.8 5.7 %collective-permute-start.5 = (bf16[64,640]{1,0:T(8,128)(2,1)S(1)}, bf16[64,640]{1,0:T(8,128)(2,1)S(1)}, u32[]{:S(2)}, u32[]{:S(2)}) collective-permute-start(bf16[64,640]{1,0:T(8,128)(2,1)S(1)} %get-tuple-element.70), channel_id=1, source_target_pairs={{0,3},{1,0},{2,1},{3,2},{4,7},{5,4},{6,5},{7,6},{8,11},{9,8},{10,9... | collective-permute-start | bytes 245768 | tf_op jit(solution)/shard_map/ppermute | solution.py:415
  27.5 7.8 %collective-permute-start.7 = (bf16[256,640]{1,0:T(8,128)(2,1)S(1)}, bf16[256,640]{1,0:T(8,128)(2,1)S(1)}, u32[]{:S(2)}, u32[]{:S(2)}) collective-permute-start(bf16[256,640]{1,0:T(8,128)(2,1)S(1)} %constant_dynamic-update-slice_fusion.p0.g0), channel_id=1, source_target_pairs={{0,60},{1,61},{2,62},{3,63},{4,8},{5,9},{6,10},{7,11},{8,4},{9,5},... | collective-permute-start | bytes 983048 | tf_op jit(solution)/shard_map/ppermute | solution.py:415
  29.5 5.8 %collective-permute-start.6 = (bf16[256,640]{1,0:T(8,128)(2,1)S(1)}, bf16[256,640]{1,0:T(8,128)(2,1)S(1)}, u32[]{:S(2)}, u32[]{:S(2)}) collective-permute-start(bf16[256,640]{1,0:T(8,128)(2,1)S(1)} %constant_dynamic-update-slice_fusion.p0.g0), channel_id=1, source_target_pairs={{0,4},{1,5},{2,6},{3,7},{4,0},{5,1},{6,2},{7,3},{8,12},{9,13},{10,... | collective-permute-start | bytes 983048 | tf_op jit(solution)/shard_map/ppermute | solution.py:415
  38.4 9.1 %collective-permute-start.8 = (bf16[128,512]{1,0:T(8,128)(2,1)S(1)}, bf16[128,512]{1,0:T(8,128)(2,1)S(1)}, u32[]{:S(2)}, u32[]{:S(2)}) collective-permute-start(bf16[128,512]{1,0:T(8,128)(2,1)S(1)} %get-tuple-element.80), channel_id=1, source_target_pairs={{0,192},{1,193},{2,194},{3,195},{4,196},{5,197},{6,198},{7,199},{8... | collective-permute-start | bytes 393224 | tf_op jit(solution)/shard_map/ppermute | solution.py:415
  45.5 6.4 %collective-permute-start.10 = (bf16[64,512]{1,0:T(8,128)(2,1)S(1)}, bf16[64,512]{1,0:T(8,128)(2,1)S(1)}, u32[]{:S(2)}, u32[]{:S(2)}) collective-permute-start(bf16[64,512]{1,0:T(8,128)(2,1)S(1)} %get-tuple-element.82), channel_id=1, source_target_pairs={{0,195},{1,192},{2,193},{3,194},{4,199},{5,196},{6,197},{7,198},{8... | collective-permute-start | bytes 196616 | tf_op jit(solution)/shard_map/ppermute | solution.py:415
  51.9 7.0 %collective-permute-start.12 = (bf16[256,512]{1,0:T(8,128)(2,1)S(1)}, bf16[256,512]{1,0:T(8,128)(2,1)S(1)}, u32[]{:S(2)}, u32[]{:S(2)}) collective-permute-start(bf16[256,512]{1,0:T(8,128)(2,1)S(1)} %constant_dynamic-update-slice_fusion.3.g0), channel_id=1, source_target_pairs={{0,60},{1,61},{2,62},{3,63},{4,8},{5,9},{6,10},{7,11},{8,4},{9,5},... | collective-permute-start | bytes 786440 | tf_op jit(solution)/shard_map/ppermute | solution.py:415
  59.5 5.5 %collective-permute-start.13 = (bf16[128,512]{1,0:T(8,128)(2,1)S(1)}, bf16[128,512]{1,0:T(8,128)(2,1)S(1)}, u32[]{:S(2)}, u32[]{:S(2)}) collective-permute-start(bf16[128,512]{1,0:T(8,128)(2,1)S(1)} %get-tuple-element.87), channel_id=1, source_target_pairs={{0,192},{1,193},{2,194},{3,195},{4,196},{5,197},{6,198},{7,199},{8... | collective-permute-start | bytes 393224 | tf_op jit(solution)/shard_map/ppermute | solution.py:415
  60.5 6.3 %collective-permute-start.14 = (bf16[64,512]{1,0:T(8,128)(2,1)S(1)}, bf16[64,512]{1,0:T(8,128)(2,1)S(1)}, u32[]{:S(2)}, u32[]{:S(2)}) collective-permute-start(bf16[64,512]{1,0:T(8,128)(2,1)S(1)} %get-tuple-element.88), channel_id=1, source_target_pairs={{0,193},{1,194},{2,195},{3,192},{4,197},{5,198},{6,199},{7,196},{8... | collective-permute-start | bytes 196616 | tf_op jit(solution)/shard_map/ppermute | solution.py:415
  64.9 6.4 %collective-permute-start.15 = (bf16[64,512]{1,0:T(8,128)(2,1)S(1)}, bf16[64,512]{1,0:T(8,128)(2,1)S(1)}, u32[]{:S(2)}, u32[]{:S(2)}) collective-permute-start(bf16[64,512]{1,0:T(8,128)(2,1)S(1)} %get-tuple-element.89), channel_id=1, source_target_pairs={{0,195},{1,192},{2,193},{3,194},{4,199},{5,196},{6,197},{7,198},{8... | collective-permute-start | bytes 196616 | tf_op jit(solution)/shard_map/ppermute | solution.py:415
  71.3 7.0 %collective-permute-start.17 = (bf16[256,512]{1,0:T(8,128)(2,1)S(1)}, bf16[256,512]{1,0:T(8,128)(2,1)S(1)}, u32[]{:S(2)}, u32[]{:S(2)}) collective-permute-start(bf16[256,512]{1,0:T(8,128)(2,1)S(1)} %constant_dynamic-update-slice_fusion.6.g0), channel_id=1, source_target_pairs={{0,60},{1,61},{2,62},{3,63},{4,8},{5,9},{6,10},{7,11},{8,4},{9,5},... | collective-permute-start | bytes 786440 | tf_op jit(solution)/shard_map/ppermute | solution.py:415
  71.4 6.9 %collective-permute-start.16 = (bf16[256,512]{1,0:T(8,128)(2,1)S(1)}, bf16[256,512]{1,0:T(8,128)(2,1)S(1)}, u32[]{:S(2)}, u32[]{:S(2)}) collective-permute-start(bf16[256,512]{1,0:T(8,128)(2,1)S(1)} %constant_dynamic-update-slice_fusion.6.g0), channel_id=1, source_target_pairs={{0,4},{1,5},{2,6},{3,7},{4,0},{5,1},{6,2},{7,3},{8,12},{9,13},{10,... | collective-permute-start | bytes 786440 | tf_op jit(solution)/shard_map/ppermute | solution.py:415
  79.1 5.8 %collective-permute-start.18 = (bf16[128,512]{1,0:T(8,128)(2,1)S(1)}, bf16[128,512]{1,0:T(8,128)(2,1)S(1)}, u32[]{:S(2)}, u32[]{:S(2)}) collective-permute-start(bf16[128,512]{1,0:T(8,128)(2,1)S(1)} %get-tuple-element.93), channel_id=1, source_target_pairs={{0,192},{1,193},{2,194},{3,195},{4,196},{5,197},{6,198},{7,199},{8... | collective-permute-start | bytes 393224 | tf_op jit(solution)/shard_map/ppermute | solution.py:415
  80.6 6.4 %collective-permute-start.20 = (bf16[64,512]{1,0:T(8,128)(2,1)S(1)}, bf16[64,512]{1,0:T(8,128)(2,1)S(1)}, u32[]{:S(2)}, u32[]{:S(2)}) collective-permute-start(bf16[64,512]{1,0:T(8,128)(2,1)S(1)} %get-tuple-element.95), channel_id=1, source_target_pairs={{0,195},{1,192},{2,193},{3,194},{4,199},{5,196},{6,197},{7,198},{8... | collective-permute-start | bytes 196616 | tf_op jit(solution)/shard_map/ppermute | solution.py:415
  87.0 7.0 %collective-permute-start.22 = (bf16[256,512]{1,0:T(8,128)(2,1)S(1)}, bf16[256,512]{1,0:T(8,128)(2,1)S(1)}, u32[]{:S(2)}, u32[]{:S(2)}) collective-permute-start(bf16[256,512]{1,0:T(8,128)(2,1)S(1)} %constant_dynamic-update-slice_fusion.9.g0), channel_id=1, source_target_pairs={{0,60},{1,61},{2,62},{3,63},{4,8},{5,9},{6,10},{7,11},{8,4},{9,5},... | collective-permute-start | bytes 786440 | tf_op jit(solution)/shard_map/ppermute | solution.py:415
  98.2 8.8 %collective-permute-start.27 = (bf16[64,1024]{1,0:T(8,128)(2,1)S(1)}, bf16[64,1024]{1,0:T(8,128)(2,1)S(1)}, u32[]{:S(2)}, u32[]{:S(2)}) collective-permute-start(bf16[64,1024]{1,0:T(8,128)(2,1)S(1)} %get-tuple-element.106), channel_id=1, source_target_pairs={{0,2},{1,3},{2,0},{3,1},{4,6},{5,7},{6,4},{7,5},{8,10},{9,11},{10,... | collective-permute-start | bytes 393224 | tf_op jit(solution)/shard_map/ppermute | solution.py:415
  99.0 12.7 %collective-permute-start.26 = (bf16[64,1024]{1,0:T(8,128)(2,1)S(1)}, bf16[64,1024]{1,0:T(8,128)(2,1)S(1)}, u32[]{:S(2)}, u32[]{:S(2)}) collective-permute-start(bf16[64,1024]{1,0:T(8,128)(2,1)S(1)} %get-tuple-element.104), channel_id=1, source_target_pairs={{0,1},{1,2},{2,3},{3,0},{4,5},{5,6},{6,7},{7,4},{8,9},{9,10},{10,1... | collective-permute-start | bytes 393224 | tf_op jit(solution)/shard_map/ppermute | solution.py:415
  101.2 10.5 %collective-permute-start.28 = (bf16[64,1024]{1,0:T(8,128)(2,1)S(1)}, bf16[64,1024]{1,0:T(8,128)(2,1)S(1)}, u32[]{:S(2)}, u32[]{:S(2)}) collective-permute-start(bf16[64,1024]{1,0:T(8,128)(2,1)S(1)} %get-tuple-element.108), channel_id=1, source_target_pairs={{0,3},{1,0},{2,1},{3,2},{4,7},{5,4},{6,5},{7,6},{8,11},{9,8},{10,9... | collective-permute-start | bytes 393224 | tf_op jit(solution)/shard_map/ppermute | solution.py:415
  102.3 9.4 %collective-permute-start.25 = (bf16[64,1024]{1,0:T(8,128)(2,1)S(1)}, bf16[64,1024]{1,0:T(8,128)(2,1)S(1)}, u32[]{:S(2)}, u32[]{:S(2)}) collective-permute-start(bf16[64,1024]{1,0:T(8,128)(2,1)S(1)} %get-tuple-element.100), channel_id=1, source_target_pairs={{0,3},{1,0},{2,1},{3,2},{4,7},{5,4},{6,5},{7,6},{8,11},{9,8},{10,9... | collective-permute-start | bytes 393224 | tf_op jit(solution)/shard_map/ppermute | solution.py:415
  104.4 9.7 %collective-permute-start.30 = (bf16[64,1024]{1,0:T(8,128)(2,1)S(1)}, bf16[64,1024]{1,0:T(8,128)(2,1)S(1)}, u32[]{:S(2)}, u32[]{:S(2)}) collective-permute-start(bf16[64,1024]{1,0:T(8,128)(2,1)S(1)} %get-tuple-element.111), channel_id=1, source_target_pairs={{0,2},{1,3},{2,0},{3,1},{4,6},{5,7},{6,4},{7,5},{8,10},{9,11},{10,... | collective-permute-start | bytes 393224 | tf_op jit(solution)/shard_map/ppermute | solution.py:415
  106.9 7.1 %collective-permute-start.29 = (bf16[64,1024]{1,0:T(8,128)(2,1)S(1)}, bf16[64,1024]{1,0:T(8,128)(2,1)S(1)}, u32[]{:S(2)}, u32[]{:S(2)}) collective-permute-start(bf16[64,1024]{1,0:T(8,128)(2,1)S(1)} %get-tuple-element.110), channel_id=1, source_target_pairs={{0,1},{1,2},{2,3},{3,0},{4,5},{5,6},{6,7},{7,4},{8,9},{9,10},{10,1... | collective-permute-start | bytes 393224 | tf_op jit(solution)/shard_map/ppermute | solution.py:415
  (14 other events, 66.8 us)
